TPU v7x, 32 devices: a whole 2x2x4 slice. The times are simulated.
32 devices in a mesh: rep: 8 (over z, y), section: 4 (over x, core).
Axes of the slice: x: 2, y: 2, z: 4, core: 2. Of those that a mesh axis runs over, the one named last changes fastest.
Arguments:
- layer_input: bfloat16 [4096, 1024], P(('rep', 'section')), may hold values from -6 to 6
- utt_frames: int32 [32, 4], P(('rep', 'section')), may hold values from 1 to 64, 128 in all within a row
- w_pointwise1: bfloat16 [1024, 2048], replicated, may hold values from -0.1875 to 0.1875
- conv_taps: bfloat16 [9, 1024], replicated, may hold values from -2 to 2
- conv_scale: float32 [1024], replicated, may hold values from 0.5 to 2
- conv_shift: float32 [1024], replicated, may hold values from -1 to 1
- w_pointwise2: bfloat16 [1024, 1024], replicated, may hold values from -0.1875 to 0.1875
- adj_grad: bfloat16 [2048, 8192], P('rep', 'section'), may hold values from -6 to 6
- proj_weight: bfloat16 [1024, 8192], P('rep', 'section'), may hold values from -0.0625 to 0.0625
- adj_target: int32 [2048, 1], replicated, may hold values from 0 to 7; in each aligned block of 64 rows (0 to 63, 64 to 127, ...) at most 16 rows name the same one
- adj_frame: int32 [2048], replicated, may hold values from 0 to 127
Outputs:
- input_grad: bfloat16 [4096, 1024], P(('rep', 'section'))
- w1_grad: float32 [1024, 2048], P(('rep', 'section'))
- w2_grad: float32 [1024, 1024], P(('rep', 'section'))
- taps_grad: float32 [1024, 9], P(('rep', 'section'))
Inputs may be any that keep to these rules, and one draw needn't show every extreme that they name: `utt_frames`: each row holds the frame counts of 4 utterances packed in order into one shard; the row sums to 128. `adj_target`: in each aligned block of 64 rows at most 16 rows name the same replica.
All inputs are finite; a program needn't handle non-finite values.
Results may differ from a plain program's by a relative error of at most 0.0075.
Values may be sent and summed in bfloat16 or wider, within the bound.
No kernel may reach another device: no remote copies, remote signals or barrier semaphores. Data moves between devices by JAX's collectives and lax.ppermute only.
A program may use at most 128 MiB of HBM per device.

v0:
```python
import jax
import jax.numpy as jnp
from jax import lax
from jax.sharding import PartitionSpec as P


def shard_backward(layer_input, lengths, grad_out, w_one, conv_taps, conv_scale, conv_shift, w_two):
    row_count, feat_width = layer_input.shape
    taps_count = conv_taps.shape[0]
    half_span = taps_count // 2
    utt_ends = jnp.cumsum(lengths)
    position = lax.broadcasted_iota(jnp.int32, (row_count, lengths.shape[0]), 0)
    segment = jnp.sum((position >= utt_ends[None, :]).astype(jnp.int32), axis=1)
    padded_seg = jnp.pad(segment, (half_span, half_span), constant_values=-1)
    as_float = layer_input.astype(jnp.float32)
    row_mean = jnp.mean(as_float, axis=1, keepdims=True)
    centred = as_float - row_mean
    inverse = lax.rsqrt(jnp.mean(centred * centred, axis=1, keepdims=True) + 1e-05)
    standard = centred * inverse
    normed = standard.astype(jnp.bfloat16)
    mixed = jnp.dot(normed, w_one, preferred_element_type=jnp.float32)
    linear = mixed[:, :feat_width]
    gate_prob = jax.nn.sigmoid(mixed[:, feat_width:])
    gated = (linear * gate_prob).astype(jnp.bfloat16)
    padded_gated = jnp.pad(gated, ((half_span, half_span), (0, 0))).astype(jnp.float32)
    tap_values = conv_taps.astype(jnp.float32)
    conv_sum = jnp.zeros((row_count, feat_width), jnp.float32)
    for k in range(taps_count):
        same_utt = padded_seg[k : k + row_count] == segment
        window = jnp.where(same_utt[:, None], padded_gated[k : k + row_count], jnp.float32(0.0))
        conv_sum = conv_sum + tap_values[k] * window
    pre_act = conv_sum * conv_scale + conv_shift
    act_prob = jax.nn.sigmoid(pre_act)
    activated = (pre_act * act_prob).astype(jnp.bfloat16)
    contract_rows = (((0,), (0,)), ((), ()))
    contract_cols = (((1,), (1,)), ((), ()))
    w2_term = lax.dot_general(
        activated, grad_out, contract_rows, preferred_element_type=jnp.float32
    )
    grad_act = lax.dot_general(grad_out, w_two, contract_cols, preferred_element_type=jnp.float32)
    grad_conv = grad_act * act_prob * (1.0 + pre_act * (1.0 - act_prob)) * conv_scale
    padded_grad = jnp.pad(grad_conv, ((half_span, half_span), (0, 0)))
    grad_gated = jnp.zeros((row_count, feat_width), jnp.float32)
    columns = []
    for k in range(taps_count):
        same_utt = padded_seg[k : k + row_count] == segment
        window = jnp.where(same_utt[:, None], padded_gated[k : k + row_count], jnp.float32(0.0))
        columns.append(jnp.sum(window * grad_conv, axis=0))
        back_start = 2 * half_span - k
        back_same = padded_seg[back_start : back_start + row_count] == segment
        grad_gated = grad_gated + tap_values[k] * jnp.where(
            back_same[:, None], padded_grad[back_start : back_start + row_count], jnp.float32(0.0)
        )
    taps_term = jnp.stack(columns, axis=1)
    grad_mixed = jnp.concatenate(
        [grad_gated * gate_prob, grad_gated * linear * gate_prob * (1.0 - gate_prob)], axis=1
    ).astype(jnp.bfloat16)
    w1_term = lax.dot_general(normed, grad_mixed, contract_rows, preferred_element_type=jnp.float32)
    grad_norm = lax.dot_general(
        grad_mixed, w_one, contract_cols, preferred_element_type=jnp.float32
    )
    grad_input = inverse * (
        grad_norm
        - jnp.mean(grad_norm, axis=1, keepdims=True)
        - standard * jnp.mean(grad_norm * standard, axis=1, keepdims=True)
    )
    input_grad = (grad_out.astype(jnp.float32) + grad_input).astype(jnp.bfloat16)
    return (input_grad, w1_term, w2_term, taps_term)


def shards(
    layer_input,
    utt_frames,
    w_pointwise1,
    conv_taps,
    conv_scale,
    conv_shift,
    w_pointwise2,
    adj_grad,
    proj_weight,
    adj_target,
    adj_frame,
):
    rep_count = lax.axis_size("rep")
    section_count = lax.axis_size("section")
    rep_here = lax.axis_index("rep")
    section_here = lax.axis_index("section")
    block_rows = adj_grad.shape[0]
    quarter_rows = block_rows // section_count
    frame_rows, feat_width = layer_input.shape
    capacity = max(2, 2 * quarter_rows // rep_count)
    full_proj = lax.all_gather(proj_weight, "rep", axis=0, tiled=True)
    feat_grad = lax.psum_scatter(
        lax.dot_general(
            adj_grad, full_proj, (((1,), (1,)), ((), ())), preferred_element_type=jnp.float32
        ),
        "section",
        scatter_dimension=0,
        tiled=True,
    ).astype(jnp.bfloat16)
    targets = adj_target[:, 0].reshape(rep_count, section_count, quarter_rows)
    frames = adj_frame.reshape(rep_count, section_count, quarter_rows)
    own_targets = lax.dynamic_index_in_dim(
        lax.dynamic_index_in_dim(targets, rep_here, 0, keepdims=False),
        section_here,
        0,
        keepdims=False,
    )
    dest_ids = lax.broadcasted_iota(jnp.int32, (quarter_rows, rep_count), 1)
    dest_hits = (own_targets[:, None] == dest_ids).astype(jnp.int32)
    earlier = jnp.sum((jnp.cumsum(dest_hits, axis=0) - dest_hits) * dest_hits, axis=1)
    send_slots = own_targets * capacity + earlier
    outgoing = (
        jnp.zeros((rep_count * capacity, feat_width), jnp.bfloat16).at[send_slots].set(feat_grad)
    )
    incoming = lax.all_to_all(
        outgoing.reshape(rep_count, capacity, feat_width),
        "rep",
        split_axis=0,
        concat_axis=0,
        tiled=True,
    )
    section_targets = lax.dynamic_index_in_dim(targets, section_here, 1, keepdims=False)
    section_frames = lax.dynamic_index_in_dim(frames, section_here, 1, keepdims=False)
    mine = (section_targets == rep_here).astype(jnp.int32)
    slot_rank = jnp.cumsum(mine, axis=1) - mine
    slot_index = jnp.where(mine > 0, slot_rank, capacity)
    source_ids = lax.broadcasted_iota(jnp.int32, (rep_count, quarter_rows), 0)
    slot_frames = (
        jnp.zeros((rep_count, capacity), jnp.int32)
        .at[source_ids, slot_index]
        .set(section_frames, mode="drop")
    )
    grad_sum = (
        jnp.zeros((frame_rows, feat_width), jnp.float32)
        .at[slot_frames.reshape(-1)]
        .add(incoming.reshape(rep_count * capacity, feat_width).astype(jnp.float32))
    )
    grad_out = grad_sum.astype(jnp.bfloat16)
    input_grad, w1_term, w2_term, taps_term = shard_backward(
        layer_input,
        utt_frames[0],
        grad_out,
        w_pointwise1,
        conv_taps,
        conv_scale,
        conv_shift,
        w_pointwise2,
    )
    w1_grad, w2_grad, taps_grad = (
        lax.psum_scatter(w1_term, ("rep", "section"), scatter_dimension=0, tiled=True),
        lax.psum_scatter(w2_term, ("rep", "section"), scatter_dimension=0, tiled=True),
        lax.psum_scatter(taps_term, ("rep", "section"), scatter_dimension=0, tiled=True),
    )
    return (input_grad, w1_grad, w2_grad, taps_grad)


def solution(mesh):
    placed = (
        P(("rep", "section"), None),
        P(("rep", "section"), None),
        P(),
        P(),
        P(),
        P(),
        P(),
        P("rep", "section"),
        P("rep", "section"),
        P(),
        P(),
    )
    return jax.shard_map(
        shards,
        mesh=mesh,
        in_specs=placed,
        out_specs=(
            P(("rep", "section"), None),
            P(("rep", "section"), None),
            P(("rep", "section"), None),
            P(("rep", "section"), None),
        ),
        check_vma=False,
    )
```

profile of v0, /device:TPU:0, one launch (start us, length us, event | category | flops | bytes accessed | tf_op | source)
XLA Modules:
  0.0 568.4 jit_solution(6547347367188439223)
XLA Ops:
  7.2 0.0 copy-start
  7.2 0.0 all-gather.2.cloned.1.call-start
  7.2 0.7 all-gather.2.cloned.1.call-update
  7.9 0.0 reduce-scatter.7.cloned.1.call-start
  8.0 0.8 reduce-window.8
  8.8 0.5 broadcast.208
  9.3 1.4 reduce.7
  10.7 0.1 reshape_squeeze.3
  10.8 0.1 fusion.39
  10.8 0.1 reduce_window_sum.30
  10.9 0.2 copy.23
  11.1 0.2 select_reduce_fusion
  11.3 1.1 convert_reduce_fusion
  12.4 6.7 %fusion.32 = s32[8,64,1]{2,0,1:T(8,128)S(1)} fusion(s32[8,64,1]{2,0,1:T(8,128)S(1)} %copy.23), kind=kOutput, calls=%fused_computation.74 | output fusion | flops 39936 | bytes 4096 | tf_op jit(solution)/shard_map/jit(cumsum)/reduce_window_sum | solution.py:126
  19.1 0.0 copy-start.12
  19.1 67.2 %all-gather.2.cloned.1.call-done = bf16[1024,2048]{1,0:T(8,128)(2,1)} async-done(((bf16[128,2048]{1,0:T(8,128)(2,1)}), bf16[1024,2048]{1,0:T(8,128)(2,1)}) %all-gather.2.cloned.1.call-update) | async-done | bytes 4194320 | tf_op jit(solution)/shard_map/all_gather | solution.py:92
  86.3 4.8 fusion.61
  91.1 0.0 reduce-scatter.7.cloned.1.call-update
  91.1 0.1 convert_reduce_fusion.1
  91.2 0.1 reshape.189
  91.3 0.1 reshape.198
  91.3 0.1 copy.26
  91.5 0.1 reshape.196
  91.6 22.1 %scatter_fusion = s32[8,16]{1,0:T(8,128)S(1)} fusion(s32[8,16]{1,0:T(8,128)S(1)} %broadcast_in_dim.182, s32[512]{0:T(512)S(1)} %reshape.196, s32[512]{0:T(512)S(1)} %reshape.198), kind=kCustom, calls=%fused_computation | custom fusion | bytes 10240 | tf_op jit(solution)/shard_map/scatter | solution.py:132
  113.7 0.1 reshape.190
  113.8 0.2 fusion.13
  114.0 0.1 fusion.40
  114.1 0.0 copy-start.13
  114.2 0.0 copy-start.14
  114.2 3.0 fusion.57
  117.2 1.0 copy-done.1
  118.1 0.1 multiply_convert_fusion.3
  118.3 0.0 reduce-scatter.7.cloned.1.call-done
  118.3 2.0 scatter_custom_fusion.1
  120.3 3.4 all-to-all-start
  123.7 0.0 reduce-scatter.13.cloned.1.call-start
  123.8 0.1 pad_convert_fusion
  123.9 1.7 multiply_add_fusion.1
  125.5 6.7 %all-to-all-done = bf16[8,16,1024]{2,1,0:T(8,128)(2,1)S(1)} async-done(((bf16[8,16,1024]{2,1,0:T(8,128)(2,1)}), bf16[8,16,1024]{2,1,0:T(8,128)(2,1)S(1)}, u32[]{:S(2)}, u32[]{:S(2)}) %all-to-all-start) | async-done | bytes 262176 | tf_op jit(solution)/shard_map/all_to_all | solution.py:116
  132.2 0.7 copy-done.10
  132.9 2.2 scatter_custom_fusion.2
  135.1 4.7 multiply_reduce_fusion
  139.8 0.8 stack.39
  140.6 1.1 copy.27
  141.7 0.0 reduce-scatter.13.cloned.1.call-update
  141.7 0.0 reduce-scatter.11.cloned.1.call-start
  141.8 4.0 fusion.30
  145.8 0.0 reduce-scatter.11.cloned.1.call-update
  145.8 0.2 reduce-scatter.9.cloned.1.call-start
  146.0 4.4 multiply_convert_fusion.2
  150.4 0.2 multiply_convert_fusion.1
  150.7 0.0 copy-start.8
  150.7 0.5 copy-done.6
  151.1 0.2 copy-done.8
  151.4 4.6 fusion.28
  156.0 0.0 reduce-scatter.9.cloned.1.call-update
  156.0 0.9 copy-done.7
  156.9 0.1 copy-done.9
  157.0 3.8 fusion.59
  160.9 1.0 fusion.12
  161.8 113.0 %reduce-scatter.13.cloned.1.call-done = f32[32,9]{1,0:T(8,128)} async-done(((f32[1024,9]{1,0:T(8,128)}), f32[32,9]{1,0:T(8,128)}) %reduce-scatter.13.cloned.1.call-update) | async-done | bytes 1168
  274.9 1.4 copy.28
  276.2 138.0 %reduce-scatter.11.cloned.1.call-done = f32[32,1024]{1,0:T(8,128)} async-done(((f32[1024,1024]{1,0:T(8,128)}), f32[32,1024]{1,0:T(8,128)}) %reduce-scatter.11.cloned.1.call-update) | async-done | bytes 131088 | tf_op jit(solution)/shard_map/reduce_scatter | solution.py:152
  414.3 147.6 %reduce-scatter.9.cloned.1.call-done = f32[32,2048]{1,0:T(8,128)} async-done(((f32[1024,2048]{1,0:T(8,128)}), f32[32,2048]{1,0:T(8,128)}) %reduce-scatter.9.cloned.1.call-update) | async-done | bytes 262160 | tf_op jit(solution)/shard_map/reduce_scatter | solution.py:151
  (29 shorter events, 0.1 us)
Async XLA Ops:
  7.2 127.9 %copy-start = (bf16[1024,1024]{1,0:T(8,128)(2,1)S(1)}, bf16[1024,1024]{1,0:T(8,128)(2,1)}, u32[]{:S(2)}) copy-start(bf16[1024,1024]{1,0:T(8,128)(2,1)} %param.17) | copy-start | bytes 6291460
  7.2 79.1 %all-gather.2.cloned.1.call-start = ((), (), s32[]{:S(2)}) async-start(), calls=%async_computation.5 | async-start | bytes 4718592 | tf_op jit(solution)/shard_map/all_gather | solution.py:92
  7.9 110.4 %reduce-scatter.7.cloned.1.call-start = ((), (), s32[]{:S(2)}) async-start(), calls=%async_computation.6 | async-start | bytes 1310720 | tf_op jit(solution)/shard_map/reduce_scatter | solution.py:93
  19.1 72.0 %copy-start.12 = (s32[2048]{0:T(1024)S(1)}, s32[2048]{0:T(1024)}, u32[]{:S(2)}) copy-start(s32[2048]{0:T(1024)} %param.21) | copy-start | bytes 24580
  91.6 22.2 %copy-start.3 = (bf16[128,1024]{1,0:T(8,128)(2,1)S(1)}, bf16[128,1024]{1,0:T(8,128)(2,1)}, u32[]{:S(2)}) copy-start(bf16[128,1024]{1,0:T(8,128)(2,1)} %param.11) | copy-start | bytes 786436
  91.6 22.5 %copy-start.11 = (bf16[9,1024]{1,0:T(8,128)(2,1)S(1)}, bf16[9,1024]{1,0:T(8,128)(2,1)}, u32[]{:S(2)}) copy-start(bf16[9,1024]{1,0:T(8,128)(2,1)} %param.14) | copy-start | bytes 55300
  114.1 9.7 %copy-start.13 = (f32[1024]{0:T(1024)S(1)}, f32[1024]{0:T(1024)}, u32[]{:S(2)}) copy-start(f32[1024]{0:T(1024)} %param.16) | copy-start | bytes 12292
  114.2 9.7 %copy-start.14 = (f32[1024]{0:T(1024)S(1)}, f32[1024]{0:T(1024)}, u32[]{:S(2)}) copy-start(f32[1024]{0:T(1024)} %param.15) | copy-start | bytes 12292
  117.1 1.0 copy-start.1
  120.3 11.9 %all-to-all-start = ((bf16[8,16,1024]{2,1,0:T(8,128)(2,1)}), bf16[8,16,1024]{2,1,0:T(8,128)(2,1)S(1)}, u32[]{:S(2)}, u32[]{:S(2)}) async-start(bf16[8,16,1024]{2,1,0:T(8,128)(2,1)} %bitcast.6), calls=%async_computation.1 | async-start | bytes 524288 | tf_op jit(solution)/shard_map/all_to_all | solution.py:116
  123.7 151.1 %reduce-scatter.13.cloned.1.call-start = ((), (), s32[]{:S(2)}) async-start(), calls=%async_computation.9 | async-start | bytes 540672
  132.2 0.7 copy-start.10
  135.1 4.7 copy-start.4
  141.7 4.3 copy-start.2
  141.7 272.5 %reduce-scatter.11.cloned.1.call-start = ((), (), s32[]{:S(2)}) async-start(), calls=%async_computation.8 | async-start | bytes 4325376 | tf_op jit(solution)/shard_map/reduce_scatter | solution.py:152
  145.8 416.0 %reduce-scatter.9.cloned.1.call-start = ((), (), s32[]{:S(2)}) async-start(), calls=%async_computation.7 | async-start | bytes 8650752 | tf_op jit(solution)/shard_map/reduce_scatter | solution.py:151
  150.4 0.7 copy-start.6
  150.7 0.7 copy-start.8
  156.0 1.0 copy-start.7
  156.0 1.0 copy-start.9
  157.0 3.9 copy-start.5
Sparse Core Ops, SparseCore 0:
  10.1 76.0 all-gather.1
  91.2 23.1 reduce-scatter.6
  141.8 132.9 reduce-scatter.12
  277.6 136.6 reduce-scatter.10
  417.0 144.8 reduce-scatter.8
where the time goes:
time: 569 us; the launch traced here: 568 us
  waiting for transfers between devices  473 us (83%)
  local copies, waits for them, and re-layouts  30 us (5%)
  matrix products  24.9 us (4%)
  other arithmetic  22.4 us (4%)
  between operations  14 us (2%)
    reduce_scatter x1, waiting for transfers between devices, shards(): lax.psum_scatter(w1_term, ('rep', 'section'), scatter_dimension=0, tiled=...  148 us
    reduce_scatter x1, waiting for transfers between devices, shards(): lax.psum_scatter(w2_term, ('rep', 'section'), scatter_dimension=0, tiled=...  138 us
    unnamed x6, waiting for transfers between devices  114 us
    all_gather x1, waiting for transfers between devices, shards(): full_proj = lax.all_gather(proj_weight, 'rep', axis=0, tiled=True)  67.2 us
    scatter x1, local copies, waits for them, and re-layouts, shards(): slot_frames = jnp.zeros((rep_count, capacity), jnp.int32).at[source_ids,...  22.1 us
  transfers between devices with their start and end apart: 6, of which 5 were waited for; matrix products, arithmetic and copies ran while one was open for 10% of the time, Pallas kernels for 0%

commit v1 on v0

v1 whole, which is shorter than its diff:
```python
import jax
import jax.numpy as jnp
from jax import lax
from jax.sharding import PartitionSpec as P

BF = jnp.bfloat16
F32 = jnp.float32
ROWS = (((0,), (0,)), ((), ()))
COLS = (((1,), (1,)), ((), ()))


def xor_perm(count, mask):
    return [(i, i ^ mask) for i in range(count)]


def forward_part(layer_input, lengths, w_one, conv_taps, conv_scale, conv_shift):
    row_count, feat_width = layer_input.shape
    taps_count = conv_taps.shape[0]
    half_span = taps_count // 2
    ends = [lengths[0]]
    for j in range(1, lengths.shape[0]):
        ends.append(ends[-1] + lengths[j])
    position = lax.broadcasted_iota(jnp.int32, (row_count,), 0)
    segment = sum((position >= e).astype(jnp.int32) for e in ends)
    padded_seg = jnp.pad(segment, (half_span, half_span), constant_values=-1)
    as_float = layer_input.astype(F32)
    row_mean = jnp.mean(as_float, axis=1, keepdims=True)
    centred = as_float - row_mean
    inverse = lax.rsqrt(jnp.mean(centred * centred, axis=1, keepdims=True) + 1e-05)
    standard = centred * inverse
    normed = standard.astype(BF)
    mixed = jnp.dot(normed, w_one, preferred_element_type=F32)
    linear = mixed[:, :feat_width]
    gate_prob = jax.nn.sigmoid(mixed[:, feat_width:])
    gated = (linear * gate_prob).astype(BF)
    padded_gated = jnp.pad(gated, ((half_span, half_span), (0, 0))).astype(F32)
    tap_values = conv_taps.astype(F32)
    conv_sum = jnp.zeros((row_count, feat_width), F32)
    for k in range(taps_count):
        same_utt = padded_seg[k : k + row_count] == segment
        window = jnp.where(same_utt[:, None], padded_gated[k : k + row_count], 0.0)
        conv_sum = conv_sum + tap_values[k] * window
    pre_act = conv_sum * conv_scale + conv_shift
    act_prob = jax.nn.sigmoid(pre_act)
    activated = (pre_act * act_prob).astype(BF)
    slope = act_prob * (1.0 + pre_act * (1.0 - act_prob)) * conv_scale
    return standard, inverse, normed, linear, gate_prob, padded_gated, padded_seg, segment, activated, slope


def shards(
    layer_input,
    utt_frames,
    w_pointwise1,
    conv_taps,
    conv_scale,
    conv_shift,
    w_pointwise2,
    adj_grad,
    proj_weight,
    adj_target,
    adj_frame,
):
    reps = lax.axis_size("rep")
    sections = lax.axis_size("section")
    rep_here = lax.axis_index("rep")
    sec_here = lax.axis_index("section")
    block_rows = adj_grad.shape[0]
    quarter = block_rows // sections
    frame_rows, feat = layer_input.shape
    taps_count = conv_taps.shape[0]
    half_span = taps_count // 2
    capacity = max(2, 2 * quarter // reps)
    outer = reps // 2
    pair_here = rep_here % 2
    outer_here = rep_here // 2
    piece = proj_weight.shape[0]

    adj_other = lax.ppermute(adj_grad, "rep", xor_perm(reps, 1))
    blocks = [proj_weight]
    for k in range(1, outer):
        blocks.append(
            lax.ppermute(
                proj_weight,
                "rep",
                [(i, ((i // 2 + k) % outer) * 2 + i % 2) for i in range(reps)],
            )
        )

    targets = adj_target[:, 0].reshape(reps, sections, quarter)
    frames = adj_frame.reshape(reps, sections, quarter)
    sec_targets = lax.dynamic_index_in_dim(targets, sec_here, 1, keepdims=False)
    sec_frames = lax.dynamic_index_in_dim(frames, sec_here, 1, keepdims=False)
    row_a = lax.broadcasted_iota(jnp.int32, (quarter, quarter), 0)
    row_b = lax.broadcasted_iota(jnp.int32, (quarter, quarter), 1)
    same = (sec_targets[:, :, None] == sec_targets[:, None, :]) & (row_b < row_a)[None]
    rank = jnp.sum(same.astype(jnp.int32), axis=2)
    mine = sec_targets == rep_here
    slots = lax.broadcasted_iota(jnp.int32, (1, capacity, 1), 1)
    hit = mine[:, None, :] & (rank[:, None, :] == slots)
    slot_frames = jnp.sum(jnp.where(hit, sec_frames[:, None, :] + 1, 0), axis=2) - 1

    def packing(block):
        tgt = lax.dynamic_index_in_dim(sec_targets, block, 0, keepdims=False)
        rnk = lax.dynamic_index_in_dim(rank, block, 0, keepdims=False)
        slot_of = tgt * capacity + rnk
        ids = lax.broadcasted_iota(jnp.int32, (reps * capacity, quarter), 0)
        return (slot_of[None, :] == ids).astype(BF)

    pack_own = packing(rep_here)
    pack_other = packing(jnp.bitwise_xor(rep_here, 1))

    standard, inverse, normed, linear, gate_prob, padded_gated, padded_seg, segment, activated, slope = forward_part(
        layer_input, utt_frames[0], w_pointwise1, conv_taps, conv_scale, conv_shift
    )
    part_rows = feat // (reps * sections)

    def by_section(values):
        return values.reshape(frame_rows, reps, sections, part_rows).transpose(2, 0, 1, 3).reshape(
            sections, frame_rows, reps * part_rows
        )

    early = jnp.concatenate([by_section(normed), by_section(activated)], axis=2)
    early_parts = []
    for k in range(sections):
        piece_k = lax.dynamic_index_in_dim(early, jnp.bitwise_xor(sec_here, k), 0, keepdims=False)
        early_parts.append(lax.ppermute(piece_k, "section", xor_perm(sections, k)) if k else piece_k)

    partial = []
    for k in range(outer):
        own = lax.dot_general(adj_grad, blocks[k], COLS, preferred_element_type=F32)
        other = lax.dot_general(adj_other, blocks[k], COLS, preferred_element_type=F32)
        partial.append(jnp.stack([own, other]).astype(BF))
    partial = jnp.stack(partial, axis=2)
    partial = partial.reshape(2, sections, quarter, outer * piece).transpose(1, 0, 2, 3)
    arrived = lax.all_to_all(partial, "section", split_axis=0, concat_axis=0, tiled=True)
    feat_grad = jnp.sum(arrived.astype(F32), axis=0).astype(BF)
    packed = jnp.stack(
        [
            jnp.dot(pack_own, feat_grad[0], preferred_element_type=F32).astype(BF),
            jnp.dot(pack_other, feat_grad[1], preferred_element_type=F32).astype(BF),
        ]
    )
    packed = packed.reshape(2, reps, capacity, outer, piece)
    packed = jnp.concatenate([packed[:, :, :, :1], packed[:, :, :, :0:-1]], axis=3)
    packed = jnp.roll(packed, outer_here, axis=3)
    outgoing = packed.transpose(1, 0, 2, 3, 4).reshape(reps, 2 * capacity, outer * piece)
    incoming = lax.all_to_all(outgoing, "rep", split_axis=0, concat_axis=0, tiled=True)
    incoming = incoming.reshape(outer, 2, 2 * capacity, outer * piece)
    slot_frames = slot_frames.reshape(outer, 2, capacity)
    frame_ids = lax.broadcasted_iota(jnp.int32, (frame_rows, outer * 2 * capacity), 0)
    halves = []
    for p in range(2):
        order = jnp.stack([slot_frames[:, p], slot_frames[:, 1 - p]], axis=1).reshape(1, -1)
        pick = (frame_ids == order).astype(BF)
        halves.append(
            jnp.dot(pick, incoming[:, p].reshape(-1, outer * piece), preferred_element_type=F32)
            .astype(BF)
            .reshape(frame_rows, outer, piece)
        )
    grad_out = jnp.stack(halves, axis=2).reshape(frame_rows, feat)

    def gather(values):
        from_two = lax.ppermute(values, "section", xor_perm(sections, 2))
        from_one = lax.ppermute(values, "section", xor_perm(sections, 1))
        from_three = lax.ppermute(from_two, "section", xor_perm(sections, 1))
        return [values, from_one, from_two, from_three]

    grad_out_all = gather(grad_out)

    grad_act = lax.dot_general(grad_out, w_pointwise2, COLS, preferred_element_type=F32)
    grad_conv = grad_act * slope
    padded_grad = jnp.pad(grad_conv, ((half_span, half_span), (0, 0)))
    grad_gated = jnp.zeros((frame_rows, feat), F32)
    tap_values = conv_taps.astype(F32)
    columns = []
    for k in range(taps_count):
        same_utt = padded_seg[k : k + frame_rows] == segment
        window = jnp.where(same_utt[:, None], padded_gated[k : k + frame_rows], 0.0)
        columns.append(jnp.sum(window * grad_conv, axis=0))
        back = 2 * half_span - k
        back_same = padded_seg[back : back + frame_rows] == segment
        grad_gated = grad_gated + tap_values[k] * jnp.where(
            back_same[:, None], padded_grad[back : back + frame_rows], 0.0
        )
    taps_rows = 16
    taps_term = jnp.pad(jnp.stack(columns, axis=0), ((0, taps_rows - taps_count), (0, 0))).astype(BF)
    first = grad_gated * gate_prob
    grad_mixed = jnp.concatenate([first, first * linear * (1.0 - gate_prob)], axis=1).astype(BF)
    late = jnp.concatenate([grad_mixed, jnp.pad(taps_term.reshape(taps_rows // 2, 2 * feat), ((0, 8), (0, 0)))], axis=0)
    late_all = gather(late)

    w1_part = sum(
        lax.dot_general(e[:, : reps * part_rows], g[:frame_rows], ROWS, preferred_element_type=F32)
        for e, g in zip(early_parts, late_all)
    )
    w2_part = sum(
        lax.dot_general(e[:, reps * part_rows :], g, ROWS, preferred_element_type=F32)
        for e, g in zip(early_parts, grad_out_all)
    )
    taps_sum = sum(g[frame_rows : frame_rows + taps_rows // 2].astype(F32) for g in late_all).reshape(taps_rows, feat)
    taps_sum = lax.dynamic_index_in_dim(
        taps_sum.reshape(taps_rows, reps, sections, part_rows), sec_here, 2, keepdims=False
    )
    taps_part = jnp.pad(
        taps_sum.transpose(1, 2, 0).reshape(reps * part_rows, taps_rows), ((0, 0), (0, 128 - taps_rows))
    )
    parts = jnp.concatenate([w1_part, w2_part, taps_part], axis=1).astype(BF)
    width = parts.shape[1]
    swapped = lax.all_to_all(
        parts.reshape(reps, part_rows, width), "rep", split_axis=0, concat_axis=0, tiled=True
    )
    total = jnp.sum(swapped.astype(F32), axis=0)

    grad_norm = lax.dot_general(grad_mixed, w_pointwise1, COLS, preferred_element_type=F32)
    grad_input = inverse * (
        grad_norm
        - jnp.mean(grad_norm, axis=1, keepdims=True)
        - standard * jnp.mean(grad_norm * standard, axis=1, keepdims=True)
    )
    input_grad = (grad_out.astype(F32) + grad_input).astype(BF)
    return (
        input_grad,
        total[:, : 2 * feat],
        total[:, 2 * feat : 3 * feat],
        total[:, 3 * feat : 3 * feat + taps_count],
    )


def solution(mesh):
    spread = P(("rep", "section"), None)
    return jax.shard_map(
        shards,
        mesh=mesh,
        in_specs=(spread, spread, P(), P(), P(), P(), P(), P("rep", "section"), P("rep", "section"), P(), P()),
        out_specs=(spread, spread, spread, spread),
        check_vma=False,
    )
```

time: 569 us -> 175 us (0.31)
  waiting for transfers between devices: 473 us -> 74.2 us
  starting transfers between devices: 3.79 us -> 24.3 us
  local copies, waits for them, and re-layouts: 30 us -> 16.5 us
  matrix products: 24.9 us -> 37.9 us
  between operations: 14 us -> 3.9 us
    reduce_scatter x3 -> x0, waiting for transfers between devices: 286 us -> none  [the longest x1 148 us: shards(): lax.psum_scatter(w1_term, ('rep', 'section'), scatter_dimension=0, tiled=...]
    unnamed x6 -> x0, waiting for transfers between devices: 114 us -> none
    all_gather x1 -> x0, waiting for transfers between devices: 67.2 us -> none  [shards(): full_proj = lax.all_gather(proj_weight, 'rep', axis=0, tiled=True)]
    all_to_all x1 -> x3, waiting for transfers between devices: 6.67 us -> 51.2 us  [the longest x1 34.6 us: shards(): lax.all_to_all(parts.reshape(reps, part_rows, width), 'rep', split_axis=0...]
    ppermute x0 -> x13, waiting for transfers between devices: none -> 23 us  [the longest x3 14.2 us: shards(): lax.ppermute(proj_weight, 'rep', [(i, (i // 2 + k) % outer * 2 + i % 2) f...]
    scatter x1 -> x0, local copies, waits for them, and re-layouts: 22.1 us -> none  [shards(): slot_frames = jnp.zeros((rep_count, capacity), jnp.int32).at[source_ids,...]
    dot_general x6 -> x23, matrix products: 24.9 us -> 37.9 us  [the longest x4 7.86 us: shards(): lax.dot_general(e[:, :reps * part_rows], g[:frame_rows], ROWS, preferred_...]
    ppermute x0 -> x13, starting transfers between devices: none -> 12.6 us  [the longest x3 6.11 us: shards(): lax.ppermute(proj_weight, 'rep', [(i, (i // 2 + k) % outer * 2 + i % 2) f...]
  transfers between devices with their start and end apart: 6 -> 16, of which waited for: 5 -> 5; matrix products, arithmetic and copies ran while one was open for 10% -> 35% of each run, Pallas kernels for 0% -> 0%
where the time goes in v1:
time: 175 us; the launch traced here: 174 us
  waiting for transfers between devices  74.2 us (42%)
  matrix products  37.9 us (22%)
  starting transfers between devices  24.3 us (14%)
  other arithmetic  17.3 us (10%)
  local copies, waits for them, and re-layouts  16.5 us (9%)
  between operations  3.9 us (2%)
    all_to_all x1, waiting for transfers between devices, shards(): lax.all_to_all(parts.reshape(reps, part_rows, width), 'rep', split_axis=0...  34.6 us
    ppermute x3, waiting for transfers between devices, shards(): lax.ppermute(proj_weight, 'rep', [(i, (i // 2 + k) % outer * 2 + i % 2) f...  14.2 us
    ppermute x2, waiting for transfers between devices, gather(): from_two = lax.ppermute(values, 'section', xor_perm(sections, 2))  8.79 us
    all_to_all x1, waiting for transfers between devices, shards(): lax.all_to_all(outgoing, 'rep', split_axis=0, concat_axis=0, tiled=True)  8.53 us
    all_to_all x1, waiting for transfers between devices, shards(): lax.all_to_all(partial, 'section', split_axis=0, concat_axis=0, tiled=True)  8.08 us
    dot_general x4, matrix products, shards(): lax.dot_general(e[:, :reps * part_rows], g[:frame_rows], ROWS, preferred_...  7.86 us
    dot_general x4, matrix products, shards(): lax.dot_general(adj_other, blocks[k], COLS, preferred_element_type=F32)  7.03 us
    dot_general x4, matrix products, shards(): own = lax.dot_general(adj_grad, blocks[k], COLS, preferred_element_type=F32)  6.75 us
  transfers between devices with their start and end apart: 16, of which 5 were waited for; matrix products, arithmetic and copies ran while one was open for 35% of the time, Pallas kernels for 0%

profile of v1, /device:TPU:0, one launch (start us, length us, event | category | flops | bytes accessed | tf_op | source)
XLA Modules:
  0.0 174.1 jit_solution(9336752108160770349)
XLA Ops:
  0.6 3.1 %collective-permute-start.1 = (bf16[128,2048]{1,0:T(8,128)(2,1)}, bf16[128,2048]{1,0:T(8,128)(2,1)}, u32[]{:S(2)}, u32[]{:S(2)}) collective-permute-start(bf16[128,2048]{1,0:T(8,128)(2,1)} %param.19), channel_id=1, source_target_pairs={{0,8},{4,12},{8,16},{12,20},{16,24},{20,28},{24,0},{28,4},{1,9},{5... | collective-permute-start | bytes 1572872 | tf_op jit(solution)/shard_map/ppermute | solution.py:82
  3.7 2.1 %collective-permute-start.3 = (bf16[128,2048]{1,0:T(8,128)(2,1)}, bf16[128,2048]{1,0:T(8,128)(2,1)}, u32[]{:S(2)}, u32[]{:S(2)}) collective-permute-start(bf16[128,2048]{1,0:T(8,128)(2,1)} %param.19), channel_id=1, source_target_pairs={{0,24},{4,28},{8,0},{12,4},{16,8},{20,12},{24,16},{28,20},{1,25},{... | collective-permute-start | bytes 1572872 | tf_op jit(solution)/shard_map/ppermute | solution.py:82
  5.8 0.9 collective-permute-start.2
  6.8 1.5 collective-permute-start
  8.3 1.1 convert_reduce_fusion.1
  9.4 1.2 fusion.22
  10.5 1.4 fusion.93
  14.5 0.7 fusion.77
  15.3 1.2 fusion.91
  16.4 1.2 fusion.15
  17.8 0.7 copy.61
  18.5 2.9 %fusion.94 = f32[128,2048]{1,0:T(8,128)S(1)} fusion(bf16[128,1024]{1,0:T(8,128)(2,1)S(1)} %fusion.15, bf16[1024,2048]{1,0:T(8,128)(2,1)} %param.13), kind=kOutput, calls=%fused_computation.203 | convolution fusion | flops 536870912 | bytes 5505024 | tf_op jit(solution)/shard_map/dot_general | solution.py:32
  21.4 1.0 copy-done.2
  22.6 0.5 copy-done.10
  23.1 1.8 %multiply_convert_fusion = (bf16[128,1024]{1,0:T(8,128)(2,1)}, f32[128,1024]{1,0:T(8,128)}) fusion(f32[1024]{0:T(1024)S(1)} %copy-done.10, f32[1024]{0:T(1024)S(1)} %copy-done.11, f32[136,1024]{1,0:T(8,128)S(1)} %pad_convert_fusion, pred[128]{0:T(512)(128)(4,1)S(1)} %get-tuple-element.66, f32[1024]{0:T(1024)S(1)} %bitcast.153, ...), kind=kLoop, calls=%fused_computation.85 | loop fusion | flops 4194304 | bytes 5551104 | tf_op jit(solution)/shard_map/convert_element_type | solution.py:45
  24.9 1.2 copy.62
  26.1 0.7 copy.63
  26.8 1.8 %fusion.45 = (bf16[128,512]{0,1:T(8,128)(2,1)}, bf16[128,512]{0,1:T(8,128)(2,1)S(1)}, bf16[128,512]{0,1:T(8,128)(2,1)}, bf16[128,512]{0,1:T(8,128)(2,1)}) fusion(s32[]{:T(128)S(6)} %select_n.142, bf16[4,128,256]{1,2,0:T(8,128)(2,1)} %bitcast.128, bf16[4,128,256]{1,2,0:T(8,128)(2,1)} %bitcast.129, s32[]{:T(128)S(6)} %select_n.114, s32[]{:T(128)S(6)} %select_n.140, ...), kind=kLoop, calls=%fused_computation.116 | loop fusion | flops 1048576 | bytes 1048592 | tf_op jit(solution)/shard_map/jit(dynamic_index_in_dim)/squeeze | solution.py:125
  28.6 1.7 fusion.3
  30.3 0.5 broadcast.123
  30.9 0.7 reduce.4
  31.6 1.7 collective-permute-start.4
  33.3 1.8 %fusion.5 = bf16[1,256,1,128]{3,1,2,0:T(8,128)(2,1)S(1)} fusion(bf16[256,2048]{1,0:T(8,128)(2,1)} %param.18, bf16[128,2048]{1,0:T(8,128)(2,1)} %collective-permute-done.1), kind=kOutput, calls=%fused_computation.27 | convolution fusion | flops 134250496 | bytes 1638400 | tf_op jit(solution)/shard_map/dot_general | solution.py:130
  35.1 0.6 collective-permute-start.6
  35.7 1.8 %fusion.9 = bf16[1,256,1,128]{3,1,2,0:T(8,128)(2,1)S(1)} fusion(bf16[256,2048]{1,0:T(8,128)(2,1)} %param.18, bf16[128,2048]{1,0:T(8,128)(2,1)} %collective-permute-done.3), kind=kOutput, calls=%fused_computation.31 | convolution fusion | flops 134250496 | bytes 1638400 | tf_op jit(solution)/shard_map/dot_general | solution.py:130
  37.5 14.2 %collective-permute-done.2 = bf16[128,2048]{1,0:T(8,128)(2,1)} collective-permute-done((bf16[128,2048]{1,0:T(8,128)(2,1)}, bf16[128,2048]{1,0:T(8,128)(2,1)}, u32[]{:S(2)}, u32[]{:S(2)}) %collective-permute-start.2) | collective-permute-done | bytes 524320 | tf_op jit(solution)/shard_map/ppermute | solution.py:82
  51.7 1.5 fusion.7
  53.2 1.8 %fusion.10 = bf16[1,256,1,128]{3,1,2,0:T(8,128)(2,1)S(1)} fusion(bf16[256,2048]{1,0:T(8,128)(2,1)} %collective-permute-done, bf16[128,2048]{1,0:T(8,128)(2,1)} %collective-permute-done.3), kind=kOutput, calls=%fused_computation.32 | convolution fusion | flops 134250496 | bytes 1638400 | tf_op jit(solution)/shard_map/dot_general | solution.py:131
  55.0 1.8 %fusion.8 = bf16[1,256,1,128]{3,1,2,0:T(8,128)(2,1)S(1)} fusion(bf16[256,2048]{1,0:T(8,128)(2,1)} %collective-permute-done, bf16[128,2048]{1,0:T(8,128)(2,1)} %collective-permute-done.2), kind=kOutput, calls=%fused_computation.30 | convolution fusion | flops 134250496 | bytes 1638400 | tf_op jit(solution)/shard_map/dot_general | solution.py:131
  56.8 1.8 %fusion.6 = bf16[1,256,1,128]{3,1,2,0:T(8,128)(2,1)S(1)} fusion(bf16[256,2048]{1,0:T(8,128)(2,1)} %collective-permute-done, bf16[128,2048]{1,0:T(8,128)(2,1)} %collective-permute-done.1), kind=kOutput, calls=%fused_computation.28 | convolution fusion | flops 134250496 | bytes 1638400 | tf_op jit(solution)/shard_map/dot_general | solution.py:131
  58.6 1.7 fusion.4
  60.4 0.4 copy.55
  60.8 1.0 reshape.274
  61.8 1.9 %copy.56 = bf16[4,2,64,512]{3,2,1,0:T(8,128)(2,1)} copy(bf16[4,2,64,512]{3,2,0,1:T(8,128)(2,1)} %bitcast.120) | data formatting | bytes 1048576 | tf_op jit(solution)/shard_map/transpose | solution.py:134
  63.7 3.5 %all-to-all-start = ((bf16[4,2,64,512]{3,2,1,0:T(8,128)(2,1)}), bf16[4,2,64,512]{3,2,1,0:T(8,128)(2,1)S(1)}, u32[]{:S(2)}, u32[]{:S(2)}) async-start(bf16[4,2,64,512]{3,2,1,0:T(8,128)(2,1)} %copy.56), calls=%async_computation | async-start | bytes 1048576 | tf_op jit(solution)/shard_map/all_to_all | solution.py:135
  67.9 8.1 %all-to-all-done = bf16[4,2,64,512]{3,2,1,0:T(8,128)(2,1)S(1)} async-done(((bf16[4,2,64,512]{3,2,1,0:T(8,128)(2,1)}), bf16[4,2,64,512]{3,2,1,0:T(8,128)(2,1)S(1)}, u32[]{:S(2)}, u32[]{:S(2)}) %all-to-all-start) | async-done | bytes 524320 | tf_op jit(solution)/shard_map/all_to_all | solution.py:135
  76.8 0.5 rev.3
  77.4 1.1 fusion.42
  78.5 0.8 reshape.275
  79.3 3.9 %all-to-all-start.1 = ((bf16[8,32,512]{2,1,0:T(8,128)(2,1)}), bf16[8,32,512]{2,1,0:T(8,128)(2,1)S(1)}, u32[]{:S(2)}, u32[]{:S(2)}) async-start(bf16[8,32,512]{2,1,0:T(8,128)(2,1)} %reshape.275), calls=%async_computation.1 | async-start | bytes 524288 | tf_op jit(solution)/shard_map/all_to_all | solution.py:147
  83.4 8.5 %all-to-all-done.1 = bf16[8,32,512]{2,1,0:T(8,128)(2,1)S(1)} async-done(((bf16[8,32,512]{2,1,0:T(8,128)(2,1)}), bf16[8,32,512]{2,1,0:T(8,128)(2,1)S(1)}, u32[]{:S(2)}, u32[]{:S(2)}) %all-to-all-start.1) | async-done | bytes 262176 | tf_op jit(solution)/shard_map/all_to_all | solution.py:147
  93.1 0.7 collective-permute-start.11
  93.8 2.7 %multiply_reduce_fusion = (bf16[1024]{0:T(1024)(128)(2,1)S(1)}, bf16[1024]{0:T(1024)(128)(2,1)S(1)}, bf16[1024]{0:T(1024)(128)(2,1)S(1)}, bf16[1024]{0:T(1024)(1...) fusion(f32[136,1024]{1,0:T(8,128)S(1)} %pad_convert_fusion, ...), kind=kOutput, calls=%fused_computation.76 | convolution fusion | flops 273013760 | bytes 8150016 | tf_op jit(solution)/shard_map/dot_general | solution.py:170
  96.5 0.9 fusion.89
  97.7 1.8 %fusion.37 = f32[256,2048]{1,0:T(8,128)} fusion(bf16[128,1024]{1,0:T(8,128)(2,1)S(1)} %multiply_convert_fusion.1, bf16[128,1024]{1,0:T(8,128)(2,1)S(1)} %get-tuple-element.37, bf16[128,512]{0,1:T(8,128)(2,1)S(1)} %get-tuple-element.42), kind=kOutput, calls=%fused_computation.102 | convolution fusion | flops 135266304 | bytes 2686976 | tf_op jit(solution)/shard_map/dot_general | solution.py:193
  99.4 1.3 fusion.55
  101.0 1.5 collective-permute-start.7
  103.0 1.6 convolution_add_fusion.5
  104.6 1.4 convolution_add_fusion.4
  106.1 1.9 %fusion.1 = bf16[256,1024]{1,0:T(8,128)(2,1)} fusion(f32[256,1024]{1,0:T(8,128)S(1)} %convolution_add_fusion.4, bf16[128,1024]{1,0:T(8,128)(2,1)S(1)} %collective-permute-done.12, bf16[128,512]{0,1:T(8,128)(2,1)} %collective-permute-done.8), kind=kOutput, calls=%fused_computation.9 | convolution fusion | flops 67633152 | bytes 1900544 | tf_op jit(solution)/shard_map/dot_general | solution.py:197
  108.0 8.8 %collective-permute-done.7 = bf16[144,2048]{1,0:T(8,128)(2,1)S(1)} collective-permute-done((bf16[144,2048]{1,0:T(8,128)(2,1)S(1)}, bf16[144,2048]{1,0:T(8,128)(2,1)S(1)}, u32[]{:S(2)}, u32[]{:S(2)}) %collective-permute-start.7) | collective-permute-done | bytes 589856 | tf_op jit(solution)/shard_map/ppermute | solution.py:163
  116.8 1.3 convolution_add_fusion.2
  118.1 2.6 %convolution_add_fusion.1 = f32[256,2048]{1,0:T(8,128)} fusion(f32[256,2048]{1,0:T(8,128)S(1)} %convolution_add_fusion.2, bf16[144,2048]{1,0:T(8,128)(2,1)S(1)} %collective-permute-done.7, bf16[128,512]{0,1:T(8,128)(2,1)} %collective-permute-done.6), kind=kOutput, calls=%fused_computation.2 | convolution fusion | flops 134742016 | bytes 4784128 | tf_op jit(solution)/shard_map/dot_general | solution.py:193
  120.7 0.8 copy-done.7
  121.9 2.2 %fusion = bf16[256,2048]{1,0:T(8,128)(2,1)S(1)} fusion(f32[256,2048]{1,0:T(8,128)} %convolution_add_fusion.1, bf16[144,2048]{1,0:T(8,128)(2,1)} %copy-done.7, bf16[128,512]{0,1:T(8,128)(2,1)} %collective-permute-done.8), kind=kOutput, calls=%fused_computation.4 | convolution fusion | flops 135266304 | bytes 3735552 | tf_op jit(solution)/shard_map/dot_general | solution.py:193
  124.2 2.4 %pad_maximum_fusion = bf16[8,32,3200]{2,1,0:T(8,128)(2,1)} fusion(bf16[8,32,128]{2,1,0:T(8,128)(2,1)S(1)} %bitcast.132, bf16[8,32,1024]{2,1,0:T(8,128)(2,1)} %bitcast.119, bf16[8,32,2048]{2,1,0:T(8,128)(2,1)S(1)} %bitcast.118), kind=kLoop, calls=%fused_computation.5 | loop fusion | flops 4915200 | bytes 3276800 | tf_op jit(solution)/shard_map/concatenate | solution.py:207
  126.5 4.4 %all-to-all-start.2 = ((bf16[8,32,3200]{2,1,0:T(8,128)(2,1)}), bf16[8,32,3200]{2,1,0:T(8,128)(2,1)}, u32[]{:S(2)}, u32[]{:S(2)}) async-start(bf16[8,32,3200]{2,1,0:T(8,128)(2,1)} %pad_maximum_fusion), calls=%async_computation.2 | async-start | bytes 3276800 | tf_op jit(solution)/shard_map/all_to_all | solution.py:209
  131.0 3.8 %fusion.88 = (f32[128]{0:T(128)S(1)}, f32[128]{0:T(128)S(1)}, f32[128,1024]{1,0:T(8,128)S(1)}) fusion(f32[128]{0:T(128)S(1)} %add_rsqrt_fusion, f32[128]{0:T(128)S(1)} %broadcast_multiply_fusion.2, bf16[128,1024]{1,0:T(8,128)(2,1)S(1)} %copy-done.5, bf16[1024,2048]{1,0:T(8,128)(2,1)} %param.13, bf16[128,1024]{1,0:T(8,128)(2,1)S(1)} %multiply_convert_fusion.1, ...), kind=kOutput, calls=%fused_computation.197 | convolution fusion | flops 538705664 | bytes 5507072 | tf_op jit(solution)/shard_map/dot_general | solution.py:214
  134.8 1.0 fusion.21
  135.8 34.6 %all-to-all-done.2 = bf16[8,32,3200]{2,1,0:T(8,128)(2,1)} async-done(((bf16[8,32,3200]{2,1,0:T(8,128)(2,1)}), bf16[8,32,3200]{2,1,0:T(8,128)(2,1)}, u32[]{:S(2)}, u32[]{:S(2)}) %all-to-all-start.2) | async-done | bytes 1638432 | tf_op jit(solution)/shard_map/all_to_all | solution.py:209
  170.3 1.7 convert_reduce_fusion
  172.0 0.7 slice.349
  172.7 0.7 slice.348
  173.4 0.7 copy.66
  (95 shorter events, 4.9 us)
Async XLA Ops:
  0.6 93.2 %copy-start = (bf16[1024,1024]{1,0:T(8,128)(2,1)S(1)}, bf16[1024,1024]{1,0:T(8,128)(2,1)}, u32[]{:S(2)}) copy-start(bf16[1024,1024]{1,0:T(8,128)(2,1)} %param.17) | copy-start | bytes 6291460
  0.6 31.0 %collective-permute-start.1 = (bf16[128,2048]{1,0:T(8,128)(2,1)}, bf16[128,2048]{1,0:T(8,128)(2,1)}, u32[]{:S(2)}, u32[]{:S(2)}) collective-permute-start(bf16[128,2048]{1,0:T(8,128)(2,1)} %param.19), channel_id=1, source_target_pairs={{0,8},{4,12},{8,16},{12,20},{16,24},{20,28},{24,0},{28,4},{1,9},{5... | collective-permute-start | bytes 1572872 | tf_op jit(solution)/shard_map/ppermute | solution.py:82
  3.7 31.4 %collective-permute-start.3 = (bf16[128,2048]{1,0:T(8,128)(2,1)}, bf16[128,2048]{1,0:T(8,128)(2,1)}, u32[]{:S(2)}, u32[]{:S(2)}) collective-permute-start(bf16[128,2048]{1,0:T(8,128)(2,1)} %param.19), channel_id=1, source_target_pairs={{0,24},{4,28},{8,0},{12,4},{16,8},{20,12},{24,16},{28,20},{1,25},{... | collective-permute-start | bytes 1572872 | tf_op jit(solution)/shard_map/ppermute | solution.py:82
  5.8 45.9 %collective-permute-start.2 = (bf16[128,2048]{1,0:T(8,128)(2,1)}, bf16[128,2048]{1,0:T(8,128)(2,1)}, u32[]{:S(2)}, u32[]{:S(2)}) collective-permute-start(bf16[128,2048]{1,0:T(8,128)(2,1)} %param.19), channel_id=1, source_target_pairs={{0,16},{4,20},{8,24},{12,28},{16,0},{20,4},{24,8},{28,12},{1,17},{... | collective-permute-start | bytes 1572872 | tf_op jit(solution)/shard_map/ppermute | solution.py:82
  6.8 46.5 %collective-permute-start = (bf16[256,2048]{1,0:T(8,128)(2,1)}, bf16[256,2048]{1,0:T(8,128)(2,1)}, u32[]{:S(2)}, u32[]{:S(2)}) collective-permute-start(bf16[256,2048]{1,0:T(8,128)(2,1)} %param.18), channel_id=1, source_target_pairs={{0,4},{4,0},{8,12},{12,8},{16,20},{20,16},{24,28},{28,24},{1,5},{5... | collective-permute-start | bytes 3145736 | tf_op jit(solution)/shard_map/ppermute | solution.py:78
  21.4 1.0 copy-start.2
  22.4 0.7 copy-start.10
  22.4 0.7 copy-start.11
  24.9 3.7 %copy-start.6 = (bf16[128,2048]{1,0:T(8,128)(2,1)S(1)}, bf16[128,2048]{1,0:T(8,128)(2,1)}, u32[]{:S(2)}) copy-start(bf16[128,2048]{1,0:T(8,128)(2,1)} %param.19) | copy-start | bytes 1572868
  24.9 5.9 %copy-start.9 = (s32[2048,1]{0,1:T(1,128)S(1)}, s32[2048,1]{0,1:T(1,128)}, u32[]{:S(2)}) copy-start(s32[2048,1]{0,1:T(1,128)} %param.20) | copy-start | bytes 24580
  28.6 77.4 %collective-permute-start.8 = (bf16[128,512]{0,1:T(8,128)(2,1)}, bf16[128,512]{0,1:T(8,128)(2,1)}, u32[]{:S(2)}, u32[]{:S(2)}) collective-permute-start(bf16[128,512]{0,1:T(8,128)(2,1)} %get-tuple-element.41), channel_id=1, source_target_pairs={{0,3},{1,2},{2,1},{3,0},{4,7},{5,6},{6,5},{7,4},{8,11},{9,10},{10,... | collective-permute-start | bytes 393224 | tf_op jit(solution)/shard_map/ppermute | solution.py:126
  31.6 20.1 %copy-start.1 = (bf16[256,2048]{1,0:T(8,128)(2,1)S(1)}, bf16[256,2048]{1,0:T(8,128)(2,1)}, u32[]{:S(2)}) copy-start(bf16[256,2048]{1,0:T(8,128)(2,1)} %param.18) | copy-start | bytes 3145732
  31.6 69.3 %collective-permute-start.4 = (bf16[128,512]{0,1:T(8,128)(2,1)}, bf16[128,512]{0,1:T(8,128)(2,1)}, u32[]{:S(2)}, u32[]{:S(2)}) collective-permute-start(bf16[128,512]{0,1:T(8,128)(2,1)} %get-tuple-element.43), channel_id=1, source_target_pairs={{0,1},{1,0},{2,3},{3,2},{4,5},{5,4},{6,7},{7,6},{8,9},{9,8},{10,11... | collective-permute-start | bytes 393224 | tf_op jit(solution)/shard_map/ppermute | solution.py:126
  35.1 69.5 %collective-permute-start.6 = (bf16[128,512]{0,1:T(8,128)(2,1)}, bf16[128,512]{0,1:T(8,128)(2,1)}, u32[]{:S(2)}, u32[]{:S(2)}) collective-permute-start(bf16[128,512]{0,1:T(8,128)(2,1)} %get-tuple-element.44), channel_id=1, source_target_pairs={{0,2},{1,3},{2,0},{3,1},{4,6},{5,7},{6,4},{7,5},{8,10},{9,11},{10,... | collective-permute-start | bytes 393224 | tf_op jit(solution)/shard_map/ppermute | solution.py:126
  60.4 7.2 %copy-start.8 = (s32[2048]{0:T(1024)S(1)}, s32[2048]{0:T(1024)}, u32[]{:S(2)}) copy-start(s32[2048]{0:T(1024)} %param.21) | copy-start | bytes 24580
  63.7 12.3 %all-to-all-start = ((bf16[4,2,64,512]{3,2,1,0:T(8,128)(2,1)}), bf16[4,2,64,512]{3,2,1,0:T(8,128)(2,1)S(1)}, u32[]{:S(2)}, u32[]{:S(2)}) async-start(bf16[4,2,64,512]{3,2,1,0:T(8,128)(2,1)} %copy.56), calls=%async_computation | async-start | bytes 1048576 | tf_op jit(solution)/shard_map/all_to_all | solution.py:135
  79.3 12.6 %all-to-all-start.1 = ((bf16[8,32,512]{2,1,0:T(8,128)(2,1)}), bf16[8,32,512]{2,1,0:T(8,128)(2,1)S(1)}, u32[]{:S(2)}, u32[]{:S(2)}) async-start(bf16[8,32,512]{2,1,0:T(8,128)(2,1)} %reshape.275), calls=%async_computation.1 | async-start | bytes 524288 | tf_op jit(solution)/shard_map/all_to_all | solution.py:147
  93.1 9.3 %collective-permute-start.11 = (bf16[128,1024]{1,0:T(8,128)(2,1)S(1)}, bf16[128,1024]{1,0:T(8,128)(2,1)}, u32[]{:S(2)}, u32[]{:S(2)}) collective-permute-start(bf16[128,1024]{1,0:T(8,128)(2,1)S(1)} %reshape.277), channel_id=1, source_target_pairs={{0,2},{1,3},{2,0},{3,1},{4,6},{5,7},{6,4},{7,5},{8,10},{9,11},{10,... | collective-permute-start | bytes 786440 | tf_op jit(solution)/shard_map/ppermute | solution.py:163
  93.8 8.8 %collective-permute-start.10 = (bf16[128,1024]{1,0:T(8,128)(2,1)S(1)}, bf16[128,1024]{1,0:T(8,128)(2,1)}, u32[]{:S(2)}, u32[]{:S(2)}) collective-permute-start(bf16[128,1024]{1,0:T(8,128)(2,1)S(1)} %reshape.277), channel_id=1, source_target_pairs={{0,1},{1,0},{2,3},{3,2},{4,5},{5,4},{6,7},{7,6},{8,9},{9,8},{10,11... | collective-permute-start | bytes 786440 | tf_op jit(solution)/shard_map/ppermute | solution.py:164
  93.8 2.7 %copy-start.3 = (f32[128,2048]{1,0:T(8,128)S(1)}, f32[128,2048]{1,0:T(8,128)}, u32[]{:S(2)}) copy-start(f32[128,2048]{1,0:T(8,128)} %copy-done.2) | copy-start | bytes 3145732
  101.0 15.8 %collective-permute-start.7 = (bf16[144,2048]{1,0:T(8,128)(2,1)S(1)}, bf16[144,2048]{1,0:T(8,128)(2,1)S(1)}, u32[]{:S(2)}, u32[]{:S(2)}) collective-permute-start(bf16[144,2048]{1,0:T(8,128)(2,1)S(1)} %fusion.16), channel_id=1, source_target_pairs={{0,2},{1,3},{2,0},{3,1},{4,6},{5,7},{6,4},{7,5},{8,10},{9,11},{10,... | collective-permute-start | bytes 1769480 | tf_op jit(solution)/shard_map/ppermute | solution.py:163
  102.5 14.3 %collective-permute-start.5 = (bf16[144,2048]{1,0:T(8,128)(2,1)S(1)}, bf16[144,2048]{1,0:T(8,128)(2,1)S(1)}, u32[]{:S(2)}, u32[]{:S(2)}) collective-permute-start(bf16[144,2048]{1,0:T(8,128)(2,1)S(1)} %fusion.16), channel_id=1, source_target_pairs={{0,1},{1,0},{2,3},{3,2},{4,5},{5,4},{6,7},{7,6},{8,9},{9,8},{10,11... | collective-permute-start | bytes 1769480 | tf_op jit(solution)/shard_map/ppermute | solution.py:164
  102.7 3.4 %collective-permute-start.12 = (bf16[128,1024]{1,0:T(8,128)(2,1)}, bf16[128,1024]{1,0:T(8,128)(2,1)S(1)}, u32[]{:S(2)}, u32[]{:S(2)}) collective-permute-start(bf16[128,1024]{1,0:T(8,128)(2,1)} %collective-permute-done.11), channel_id=1, source_target_pairs={{0,1},{1,0},{2,3},{3,2},{4,5},{5,4},{6,7},{7,6},{8,9},{9,8},{10,11... | collective-permute-start | bytes 786440 | tf_op jit(solution)/shard_map/ppermute | solution.py:165
  104.6 12.2 %copy-start.4 = (f32[256,2048]{1,0:T(8,128)S(1)}, f32[256,2048]{1,0:T(8,128)}, u32[]{:S(2)}) copy-start(f32[256,2048]{1,0:T(8,128)} %fusion.37) | copy-start | bytes 6291460
  116.8 3.9 %collective-permute-start.9 = (bf16[144,2048]{1,0:T(8,128)(2,1)S(1)}, bf16[144,2048]{1,0:T(8,128)(2,1)S(1)}, u32[]{:S(2)}, u32[]{:S(2)}) collective-permute-start(bf16[144,2048]{1,0:T(8,128)(2,1)S(1)} %collective-permute-done.7), channel_id=1, source_target_pairs={{0,1},{1,0},{2,3},{3,2},{4,5},{5,4},{6,7},{7,6},{8,9},{9,8},{10,11... | collective-permute-start | bytes 1769480 | tf_op jit(solution)/shard_map/ppermute | solution.py:165
  120.7 0.8 copy-start.7
  126.5 4.5 %copy-start.5 = (bf16[128,1024]{1,0:T(8,128)(2,1)S(1)}, bf16[128,1024]{1,0:T(8,128)(2,1)}, u32[]{:S(2)}) copy-start(bf16[128,1024]{1,0:T(8,128)(2,1)} %param.11) | copy-start | bytes 786436
  126.5 43.8 %all-to-all-start.2 = ((bf16[8,32,3200]{2,1,0:T(8,128)(2,1)}), bf16[8,32,3200]{2,1,0:T(8,128)(2,1)}, u32[]{:S(2)}, u32[]{:S(2)}) async-start(bf16[8,32,3200]{2,1,0:T(8,128)(2,1)} %pad_maximum_fusion), calls=%async_computation.2 | async-start | bytes 3276800 | tf_op jit(solution)/shard_map/all_to_all | solution.py:209

commit v2 on v1

v2 whole, which is shorter than its diff:
```python
import jax
import jax.numpy as jnp
from jax import lax
from jax.experimental import pallas as pl
from jax.experimental.pallas import tpu as pltpu
from jax.sharding import PartitionSpec as P

BF = jnp.bfloat16
F32 = jnp.float32
ROWS = (((0,), (0,)), ((), ()))
COLS = (((1,), (1,)), ((), ()))


def xor_perm(count, mask):
    return [(i, i ^ mask) for i in range(count)]


def size_of(axis):
    if isinstance(axis, tuple):
        return lax.axis_size(axis[0]) * lax.axis_size(axis[1])
    return lax.axis_size(axis)


def swap(axis, values, mask):
    return lax.ppermute(values, axis, xor_perm(size_of(axis), mask))


def xor_order(items, place):
    step = 1
    while step < len(items):
        flip = jnp.bitwise_and(place, step) > 0
        items = [jnp.where(flip, items[i ^ step], items[i]) for i in range(len(items))]
        step *= 2
    return items


def local_call(body, ids, operands, outs, scratch=(), flops=0, name=None):
    moved = sum(o.size * o.dtype.itemsize for o in operands) + sum(
        o.size * o.dtype.itemsize for o in outs
    )
    return pl.pallas_call(
        body,
        out_shape=tuple(outs),
        in_specs=[pl.BlockSpec(memory_space=pltpu.SMEM)] + [pl.BlockSpec(memory_space=pltpu.VMEM)] * len(operands),
        out_specs=tuple(pl.BlockSpec(memory_space=pltpu.VMEM) for _ in outs),
        scratch_shapes=list(scratch),
        compiler_params=pltpu.CompilerParams(vmem_limit_bytes=24 * 1024 * 1024),
        cost_estimate=pl.CostEstimate(flops=flops, bytes_accessed=moved, transcendentals=0),
        name=name,
    )(ids, *operands)


def like(shape, dtype):
    return jax.ShapeDtypeStruct(shape, dtype)


def aligned(index, size):
    return pl.ds(pl.multiple_of(index * size, size), size)


def forward_kernel(
    ids, x, w_one, taps, scale, shift,
    standard, inverse, linear, gate_prob, gated, slope, masks, mine, theirs, wide, flipped,
):
    core = ids[3]
    frame_rows, feat = x.shape
    taps_count = taps.shape[0]
    half = taps_count // 2
    utterances = ids.shape[0] - 4
    ends = [ids[4]]
    for u in range(1, utterances):
        ends.append(ends[-1] + ids[4 + u])
    position = lax.broadcasted_iota(jnp.int32, (frame_rows, 128), 0)

    def segment(at):
        return sum(jnp.where(at >= e, 1, 0) for e in ends)

    here = segment(position)
    for k in range(taps_count):
        at = position + (k - half)
        good = (segment(at) == here) & (at >= 0) & (at < frame_rows)
        masks[k] = jnp.where(good, 1.0, 0.0)
    as_float = x[...].astype(F32)
    centred = as_float - jnp.mean(as_float, axis=1, keepdims=True)
    inv = lax.rsqrt(jnp.mean(centred * centred, axis=1, keepdims=True) + 1e-05)
    inverse[...] = jnp.broadcast_to(inv, inverse.shape)
    standard[...] = centred * inv
    normed = standard[...].astype(BF)
    edge = jnp.zeros((8, feat), F32)
    wide[0:8, :] = edge
    wide[8 + frame_rows : 16 + frame_rows, :] = edge
    step = 256
    for c in range(feat // step):
        cols = slice(c * step, (c + 1) * step)
        lin = jnp.dot(normed, w_one[:, cols], preferred_element_type=F32)
        gate = jax.nn.sigmoid(
            jnp.dot(normed, w_one[:, feat + c * step : feat + (c + 1) * step], preferred_element_type=F32)
        )
        linear[:, cols] = lin
        gate_prob[:, cols] = gate
        product = (lin * gate).astype(BF)
        gated[:, cols] = product
        wide[8 : 8 + frame_rows, cols] = product.astype(F32)
    for c in range(feat // 128):
        cols = slice(c * 128, (c + 1) * 128)
        total = jnp.zeros((frame_rows, 128), F32)
        for k in range(taps_count):
            start = 8 + k - half
            total = total + taps[k : k + 1, cols] * (wide[start : start + frame_rows, cols] * masks[k])
        pre = total * scale[:, cols] + shift[:, cols]
        prob = jax.nn.sigmoid(pre)
        slope[:, cols] = prob * (1.0 + pre * (1.0 - prob)) * scale[:, cols]
        flipped[0, cols, :] = normed[:, cols].astype(F32).T
        flipped[1, cols, :] = (pre * prob).astype(BF).astype(F32).T
    groups = mine.shape[0] // feat * 16
    part = feat // (2 * groups)
    for h in range(2):
        for g in range(groups):
            at = slice(h * (feat // 2) + g * part, h * (feat // 2) + (g + 1) * part)
            mine[at, :] = flipped[h, aligned(2 * g + core, part), :].astype(BF)
            theirs[at, :] = flipped[h, aligned(2 * g + 1 - core, part), :].astype(BF)


def partial_kernel(ids, *refs):
    own_rows, other_rows, *blocks = refs[:-5]
    outs, rows = refs[-5:-1], refs[-1]
    sec, z = ids[0], ids[1]
    quarter = outs[0].shape[0] // 2
    piece = blocks[0].shape[0]
    if len(blocks) == 2:
        middle = (z == 1) | (z == 2)
        lots = [jnp.where(middle, blocks[0][...], blocks[1][...])]
    else:
        lots = [jnp.concatenate([blocks[0][...], blocks[1][...]], axis=0), blocks[2][...]]
    first = 0
    for lot in lots:
        last = first + lot.shape[0]
        for w, a in enumerate((own_rows, other_rows)):
            rows[w, :, first:last] = lax.dot_general(a[...], lot, COLS, preferred_element_type=F32)
        first = last
    for m, out in enumerate(outs):
        q = jnp.bitwise_xor(sec, m)
        for w in range(2):
            out[w * quarter : (w + 1) * quarter, :] = rows[w, aligned(q, quarter), :].astype(out.dtype)


def packing_kernel(ids, own, r1, r2, r3, own_last, l1, l2, l3, pack, out):
    total = own[...] + r1[...].astype(F32) + r2[...].astype(F32) + r3[...].astype(F32)
    last = own_last[...] + l1[...].astype(F32) + l2[...].astype(F32) + l3[...].astype(F32)
    piece = last.shape[1]
    parts = xor_order([total[:, k * piece : (k + 1) * piece] for k in range(3)] + [last], ids[1])
    rows = jnp.concatenate(parts, axis=1).astype(BF)
    out[...] = jnp.dot(pack[...], rows, preferred_element_type=F32).astype(BF)


def module_kernel(
    ids, incoming, order, w_two, slope, gated, masks, gate_prob, linear, taps, halves,
    grad_out, grad_mixed, p0, p2, p4, p6, wide_gated, wide_grad,
):
    place = ids[2]
    frame_rows, feat = grad_out.shape
    taps_count = taps.shape[0]
    half = taps_count // 2
    sources, slots, width = incoming.shape
    outer = sources // 2
    piece = width // outer
    frame_ids = lax.broadcasted_iota(jnp.int32, (frame_rows, outer * slots), 0)
    for p in range(2):
        pick = (frame_ids == order[p : p + 1, :]).astype(F32).astype(BF)
        rows = jnp.concatenate([incoming[2 * o + p] for o in range(outer)], axis=0)
        got = jnp.dot(pick, rows, preferred_element_type=F32).astype(BF)
        for o in range(outer):
            first = (2 * o + p) * piece
            grad_out[:, first : first + piece] = got[:, o * piece : (o + 1) * piece]
    edge = jnp.zeros((8, feat), F32)
    for wide in (wide_gated, wide_grad):
        wide[0:8, :] = edge
        wide[8 + frame_rows : 16 + frame_rows, :] = edge
    wide_gated[8 : 8 + frame_rows, :] = gated[...].astype(F32)
    grad_act = lax.dot_general(grad_out[...], w_two[...], COLS, preferred_element_type=F32)
    wide_grad[8 : 8 + frame_rows, :] = grad_act * slope[...]
    step = 128
    tap_rows = []
    for c in range(feat // step):
        cols = slice(c * step, (c + 1) * step)
        grad_conv = wide_grad[8 : 8 + frame_rows, cols]
        total = jnp.zeros((frame_rows, step), F32)
        columns = []
        for k in range(taps_count):
            start = 8 + k - half
            window = wide_gated[start : start + frame_rows, cols] * masks[k]
            columns.append(jnp.sum(window * grad_conv, axis=0, keepdims=True))
            start = 8 + half - k
            back = 2 * half - k
            total = total + taps[k : k + 1, cols] * (
                wide_grad[start : start + frame_rows, cols] * masks[back]
            )
        tap_rows.append(jnp.concatenate(columns + [jnp.zeros((16 - taps_count, step), F32)], axis=0))
        gate = gate_prob[:, cols]
        first = total * gate
        grad_mixed[:, c * step : (c + 1) * step] = first.astype(BF)
        grad_mixed[:, feat + c * step : feat + (c + 1) * step] = (first * linear[:, cols] * (1.0 - gate)).astype(BF)
    tap_rows = jnp.concatenate(tap_rows, axis=1).astype(BF)
    tap_halves = jnp.dot(tap_rows, halves[...], preferred_element_type=F32)
    tap_halves = tap_halves.astype(BF)
    w1_cols, w2_cols = feat // 2, feat // 4
    for mask, out in enumerate((p0, p2, p4, p6)):
        q = jnp.bitwise_xor(place, mask)
        out[0:frame_rows, 0:w1_cols] = grad_mixed[:, aligned(q, w1_cols)]
        out[0:frame_rows, w1_cols:] = grad_out[:, aligned(q, w2_cols)]
        for h in range(2):
            tap_at = slice(frame_rows + 16 * h, frame_rows + 16 * (h + 1))
            out[tap_at, 0:w1_cols] = tap_halves[:, h * w1_cols : (h + 1) * w1_cols]
            out[tap_at, w1_cols:] = jnp.zeros((16, w2_cols), BF)


def weights_kernel(ids, e0, e1, e2, e3, e4, e5, e6, e7, g0, g1, g2, g3, g4, g5, g6, g7, own, s1, s2, s3, rows, tap_sum):
    z, core = ids[1], ids[3]
    frame_rows = e0.shape[1]
    half = e0.shape[0] // 2
    w1_cols = half
    tap_sum[...] = sum(
        g[aligned(core + frame_rows // 16, 16), 0:w1_cols].astype(F32) for g in (g0, g1, g2, g3, g4, g5, g6, g7))
    pairs = ((e0, e1, g0, g1), (e2, e3, g2, g3), (e4, e5, g4, g5), (e6, e7, g6, g7))
    for cols, first in ((slice(0, w1_cols), 0), (slice(w1_cols, g0.shape[1]), half)):
        total = None
        for ea, eb, ga, gb in pairs:
            both = jnp.concatenate([ga[0:frame_rows, cols], gb[0:frame_rows, cols]], axis=0)
            feats = jnp.concatenate([ea[first : first + half, :], eb[first : first + half, :]], axis=1)
            term = jnp.dot(feats, both, preferred_element_type=F32)
            total = term if total is None else total + term
        rows[:, cols] = total
    block = half // 4
    for m, out in enumerate((own, s1, s2, s3)):
        o = jnp.bitwise_xor(z, m)
        out[0:block, :] = rows[aligned(o, block), :].astype(out.dtype)
        out[block:, 0:block] = tap_sum[:, aligned(o, block)].astype(out.dtype)
        out[block:, block:] = jnp.zeros((out.shape[0] - block, out.shape[1] - block), out.dtype)


def sum_kernel(ids, own, r1, r2, r3, mine, f1, f2, f3, taps, rows):
    place = ids[2]
    block = taps.shape[1]
    rows[...] = own[...] + r1[...].astype(F32) + r2[...].astype(F32) + r3[...].astype(F32)
    part = block // 4
    for m, out in enumerate((mine, f1, f2, f3)):
        out[...] = rows[aligned(jnp.bitwise_xor(place, m), part), :].astype(out.dtype)
    taps[...] = rows[block:, 0:block]


def assembly_kernel(ids, mine, r1, r2, r3, w1, w2):
    place = ids[2]
    w1_cols, w2_cols = w1.shape[1] // 4, w2.shape[1] // 4
    for m, part in enumerate((mine, r1, r2, r3)):
        q = jnp.bitwise_xor(place, m)
        w1[:, aligned(q, w1_cols)] = part[:, 0:w1_cols].astype(F32)
        w2[:, aligned(q, w2_cols)] = part[:, w1_cols:].astype(F32)


def forward_part(layer_input, lengths, w_one, conv_taps, conv_scale, conv_shift):
    row_count, feat_width = layer_input.shape
    taps_count = conv_taps.shape[0]
    half_span = taps_count // 2
    ends = [lengths[0]]
    for j in range(1, lengths.shape[0]):
        ends.append(ends[-1] + lengths[j])
    position = lax.broadcasted_iota(jnp.int32, (row_count,), 0)
    segment = sum((position >= e).astype(jnp.int32) for e in ends)
    padded_seg = jnp.pad(segment, (half_span, half_span), constant_values=-1)
    as_float = layer_input.astype(F32)
    row_mean = jnp.mean(as_float, axis=1, keepdims=True)
    centred = as_float - row_mean
    inverse = lax.rsqrt(jnp.mean(centred * centred, axis=1, keepdims=True) + 1e-05)
    standard = centred * inverse
    normed = standard.astype(BF)
    mixed = jnp.dot(normed, w_one, preferred_element_type=F32)
    linear = mixed[:, :feat_width]
    gate_prob = jax.nn.sigmoid(mixed[:, feat_width:])
    gated = (linear * gate_prob).astype(BF)
    padded_gated = jnp.pad(gated, ((half_span, half_span), (0, 0))).astype(F32)
    tap_values = conv_taps.astype(F32)
    conv_sum = jnp.zeros((row_count, feat_width), F32)
    for k in range(taps_count):
        same_utt = padded_seg[k : k + row_count] == segment
        window = jnp.where(same_utt[:, None], padded_gated[k : k + row_count], 0.0)
        conv_sum = conv_sum + tap_values[k] * window
    pre_act = conv_sum * conv_scale + conv_shift
    act_prob = jax.nn.sigmoid(pre_act)
    activated = (pre_act * act_prob).astype(BF)
    slope = act_prob * (1.0 + pre_act * (1.0 - act_prob)) * conv_scale
    return standard, inverse, normed, linear, gate_prob, padded_gated, padded_seg, segment, activated, slope


def plain_shards(
    layer_input,
    utt_frames,
    w_pointwise1,
    conv_taps,
    conv_scale,
    conv_shift,
    w_pointwise2,
    adj_grad,
    proj_weight,
    adj_target,
    adj_frame,
):
    reps = lax.axis_size("rep")
    sections = lax.axis_size("section")
    rep_here = lax.axis_index("rep")
    sec_here = lax.axis_index("section")
    block_rows = adj_grad.shape[0]
    quarter = block_rows // sections
    frame_rows, feat = layer_input.shape
    taps_count = conv_taps.shape[0]
    half_span = taps_count // 2
    capacity = max(2, 2 * quarter // reps)
    outer = reps // 2
    pair_here = rep_here % 2
    outer_here = rep_here // 2
    piece = proj_weight.shape[0]

    adj_other = swap("rep", adj_grad, 1)
    blocks = [proj_weight] + [swap("rep", proj_weight, 2 * k) for k in range(1, outer)]

    targets = adj_target[:, 0].reshape(reps, sections, quarter)
    frames = adj_frame.reshape(reps, sections, quarter)
    sec_targets = lax.dynamic_index_in_dim(targets, sec_here, 1, keepdims=False)
    sec_frames = lax.dynamic_index_in_dim(frames, sec_here, 1, keepdims=False)
    row_a = lax.broadcasted_iota(jnp.int32, (quarter, quarter), 0)
    row_b = lax.broadcasted_iota(jnp.int32, (quarter, quarter), 1)
    same = (sec_targets[:, :, None] == sec_targets[:, None, :]) & (row_b < row_a)[None]
    rank = jnp.sum(same.astype(jnp.int32), axis=2)
    mine = sec_targets == rep_here
    slots = lax.broadcasted_iota(jnp.int32, (1, capacity, 1), 1)
    hit = mine[:, None, :] & (rank[:, None, :] == slots)
    slot_frames = jnp.sum(jnp.where(hit, sec_frames[:, None, :] + 1, 0), axis=2) - 1

    pair_blocks = jnp.stack([rep_here, jnp.bitwise_xor(rep_here, 1)])
    pair_targets = jnp.concatenate([lax.dynamic_index_in_dim(sec_targets, pair_blocks[w], 0, keepdims=False) for w in range(2)])
    pair_rank = jnp.concatenate([lax.dynamic_index_in_dim(rank, pair_blocks[w], 0, keepdims=False) for w in range(2)])
    member = lax.broadcasted_iota(jnp.int32, (2 * quarter,), 0) // quarter
    slot_of = (pair_targets * 2 + member) * capacity + pair_rank
    slot_ids = lax.broadcasted_iota(jnp.int32, (reps * 2 * capacity, 2 * quarter), 0)
    pack = (slot_of[None, :] == slot_ids).astype(BF)

    standard, inverse, normed, linear, gate_prob, padded_gated, padded_seg, segment, activated, slope = forward_part(
        layer_input, utt_frames[0], w_pointwise1, conv_taps, conv_scale, conv_shift
    )
    part_rows = feat // (reps * sections)

    here = rep_here * sections + sec_here
    core = here % 2
    place = (here // 2) % 4
    BOTH = ("rep", "section")

    def core_halves(values):
        return values.reshape(frame_rows, reps * sections // 2, 2, part_rows).transpose(2, 0, 1, 3).reshape(
            2, frame_rows, feat // 2
        )

    halves = jnp.concatenate([core_halves(normed), core_halves(activated)], axis=2)
    mine_half = lax.dynamic_index_in_dim(halves, core, 0, keepdims=False)
    their_half = lax.dynamic_index_in_dim(halves, 1 - core, 0, keepdims=False)
    chip_half = jnp.concatenate([mine_half, swap(BOTH, their_half, 1)], axis=0)
    early = {0: chip_half}
    for m in (2, 4, 6):
        early[m] = swap(BOTH, chip_half, m)
    near = early[0]
    straight = jnp.concatenate([early[m][:frame_rows] for m in (2, 4, 6)], axis=0)
    across = jnp.concatenate([early[m][frame_rows:] for m in (2, 4, 6)], axis=0)

    adj_pair = jnp.concatenate([adj_grad, adj_other], axis=0)

    def section_sum(lot):
        terms = [lax.dot_general(adj_pair, b, COLS, preferred_element_type=F32).astype(BF) for b in lot]
        terms = jnp.concatenate(terms, axis=1).reshape(2, sections, quarter, len(lot) * piece)
        total = lax.dynamic_index_in_dim(terms, sec_here, 1, keepdims=False).astype(F32)
        for m in range(1, sections):
            given = lax.dynamic_index_in_dim(terms, jnp.bitwise_xor(sec_here, m), 1, keepdims=False)
            total = total + swap("section", given, m).astype(F32)
        total = total.astype(BF).reshape(2 * quarter, len(lot) * piece)
        return [total[:, i * piece : (i + 1) * piece] for i in range(len(lot))]

    feat_grad = section_sum(blocks[:-1]) + section_sum(blocks[-1:])
    feat_grad = jnp.concatenate(xor_order(feat_grad, outer_here), axis=1)
    packed = jnp.dot(pack, feat_grad, preferred_element_type=F32).astype(BF)
    outgoing = packed.reshape(reps, 2 * capacity, outer * piece)
    incoming = lax.all_to_all(outgoing, "rep", split_axis=0, concat_axis=0, tiled=True)
    incoming = incoming.reshape(outer, 2, 2 * capacity, outer * piece)
    slot_frames = slot_frames.reshape(outer, 2, capacity)
    frame_ids = lax.broadcasted_iota(jnp.int32, (frame_rows, outer * 2 * capacity), 0)
    out_halves = []
    for p in range(2):
        order = jnp.stack([slot_frames[:, p], slot_frames[:, 1 - p]], axis=1).reshape(1, -1)
        pick = (frame_ids == order).astype(BF)
        out_halves.append(
            jnp.dot(pick, incoming[:, p].reshape(-1, outer * piece), preferred_element_type=F32)
            .astype(BF)
            .reshape(frame_rows, outer, piece)
        )
    grad_out = jnp.stack(out_halves, axis=2).reshape(frame_rows, feat)

    def weight_grad(first_col, values):
        width = values.shape[1] // 4
        lots = [values[:, q * width : (q + 1) * width] for q in range(4)]
        lots = xor_order(lots, place)
        got = {0: lots[0]}
        for m in (2, 4, 6):
            got[m] = swap(BOTH, lots[m // 2], m)
        for m in (0, 2, 4, 6):
            got[m + 1] = swap(BOTH, got[m], 1)
        cols = slice(first_col, first_col + feat // 2)
        part = lax.dot_general(near[:, cols], jnp.concatenate([got[0], got[1]]), ROWS, preferred_element_type=F32)
        part += lax.dot_general(
            straight[:, cols], jnp.concatenate([got[m] for m in (2, 4, 6)]), ROWS, preferred_element_type=F32
        )
        part += lax.dot_general(
            across[:, cols], jnp.concatenate([got[m] for m in (3, 5, 7)]), ROWS, preferred_element_type=F32
        )
        part = part.reshape(outer, 4 * part_rows, width)
        total = lax.dynamic_index_in_dim(part, outer_here, 0, keepdims=False)
        sent = part.astype(BF)
        for m in range(1, outer):
            given = lax.dynamic_index_in_dim(sent, jnp.bitwise_xor(outer_here, m), 0, keepdims=False)
            total = total + swap(BOTH, given, 8 * m).astype(F32)
        total = total.astype(BF)
        lots = xor_order([total[q * part_rows : (q + 1) * part_rows] for q in range(4)], place)
        lots = [lots[0]] + [swap(BOTH, lots[m], 2 * m) for m in (1, 2, 3)]
        return jnp.concatenate(xor_order(lots, place), axis=1).astype(F32)

    w2_grad = weight_grad(feat // 2, grad_out)

    grad_act = lax.dot_general(grad_out, w_pointwise2, COLS, preferred_element_type=F32)
    grad_conv = grad_act * slope
    padded_grad = jnp.pad(grad_conv, ((half_span, half_span), (0, 0)))
    grad_gated = jnp.zeros((frame_rows, feat), F32)
    tap_values = conv_taps.astype(F32)
    columns = []
    for k in range(taps_count):
        same_utt = padded_seg[k : k + frame_rows] == segment
        window = jnp.where(same_utt[:, None], padded_gated[k : k + frame_rows], 0.0)
        columns.append(jnp.sum(window * grad_conv, axis=0))
        back = 2 * half_span - k
        back_same = padded_seg[back : back + frame_rows] == segment
        grad_gated = grad_gated + tap_values[k] * jnp.where(
            back_same[:, None], padded_grad[back : back + frame_rows], 0.0
        )
    first = grad_gated * gate_prob
    grad_mixed = jnp.concatenate([first, first * linear * (1.0 - gate_prob)], axis=1).astype(BF)
    w1_grad = weight_grad(0, grad_mixed)
    taps_term = jnp.stack(columns, axis=0).reshape(taps_count, reps * sections, part_rows)
    taps_term = jnp.pad(taps_term.transpose(1, 0, 2), ((0, 0), (0, 16 - taps_count), (0, 0))).astype(BF)
    taps_all = lax.all_to_all(taps_term, BOTH, split_axis=0, concat_axis=0, tiled=True)
    taps_grad = jnp.sum(taps_all.astype(F32), axis=0)[:taps_count].T

    grad_norm = lax.dot_general(grad_mixed, w_pointwise1, COLS, preferred_element_type=F32)
    grad_input = inverse * (
        grad_norm
        - jnp.mean(grad_norm, axis=1, keepdims=True)
        - standard * jnp.mean(grad_norm * standard, axis=1, keepdims=True)
    )
    input_grad = (grad_out.astype(F32) + grad_input).astype(BF)
    return input_grad, w1_grad, w2_grad, taps_grad


def line_shards(
    layer_input,
    utt_frames,
    w_pointwise1,
    conv_taps,
    conv_scale,
    conv_shift,
    w_pointwise2,
    adj_grad,
    proj_weight,
    adj_target,
    adj_frame,
):
    reps = lax.axis_size("rep")
    sections = lax.axis_size("section")
    rep_here = lax.axis_index("rep")
    sec_here = lax.axis_index("section")
    block_rows = adj_grad.shape[0]
    quarter = block_rows // sections
    frame_rows, feat = layer_input.shape
    taps_count = conv_taps.shape[0]
    half_span = taps_count // 2
    capacity = max(2, 2 * quarter // reps)
    outer = reps // 2
    pair_here = rep_here % 2
    outer_here = rep_here // 2
    piece = proj_weight.shape[0]

    two = swap("rep", proj_weight, 4)
    one = swap("rep", proj_weight, 2)
    adj_other = swap("rep", adj_grad, 1)
    proj_again, two = lax.optimization_barrier((proj_weight, two))
    inner = lax.ppermute(proj_again, "rep", [(o * 2 + p, (3 - o) * 2 + p) for o in (1, 2) for p in (0, 1)])
    ends = lax.ppermute(two, "rep", [(o * 2 + p, (o ^ 1) * 2 + p) for o in (1, 2) for p in (0, 1)])

    targets = adj_target[:, 0].reshape(reps, sections, quarter)
    frames = adj_frame.reshape(reps, sections, quarter)
    sec_targets = lax.dynamic_index_in_dim(targets, sec_here, 1, keepdims=False)
    sec_frames = lax.dynamic_index_in_dim(frames, sec_here, 1, keepdims=False)
    row_a = lax.broadcasted_iota(jnp.int32, (quarter, quarter), 0)
    row_b = lax.broadcasted_iota(jnp.int32, (quarter, quarter), 1)
    same = (sec_targets[:, :, None] == sec_targets[:, None, :]) & (row_b < row_a)[None]
    rank = jnp.sum(same.astype(jnp.int32), axis=2)
    mine = sec_targets == rep_here
    slots = lax.broadcasted_iota(jnp.int32, (1, capacity, 1), 1)
    hit = mine[:, None, :] & (rank[:, None, :] == slots)
    slot_frames = jnp.sum(jnp.where(hit, sec_frames[:, None, :] + 1, 0), axis=2) - 1

    pair_blocks = jnp.stack([rep_here, jnp.bitwise_xor(rep_here, 1)])
    pair_targets = jnp.concatenate([lax.dynamic_index_in_dim(sec_targets, pair_blocks[w], 0, keepdims=False) for w in range(2)])
    pair_rank = jnp.concatenate([lax.dynamic_index_in_dim(rank, pair_blocks[w], 0, keepdims=False) for w in range(2)])
    member = lax.broadcasted_iota(jnp.int32, (2 * quarter,), 0) // quarter
    slot_of = (pair_targets * 2 + member) * capacity + pair_rank
    slot_ids = lax.broadcasted_iota(jnp.int32, (reps * 2 * capacity, 2 * quarter), 0)
    pack = (slot_of[None, :] == slot_ids).astype(BF)

    part_rows = feat // (reps * sections)

    here = rep_here * sections + sec_here
    core = here % 2
    place = (here // 2) % 4
    BOTH = ("rep", "section")

    ids = jnp.stack([sec_here, outer_here, place, core]).astype(jnp.int32)
    ids = jnp.concatenate([ids, utt_frames[0]])
    tap_values = conv_taps.astype(F32)
    square = like((frame_rows, feat), F32)
    half_t = like((feat, frame_rows), BF)
    standard, inverse, linear, gate_prob, gated, slope, masks, mine_half, their_half = local_call(
        forward_kernel,
        ids,
        (layer_input, w_pointwise1, tap_values, conv_scale.reshape(1, -1), conv_shift.reshape(1, -1)),
        [square, like((frame_rows, 128), F32), square, square, like((frame_rows, feat), BF), square]
        + [like((taps_count, frame_rows, 128), F32), half_t, half_t],
        [pltpu.VMEM((frame_rows + 16, feat), F32), pltpu.VMEM((2, feat, frame_rows), F32)],
        flops=4 * frame_rows * feat * feat,
        name="forward",
    )
    inverse = inverse[:, :1]
    early = [mine_half] + [swap(BOTH, their_half if m % 2 else mine_half, m) for m in range(1, 8)]

    rows = 2 * quarter

    def products(name, *lot):
        cols = piece * (3 if len(lot) == 3 else 1)
        sums = local_call(
            partial_kernel,
            ids,
            (adj_grad, adj_other, *lot),
            [like((rows, cols), F32)] + [like((rows, cols), BF)] * 3,
            [pltpu.VMEM((2, block_rows, cols), F32)],
            flops=4 * block_rows * adj_grad.shape[1] * cols,
            name=name,
        )
        return [sums[0]] + [swap("section", sums[m], m) for m in (1, 2, 3)]

    two, early[1:4] = lax.optimization_barrier((two, early[1:4]))
    lot_one = products("products", proj_weight, one, two)
    inner, ends, lot_one[0] = lax.optimization_barrier((inner, ends, lot_one[0]))
    lot_two = products("last_products", inner, ends)
    lot_two[0], early[4:] = lax.optimization_barrier((lot_two[0], early[4:]))
    lane = outer * piece
    (packed,) = local_call(
        packing_kernel,
        ids,
        (*lot_one, *lot_two, pack),
        [like((reps * 2 * capacity, lane), BF)],
        name="packing",
        flops=2 * pack.size * lane,
    )
    outgoing = packed.reshape(reps, 2 * capacity, lane)
    incoming = lax.all_to_all(outgoing, "rep", split_axis=0, concat_axis=0, tiled=True)
    slot_frames = slot_frames.reshape(outer, 2, capacity)
    order = jnp.stack([jnp.stack([slot_frames[:, p], slot_frames[:, 1 - p]], axis=1).reshape(-1) for p in range(2)])
    channel = lax.broadcasted_iota(jnp.int32, (feat, feat), 0)
    column = lax.broadcasted_iota(jnp.int32, (feat, feat), 1)
    group = channel // part_rows
    moved = (group % 2) * (feat // 2) + (group // 2) * part_rows + channel % part_rows
    to_halves = (moved == column).astype(BF)
    late = like((frame_rows + 32, 3 * feat // 4), BF)
    lot = like((frame_rows + 16, 3 * feat // 4), BF)
    wide = pltpu.VMEM((frame_rows + 16, feat), F32)
    grad_out, grad_mixed, p0, p2, p4, p6 = local_call(
        module_kernel,
        ids,
        (incoming, order, w_pointwise2, slope, gated, masks, gate_prob, linear, tap_values, to_halves),
        [like((frame_rows, feat), BF), like((frame_rows, 2 * feat), BF)] + [late] * 4,
        [wide, wide],
        flops=2 * frame_rows * feat * feat + 60 * frame_rows * feat,
        name="module",
    )
    got = [p0, swap(BOTH, p0, 1)]
    far = [swap(BOTH, p, m) for m, p in ((2, p2), (4, p4), (6, p6))]
    for p in far:
        got += [p, swap(BOTH, p, 1)]
    sums = local_call(
        weights_kernel,
        ids,
        (*early, *got),
        [like(lot.shape, F32)] + [lot] * 3,
        [pltpu.VMEM((feat // 2, 3 * feat // 4), F32), pltpu.VMEM((16, feat // 2), F32)],
        flops=2 * 8 * frame_rows * (feat // 2) * (3 * feat // 4),
        name="weights",
    )
    given = [swap(BOTH, sums[m], 8 * m) for m in (1, 2, 3)]
    final = (part_rows, 3 * feat // 4)
    mine_part, f1, f2, f3, tap_part = local_call(
        sum_kernel,
        ids,
        (sums[0], *given),
        [like(final, F32)] + [like(final, BF)] * 3 + [like((16, 4 * part_rows), F32)],
        [pltpu.VMEM(lot.shape, F32)],
        name="sums",
    )
    given = [swap(BOTH, f, 2 * m) for m, f in ((1, f1), (2, f2), (3, f3))]
    w1_grad, w2_grad = local_call(
        assembly_kernel,
        ids,
        (mine_part, *given),
        [like((part_rows, 2 * feat), F32), like((part_rows, feat), F32)],
        name="assembly",
    )
    taps_grad = lax.dynamic_index_in_dim(tap_part.reshape(16, 4, part_rows), place, 1, keepdims=False)[:taps_count].T

    grad_norm = lax.dot_general(grad_mixed, w_pointwise1, COLS, preferred_element_type=F32)
    grad_input = inverse * (
        grad_norm
        - jnp.mean(grad_norm, axis=1, keepdims=True)
        - standard * jnp.mean(grad_norm * standard, axis=1, keepdims=True)
    )
    input_grad = (grad_out.astype(F32) + grad_input).astype(BF)
    return input_grad, w1_grad, w2_grad, taps_grad


def shards(layer_input, *rest):
    if lax.axis_size("rep") == 8 and lax.axis_size("section") == 4:
        return line_shards(layer_input, *rest)
    return plain_shards(layer_input, *rest)


def solution(mesh):
    spread = P(("rep", "section"), None)
    return jax.shard_map(
        shards,
        mesh=mesh,
        in_specs=(spread, spread, P(), P(), P(), P(), P(), P("rep", "section"), P("rep", "section"), P(), P()),
        out_specs=(spread, spread, spread, spread),
        check_vma=False,
    )
```

time: 175 us -> 157 us (0.90); the launches traced: 174 us -> 154 us
  matrix products: 37.9 us -> 1.61 us
  Pallas kernels: 0 us -> 20.6 us
  waiting for transfers between devices: 74.2 us -> 59.1 us
  local copies, waits for them, and re-layouts: 16.5 us -> 31.1 us
  other arithmetic: 17.3 us -> 5.34 us
  starting transfers between devices: 24.3 us -> 35.4 us
  between operations: 3.9 us -> 0.93 us
    all_to_all x3 -> x1, waiting for transfers between devices: 51.2 us -> 7.2 us  [line_shards(): lax.all_to_all(outgoing, 'rep', split_axis=0, concat_axis=0, tiled=True)]
    dot_general x23 -> x1, matrix products: 37.9 us -> 1.61 us  [line_shards(): lax.dot_general(grad_mixed, w_pointwise1, COLS, preferred_element_type=F32)]
    ppermute x13 -> x31, waiting for transfers between devices: 23 us -> 51.9 us  [the longest x29 51.9 us: swap(): return lax.ppermute(values, axis, xor_perm(size_of(axis), mask))]
    unnamed x28 -> x85, local copies, waits for them, and re-layouts: 3.63 us -> 28.3 us
    pallas_call x0 -> x8, Pallas kernels: none -> 20.6 us  [local_call(): pl.pallas_call(body, out_shape=tuple(outs), in_specs=[pl.BlockSpec(memory...]
    ppermute x13 -> x31, starting transfers between devices: 12.6 us -> 31.9 us  [the longest x29 29.1 us: swap(): return lax.ppermute(values, axis, xor_perm(size_of(axis), mask))]
    all_to_all x3 -> x1, starting transfers between devices: 11.8 us -> 3.59 us  [line_shards(): lax.all_to_all(outgoing, 'rep', split_axis=0, concat_axis=0, tiled=True)]
    reduce_sum x6 -> x2, other arithmetic: 4.53 us -> 0.53 us  [the longest x1 0.32 us: line_shards(): rank = jnp.sum(same.astype(jnp.int32), axis=2)]
  transfers between devices with their start and end apart: 16 -> 32, of which waited for: 5 -> 17; matrix products, arithmetic and copies ran while one was open for 35% -> 7% of each run, Pallas kernels for 0% -> 7%
where the time goes in v2:
time: 157 us; the launch traced here: 154 us
  waiting for transfers between devices  59.1 us (38%)
  starting transfers between devices  35.4 us (23%)
  local copies, waits for them, and re-layouts  31.1 us (20%)
  Pallas kernels  20.6 us (13%)
  other arithmetic  5.34 us (3%)
  matrix products  1.61 us (1%)
    ppermute x29, waiting for transfers between devices, swap(): return lax.ppermute(values, axis, xor_perm(size_of(axis), mask))  51.9 us
    ppermute x29, starting transfers between devices, swap(): return lax.ppermute(values, axis, xor_perm(size_of(axis), mask))  29.1 us
    unnamed x85, local copies, waits for them, and re-layouts  28.3 us
    pallas_call x8, Pallas kernels, local_call(): pl.pallas_call(body, out_shape=tuple(outs), in_specs=[pl.BlockSpec(memory...  20.6 us
    all_to_all x1, waiting for transfers between devices, line_shards(): lax.all_to_all(outgoing, 'rep', split_axis=0, concat_axis=0, tiled=True)  7.2 us
    all_to_all x1, starting transfers between devices, line_shards(): lax.all_to_all(outgoing, 'rep', split_axis=0, concat_axis=0, tiled=True)  3.59 us
  transfers between devices with their start and end apart: 32, of which 17 were waited for; matrix products, arithmetic and copies ran while one was open for 7% of the time, Pallas kernels for 7%

profile of v2, /device:TPU:0, one launch (start us, length us, event | category | flops | bytes accessed | tf_op | source)
XLA Modules:
  0.0 154.1 jit_solution(2397619422318605709)
XLA Ops:
  0.7 4.1 %collective-permute-start = (bf16[128,2048]{1,0:T(8,128)(2,1)}, bf16[128,2048]{1,0:T(8,128)(2,1)}, u32[]{:S(2)}, u32[]{:S(2)}) collective-permute-start(bf16[128,2048]{1,0:T(8,128)(2,1)} %refs_2_.1), channel_id=1, source_target_pairs={{0,16},{4,20},{8,24},{12,28},{16,0},{20,4},{24,8},{28,12},{1,17},{... | collective-permute-start | bytes 1572872 | tf_op jit(solution)/shard_map/ppermute | solution.py:25
  4.8 1.6 %collective-permute-start.4 = (bf16[128,2048]{1,0:T(8,128)(2,1)}, bf16[128,2048]{1,0:T(8,128)(2,1)}, u32[]{:S(2)}, u32[]{:S(2)}) collective-permute-start(bf16[128,2048]{1,0:T(8,128)(2,1)} %refs_2_.1), channel_id=1, source_target_pairs={{0,8},{4,12},{8,0},{12,4},{16,24},{20,28},{24,16},{28,20},{1,9},{5... | collective-permute-start | bytes 1572872 | tf_op jit(solution)/shard_map/ppermute | solution.py:25
  6.3 0.8 convert_element_type.18.taps
  7.1 0.7 concatenate.25.ids
  7.8 2.2 %copy-done = bf16[1024,2048]{1,0:T(8,128)(2,1)S(1)} copy-done((bf16[1024,2048]{1,0:T(8,128)(2,1)S(1)}, bf16[1024,2048]{1,0:T(8,128)(2,1)}, u32[]{:S(2)}) %copy-start) | copy-done | bytes 4194328
  10.0 0.9 copy-done.15
  12.3 3.8 %forward.1 = (f32[128,1024]{1,0:T(8,128)S(1)}, f32[128,128]{1,0:T(8,128)S(1)}, f32[128,1024]{1,0:T(8,128)S(1)}, f32[128,1024]{1,0:T(8,128)S(1)}, bf16[128,1024]{...) custom-call(s32[8]{0:T(128)S(1)} %concatenate.25.ids, ...), custom_call_target="tpu_custom_call" | custom-call | flops 536870912 | bytes 8040448 | tf_op jit(solution)/shard_map/forward/pallas_call | solution.py:41
  16.2 0.8 copy-done.3
  17.0 0.8 copy-done.6
  17.8 0.8 copy-done.8
  18.6 0.8 copy-done.10
  19.4 0.8 copy-done.12
  21.5 1.5 collective-permute-start.6
  23.0 1.5 collective-permute-start.3
  24.6 1.6 %fusion.9.halves = bf16[1024,1024]{1,0:T(8,128)(2,1)S(1)} fusion(s32[1024]{0:T(1024)S(1)} %get-tuple-element.112, s32[1024]{0:T(1024)S(1)} %get-tuple-element.113, s32[1024]{0:T(1024)S(1)} %get-tuple-element.111, s32[1024]{0:T(1024)S(1)} %get-tuple-element.114, pred[1024]{0:T(1024)(128)(4,1)S(1)} %get-tuple-element.115, ...), kind=kLoop, calls=%fused_computation.17 | loop fusion | flops 28311552 | bytes 2115584 | tf_op jit(solution)/shard_map/convert_element_type | solution.py:584
  28.3 1.3 collective-permute-start.2
  30.3 1.5 collective-permute-start.1
  32.6 6.0 %collective-permute-done.7.e3 = bf16[1024,128]{1,0:T(8,128)(2,1)} collective-permute-done((bf16[1024,128]{1,0:T(8,128)(2,1)}, bf16[1024,128]{1,0:T(8,128)(2,1)}, u32[]{:S(2)}, u32[]{:S(2)}) %collective-permute-start.7) | collective-permute-done | bytes 262176 | tf_op jit(solution)/shard_map/ppermute | solution.py:25
  38.6 1.6 %collective-permute-start.11 = (bf16[1024,128]{1,0:T(8,128)(2,1)S(1)}, bf16[1024,128]{1,0:T(8,128)(2,1)S(1)}, u32[]{:S(2)}, u32[]{:S(2)}) collective-permute-start(bf16[1024,128]{1,0:T(8,128)(2,1)S(1)} %get-tuple-element.55.e0), channel_id=1, source_target_pairs={{0,4},{1,5},{2,6},{3,7},{4,0},{5,1},{6,2},{7,3},{8,12},{9,13},{10,... | collective-permute-start | bytes 786440 | tf_op jit(solution)/shard_map/ppermute | solution.py:25
  40.2 8.9 %collective-permute-done.3.refs_1_ = bf16[256,2048]{1,0:T(8,128)(2,1)} collective-permute-done((bf16[256,2048]{1,0:T(8,128)(2,1)S(1)}, bf16[256,2048]{1,0:T(8,128)(2,1)}, u32[]{:S(2)}, u32[]{:S(2)}) %collective-permute-start.3) | collective-permute-done | bytes 1048608 | tf_op jit(solution)/shard_map/ppermute | solution.py:25
  49.1 1.5 collective-permute-start.13
  51.4 1.0 copy-done.14
  52.4 3.5 %products.1 = (f32[128,384]{1,0:T(8,128)S(1)}, bf16[128,384]{1,0:T(8,128)(2,1)}, bf16[128,384]{1,0:T(8,128)(2,1)}, bf16[128,384]{1,0:T(8,128)(2,1)}) custom-call(s32[8]{0:T(128)S(1)} %concatenate.25.ids, bf16[256,2048]{1,0:T(8,128)(2,1)S(1)} %copy-done.2, bf16[256,2048]{1,0:T(8,128)(2,1)} %collective-permute-done.3.refs_1_, ...), custom_call_target="tpu_custom_call" | custom-call | flops 805306368 | bytes 4161536 | tf_op jit(solution)/shard_map/products/pallas_call | solution.py:41
  55.9 2.9 %last_products.1 = (f32[128,128]{1,0:T(8,128)S(1)}, bf16[128,128]{1,0:T(8,128)(2,1)S(1)}, bf16[128,128]{1,0:T(8,128)(2,1)}, bf16[128,128]{1,0:T(8,128)(2,1)}) custom-call(s32[8]{0:T(128)S(1)} %concatenate.25.ids, bf16[256,2048]{1,0:T(8,128)(2,1)S(1)} %copy-done.2, bf16[256,2048]{1,0:T(8,128)(2,1)} %collective-permute-done.3.refs_1_, ...), custom_call_target="tpu_custom_call" | custom-call | flops 268435456 | bytes 3309568 | tf_op jit(solution)/shard_map/last_products/pallas_call | solution.py:41
  59.5 1.6 %collective-permute-start.15 = (bf16[128,128]{1,0:T(8,128)(2,1)S(1)}, bf16[128,128]{1,0:T(8,128)(2,1)S(1)}, u32[]{:S(2)}, u32[]{:S(2)}) collective-permute-start(bf16[128,128]{1,0:T(8,128)(2,1)S(1)} %get-tuple-element.66), channel_id=1, source_target_pairs={{0,1},{1,0},{2,3},{3,2},{4,5},{5,4},{6,7},{7,6},{8,9},{9,8},{10,11... | collective-permute-start | bytes 98312 | tf_op jit(solution)/shard_map/ppermute | solution.py:25
  61.3 4.6 %collective-permute-done.11.e4 = bf16[1024,128]{1,0:T(8,128)(2,1)S(1)} collective-permute-done((bf16[1024,128]{1,0:T(8,128)(2,1)S(1)}, bf16[1024,128]{1,0:T(8,128)(2,1)S(1)}, u32[]{:S(2)}, u32[]{:S(2)}) %collective-permute-start.11) | collective-permute-done | bytes 262176 | tf_op jit(solution)/shard_map/ppermute | solution.py:25
  67.1 3.0 %collective-permute-done.12.e5 = bf16[1024,128]{1,0:T(8,128)(2,1)S(1)} collective-permute-done((bf16[1024,128]{1,0:T(8,128)(2,1)}, bf16[1024,128]{1,0:T(8,128)(2,1)S(1)}, u32[]{:S(2)}, u32[]{:S(2)}) %collective-permute-start.12) | collective-permute-done | bytes 262176 | tf_op jit(solution)/shard_map/ppermute | solution.py:25
  70.8 0.9 collective-permute-start.17
  72.3 0.9 collective-permute-start.10
  73.9 0.7 collective-permute-start.8
  77.6 2.6 %collective-permute-done.9.r2 = bf16[128,384]{1,0:T(8,128)(2,1)S(1)} collective-permute-done((bf16[128,384]{1,0:T(8,128)(2,1)}, bf16[128,384]{1,0:T(8,128)(2,1)S(1)}, u32[]{:S(2)}, u32[]{:S(2)}) %collective-permute-start.9) | collective-permute-done | bytes 98336 | tf_op jit(solution)/shard_map/ppermute | solution.py:25
  80.2 0.9 copy-done.27
  81.1 0.8 copy-done.29
  82.0 0.8 copy-done.32
  82.7 0.8 copy-done.34
  83.5 0.8 copy-done.36
  84.2 1.5 packing.1
  85.7 3.6 %all-to-all-start = ((bf16[8,32,512]{2,1,0:T(8,128)(2,1)}), bf16[8,32,512]{2,1,0:T(8,128)(2,1)S(1)}, u32[]{:S(2)}, u32[]{:S(2)}) async-start(bf16[8,32,512]{2,1,0:T(8,128)(2,1)} %bitcast.12), calls=%async_computation | async-start | bytes 524288 | tf_op jit(solution)/shard_map/all_to_all | solution.py:577
  89.5 0.9 slice_reduce_fusion
  90.4 7.2 %all-to-all-done.incoming = bf16[8,32,512]{2,1,0:T(8,128)(2,1)S(1)} async-done(((bf16[8,32,512]{2,1,0:T(8,128)(2,1)}), bf16[8,32,512]{2,1,0:T(8,128)(2,1)S(1)}, u32[]{:S(2)}, u32[]{:S(2)}) %all-to-all-start) | async-done | bytes 262176 | tf_op jit(solution)/shard_map/all_to_all | solution.py:577
  97.6 1.7 %copy-done.5 = bf16[1024,1024]{1,0:T(8,128)(2,1)S(1)} copy-done((bf16[1024,1024]{1,0:T(8,128)(2,1)S(1)}, bf16[1024,1024]{1,0:T(8,128)(2,1)}, u32[]{:S(2)}) %copy-start.5) | copy-done | bytes 2097176
  99.4 1.2 copy-done.7
  100.6 1.0 copy-done.9
  101.6 1.0 copy-done.11
  102.7 1.0 copy-done.13
  103.7 0.9 copy-done.17
  104.7 4.6 %module.1 = (bf16[128,1024]{1,0:T(8,128)(2,1)S(1)}, bf16[128,2048]{1,0:T(8,128)(2,1)S(1)}, bf16[160,768]{1,0:T(8,128)(2,1)S(1)}, bf16[160,768]{1,0:T(8,128)(2,1)...) custom-call(s32[8]{0:T(128)S(1)} %concatenate.25.ids, bf16[8,32,512]{2,1,0:T(8,128)(2,1)S(1)} %all-to-all-done.incoming, ...), custom_call_target="tpu_custom_call" | custom-call | flops 276299776 | bytes 8688640 | tf_op jit(solution)/shard_map/module/pallas_call | solution.py:41
  109.3 1.5 collective-permute-start.19
  110.8 1.4 collective-permute-start.21
  112.9 1.6 %fusion.25 = (f32[128]{0:T(128)S(1)}, f32[128]{0:T(128)S(1)}, f32[128,1024]{1,0:T(8,128)S(1)}) fusion(f32[128,1024]{1,0:T(8,128)S(1)} %copy-done.4, bf16[128,2048]{1,0:T(8,128)(2,1)S(1)} %get-tuple-element.76, bf16[1024,2048]{1,0:T(8,128)(2,1)S(1)} %copy-done.1), kind=kOutput, calls=%fused_computation.65 | convolution fusion | flops 537263872 | bytes 5768192 | tf_op jit(solution)/shard_map/dot_general | solution.py:630
  114.5 3.2 %collective-permute-done.19.g2 = bf16[160,768]{1,0:T(8,128)(2,1)S(1)} collective-permute-done((bf16[160,768]{1,0:T(8,128)(2,1)S(1)}, bf16[160,768]{1,0:T(8,128)(2,1)S(1)}, u32[]{:S(2)}, u32[]{:S(2)}) %collective-permute-start.19) | collective-permute-done | bytes 245792 | tf_op jit(solution)/shard_map/ppermute | solution.py:25
  117.7 4.0 %collective-permute-done.21.g4 = bf16[160,768]{1,0:T(8,128)(2,1)S(1)} collective-permute-done((bf16[160,768]{1,0:T(8,128)(2,1)S(1)}, bf16[160,768]{1,0:T(8,128)(2,1)S(1)}, u32[]{:S(2)}, u32[]{:S(2)}) %collective-permute-start.21) | collective-permute-done | bytes 245792 | tf_op jit(solution)/shard_map/ppermute | solution.py:25
  122.2 1.0 collective-permute-done.22.g5
  123.5 2.2 %weights.1 = (f32[144,768]{1,0:T(8,128)S(1)}, bf16[144,768]{1,0:T(8,128)(2,1)S(1)}, bf16[144,768]{1,0:T(8,128)(2,1)S(1)}, bf16[144,768]{1,0:T(8,128)(2,1)S(1)}) custom-call(s32[8]{0:T(128)S(1)} %concatenate.25.ids, bf16[1024,128]{1,0:T(8,128)(2,1)S(1)} %get-tuple-element.55.e0, bf16[1024,128]{1,0:T(8,128)(2,1)} %collective-permute-done.5.e1, ...), custom_call_target="tpu_custom_call" | custom-call | flops 805306368 | bytes 5169152 | tf_op jit(solution)/shard_map/weights/pallas_call | solution.py:41
  126.5 2.6 %collective-permute-start.26 = (bf16[144,768]{1,0:T(8,128)(2,1)S(1)}, bf16[144,768]{1,0:T(8,128)(2,1)S(1)}, u32[]{:S(2)}, u32[]{:S(2)}) collective-permute-start(bf16[144,768]{1,0:T(8,128)(2,1)S(1)} %get-tuple-element.91), channel_id=1, source_target_pairs={{0,16},{1,17},{2,18},{3,19},{4,20},{5,21},{6,22},{7,23},{8,24},{9,... | collective-permute-start | bytes 663560 | tf_op jit(solution)/shard_map/ppermute | solution.py:25
  129.1 1.1 collective-permute-start.27
  130.2 0.9 add_convert_fusion
  131.1 6.7 %collective-permute-done.25.r1 = bf16[144,768]{1,0:T(8,128)(2,1)S(1)} collective-permute-done((bf16[144,768]{1,0:T(8,128)(2,1)S(1)}, bf16[144,768]{1,0:T(8,128)(2,1)S(1)}, u32[]{:S(2)}, u32[]{:S(2)}) %collective-permute-start.25) | collective-permute-done | bytes 221216 | tf_op jit(solution)/shard_map/ppermute | solution.py:25
  137.8 7.4 %collective-permute-done.26.r2 = bf16[144,768]{1,0:T(8,128)(2,1)S(1)} collective-permute-done((bf16[144,768]{1,0:T(8,128)(2,1)S(1)}, bf16[144,768]{1,0:T(8,128)(2,1)S(1)}, u32[]{:S(2)}, u32[]{:S(2)}) %collective-permute-start.26) | collective-permute-done | bytes 221216 | tf_op jit(solution)/shard_map/ppermute | solution.py:25
  145.9 1.3 collective-permute-start.28
  147.8 1.7 %collective-permute-start.30 = (bf16[32,768]{1,0:T(8,128)(2,1)S(1)}, bf16[32,768]{1,0:T(8,128)(2,1)S(1)}, u32[]{:S(2)}, u32[]{:S(2)}) collective-permute-start(bf16[32,768]{1,0:T(8,128)(2,1)S(1)} %get-tuple-element.96), channel_id=1, source_target_pairs={{0,6},{1,7},{2,4},{3,5},{4,2},{5,3},{6,0},{7,1},{8,14},{9,15},{10,... | collective-permute-start | bytes 147464 | tf_op jit(solution)/shard_map/ppermute | solution.py:25
  150.2 1.1 collective-permute-done.29.r2
  151.3 1.5 collective-permute-done.30.r3
  152.8 1.3 assembly.1
  (124 shorter events, 18.6 us)
Async XLA Ops:
  0.6 26.0 %copy-start.40 = (s32[2048,1]{0,1:T(1,128)S(1)}, s32[2048,1]{0,1:T(1,128)}, u32[]{:S(2)}) copy-start(s32[2048,1]{0,1:T(1,128)} %param.20) | copy-start | bytes 24580
  0.6 31.3 %copy-start.39 = (s32[2048]{0:T(1024)S(1)}, s32[2048]{0:T(1024)}, u32[]{:S(2)}) copy-start(s32[2048]{0:T(1024)} %param.21) | copy-start | bytes 24580
  0.7 27.7 %collective-permute-start = (bf16[128,2048]{1,0:T(8,128)(2,1)}, bf16[128,2048]{1,0:T(8,128)(2,1)}, u32[]{:S(2)}, u32[]{:S(2)}) collective-permute-start(bf16[128,2048]{1,0:T(8,128)(2,1)} %refs_2_.1), channel_id=1, source_target_pairs={{0,16},{4,20},{8,24},{12,28},{16,0},{20,4},{24,8},{28,12},{1,17},{... | collective-permute-start | bytes 1572872 | tf_op jit(solution)/shard_map/ppermute | solution.py:25
  4.8 35.4 %collective-permute-start.4 = (bf16[128,2048]{1,0:T(8,128)(2,1)}, bf16[128,2048]{1,0:T(8,128)(2,1)}, u32[]{:S(2)}, u32[]{:S(2)}) collective-permute-start(bf16[128,2048]{1,0:T(8,128)(2,1)} %refs_2_.1), channel_id=1, source_target_pairs={{0,8},{4,12},{8,0},{12,4},{16,24},{20,28},{24,16},{28,20},{1,9},{5... | collective-permute-start | bytes 1572872 | tf_op jit(solution)/shard_map/ppermute | solution.py:25
  7.8 2.2 %copy-start = (bf16[1024,2048]{1,0:T(8,128)(2,1)S(1)}, bf16[1024,2048]{1,0:T(8,128)(2,1)}, u32[]{:S(2)}) copy-start(bf16[1024,2048]{1,0:T(8,128)(2,1)} %w_one.1) | copy-start | bytes 12582916
  10.0 0.9 copy-start.15
  12.3 10.7 %copy-start.2 = (bf16[256,2048]{1,0:T(8,128)(2,1)S(1)}, bf16[256,2048]{1,0:T(8,128)(2,1)}, u32[]{:S(2)}) copy-start(bf16[256,2048]{1,0:T(8,128)(2,1)} %refs_0_.3) | copy-start | bytes 3145732
  16.2 0.8 copy-start.3
  17.0 0.8 copy-start.6
  17.8 0.8 copy-start.8
  18.6 0.8 copy-start.10
  19.4 0.8 copy-start.12
  20.2 0.7 copy-start.16
  21.5 8.2 %collective-permute-start.5 = (bf16[1024,128]{1,0:T(8,128)(2,1)}, bf16[1024,128]{1,0:T(8,128)(2,1)}, u32[]{:S(2)}, u32[]{:S(2)}) collective-permute-start(bf16[1024,128]{1,0:T(8,128)(2,1)} %get-tuple-element.54), channel_id=1, source_target_pairs={{0,1},{1,0},{2,3},{3,2},{4,5},{5,4},{6,7},{7,6},{8,9},{9,8},{10,11... | collective-permute-start | bytes 786440 | tf_op jit(solution)/shard_map/ppermute | solution.py:25
  21.5 8.8 %collective-permute-start.6 = (bf16[1024,128]{1,0:T(8,128)(2,1)S(1)}, bf16[1024,128]{1,0:T(8,128)(2,1)}, u32[]{:S(2)}, u32[]{:S(2)}) collective-permute-start(bf16[1024,128]{1,0:T(8,128)(2,1)S(1)} %get-tuple-element.55.e0), channel_id=1, source_target_pairs={{0,2},{1,3},{2,0},{3,1},{4,6},{5,7},{6,4},{7,5},{8,10},{9,11},{10,... | collective-permute-start | bytes 786440 | tf_op jit(solution)/shard_map/ppermute | solution.py:25
  23.0 26.1 %collective-permute-start.3 = (bf16[256,2048]{1,0:T(8,128)(2,1)S(1)}, bf16[256,2048]{1,0:T(8,128)(2,1)}, u32[]{:S(2)}, u32[]{:S(2)}) collective-permute-start(bf16[256,2048]{1,0:T(8,128)(2,1)S(1)} %copy-done.2), channel_id=1, source_target_pairs={{0,4},{4,0},{8,12},{12,8},{16,20},{20,16},{24,28},{28,24},{1,5},{5... | collective-permute-start | bytes 3145736 | tf_op jit(solution)/shard_map/ppermute | solution.py:25
  28.3 22.3 %collective-permute-start.2 = (bf16[128,2048]{1,0:T(8,128)(2,1)}, bf16[128,2048]{1,0:T(8,128)(2,1)}, u32[]{:S(2)}, u32[]{:S(2)}) collective-permute-start(bf16[128,2048]{1,0:T(8,128)(2,1)} %collective-permute-done.refs_4_), channel_id=1, source_target_pairs={{8,0},{12,4},{16,24},{20,28},{9,1},{13,5},{17,25},{21,29},{10,2},{... | collective-permute-start | bytes 1572872 | tf_op jit(solution)/shard_map/ppermute | solution.py:499
  29.7 8.9 %collective-permute-start.7 = (bf16[1024,128]{1,0:T(8,128)(2,1)}, bf16[1024,128]{1,0:T(8,128)(2,1)}, u32[]{:S(2)}, u32[]{:S(2)}) collective-permute-start(bf16[1024,128]{1,0:T(8,128)(2,1)} %get-tuple-element.54), channel_id=1, source_target_pairs={{0,3},{1,2},{2,1},{3,0},{4,7},{5,6},{6,5},{7,4},{8,11},{9,10},{10,... | collective-permute-start | bytes 786440 | tf_op jit(solution)/shard_map/ppermute | solution.py:25
  30.3 25.6 %collective-permute-start.1 = (bf16[128,2048]{1,0:T(8,128)(2,1)}, bf16[128,2048]{1,0:T(8,128)(2,1)}, u32[]{:S(2)}, u32[]{:S(2)}) collective-permute-start(bf16[128,2048]{1,0:T(8,128)(2,1)} %refs_2_.1), channel_id=1, source_target_pairs={{8,16},{12,20},{16,8},{20,12},{9,17},{13,21},{17,9},{21,13},{10,18... | collective-permute-start | bytes 1572872 | tf_op jit(solution)/shard_map/ppermute | solution.py:498
  38.6 27.3 %collective-permute-start.11 = (bf16[1024,128]{1,0:T(8,128)(2,1)S(1)}, bf16[1024,128]{1,0:T(8,128)(2,1)S(1)}, u32[]{:S(2)}, u32[]{:S(2)}) collective-permute-start(bf16[1024,128]{1,0:T(8,128)(2,1)S(1)} %get-tuple-element.55.e0), channel_id=1, source_target_pairs={{0,4},{1,5},{2,6},{3,7},{4,0},{5,1},{6,2},{7,3},{8,12},{9,13},{10,... | collective-permute-start | bytes 786440 | tf_op jit(solution)/shard_map/ppermute | solution.py:25
  40.2 29.9 %collective-permute-start.12 = (bf16[1024,128]{1,0:T(8,128)(2,1)}, bf16[1024,128]{1,0:T(8,128)(2,1)S(1)}, u32[]{:S(2)}, u32[]{:S(2)}) collective-permute-start(bf16[1024,128]{1,0:T(8,128)(2,1)} %get-tuple-element.54), channel_id=1, source_target_pairs={{0,5},{1,4},{2,7},{3,6},{4,1},{5,0},{6,3},{7,2},{8,13},{9,12},{10,... | collective-permute-start | bytes 786440 | tf_op jit(solution)/shard_map/ppermute | solution.py:25
  49.1 22.5 %collective-permute-start.13 = (bf16[1024,128]{1,0:T(8,128)(2,1)S(1)}, bf16[1024,128]{1,0:T(8,128)(2,1)S(1)}, u32[]{:S(2)}, u32[]{:S(2)}) collective-permute-start(bf16[1024,128]{1,0:T(8,128)(2,1)S(1)} %get-tuple-element.55.e0), channel_id=1, source_target_pairs={{0,6},{1,7},{2,4},{3,5},{4,2},{5,3},{6,0},{7,1},{8,14},{9,15},{10,... | collective-permute-start | bytes 786440 | tf_op jit(solution)/shard_map/ppermute | solution.py:25
  50.6 22.6 %collective-permute-start.14 = (bf16[1024,128]{1,0:T(8,128)(2,1)}, bf16[1024,128]{1,0:T(8,128)(2,1)S(1)}, u32[]{:S(2)}, u32[]{:S(2)}) collective-permute-start(bf16[1024,128]{1,0:T(8,128)(2,1)} %get-tuple-element.54), channel_id=1, source_target_pairs={{0,7},{1,6},{2,5},{3,4},{4,3},{5,2},{6,1},{7,0},{8,15},{9,14},{10,... | collective-permute-start | bytes 786440 | tf_op jit(solution)/shard_map/ppermute | solution.py:25
  51.3 1.0 copy-start.14
  55.9 17.3 %copy-start.26 = (f32[128,384]{1,0:T(8,128)}, f32[128,384]{1,0:T(8,128)S(1)}, u32[]{:S(2)}) copy-start(f32[128,384]{1,0:T(8,128)S(1)} %get-tuple-element.58.own) | copy-start | bytes 589828
  59.5 15.2 %collective-permute-start.15 = (bf16[128,128]{1,0:T(8,128)(2,1)S(1)}, bf16[128,128]{1,0:T(8,128)(2,1)S(1)}, u32[]{:S(2)}, u32[]{:S(2)}) collective-permute-start(bf16[128,128]{1,0:T(8,128)(2,1)S(1)} %get-tuple-element.66), channel_id=1, source_target_pairs={{0,1},{1,0},{2,3},{3,2},{4,5},{5,4},{6,7},{7,6},{8,9},{9,8},{10,11... | collective-permute-start | bytes 98312 | tf_op jit(solution)/shard_map/ppermute | solution.py:25
  65.9 0.7 copy-start.18
  66.6 9.3 %collective-permute-start.16 = (bf16[128,128]{1,0:T(8,128)(2,1)}, bf16[128,128]{1,0:T(8,128)(2,1)S(1)}, u32[]{:S(2)}, u32[]{:S(2)}) collective-permute-start(bf16[128,128]{1,0:T(8,128)(2,1)} %get-tuple-element.67), channel_id=1, source_target_pairs={{0,2},{1,3},{2,0},{3,1},{4,6},{5,7},{6,4},{7,5},{8,10},{9,11},{10,... | collective-permute-start | bytes 98312 | tf_op jit(solution)/shard_map/ppermute | solution.py:25
  70.8 5.7 %collective-permute-start.17 = (bf16[128,128]{1,0:T(8,128)(2,1)}, bf16[128,128]{1,0:T(8,128)(2,1)S(1)}, u32[]{:S(2)}, u32[]{:S(2)}) collective-permute-start(bf16[128,128]{1,0:T(8,128)(2,1)} %get-tuple-element.68), channel_id=1, source_target_pairs={{0,3},{1,2},{2,1},{3,0},{4,7},{5,6},{6,5},{7,4},{8,11},{9,10},{10,... | collective-permute-start | bytes 98312 | tf_op jit(solution)/shard_map/ppermute | solution.py:25
  72.3 5.3 %collective-permute-start.10 = (bf16[128,384]{1,0:T(8,128)(2,1)}, bf16[128,384]{1,0:T(8,128)(2,1)S(1)}, u32[]{:S(2)}, u32[]{:S(2)}) collective-permute-start(bf16[128,384]{1,0:T(8,128)(2,1)} %get-tuple-element.61), channel_id=1, source_target_pairs={{0,3},{1,2},{2,1},{3,0},{4,7},{5,6},{6,5},{7,4},{8,11},{9,10},{10,... | collective-permute-start | bytes 294920 | tf_op jit(solution)/shard_map/ppermute | solution.py:25
  73.2 0.7 copy-start.24
  73.9 3.7 %collective-permute-start.8 = (bf16[128,384]{1,0:T(8,128)(2,1)}, bf16[128,384]{1,0:T(8,128)(2,1)S(1)}, u32[]{:S(2)}, u32[]{:S(2)}) collective-permute-start(bf16[128,384]{1,0:T(8,128)(2,1)} %get-tuple-element.59), channel_id=1, source_target_pairs={{0,1},{1,0},{2,3},{3,2},{4,5},{5,4},{6,7},{7,6},{8,9},{9,8},{10,11... | collective-permute-start | bytes 294920 | tf_op jit(solution)/shard_map/ppermute | solution.py:25
  75.3 4.9 %collective-permute-start.9 = (bf16[128,384]{1,0:T(8,128)(2,1)}, bf16[128,384]{1,0:T(8,128)(2,1)S(1)}, u32[]{:S(2)}, u32[]{:S(2)}) collective-permute-start(bf16[128,384]{1,0:T(8,128)(2,1)} %get-tuple-element.60), channel_id=1, source_target_pairs={{0,2},{1,3},{2,0},{3,1},{4,6},{5,7},{6,4},{7,5},{8,10},{9,11},{10,... | collective-permute-start | bytes 294920 | tf_op jit(solution)/shard_map/ppermute | solution.py:25
  75.9 37.0 %copy-start.4 = (f32[128,1024]{1,0:T(8,128)S(1)}, f32[128,1024]{1,0:T(8,128)}, u32[]{:S(2)}) copy-start(f32[128,1024]{1,0:T(8,128)} %copy-done.3) | copy-start | bytes 1572868
  80.2 0.9 copy-start.27
  81.1 0.8 copy-start.29
  81.9 0.8 copy-start.32
  82.7 0.8 copy-start.34
  83.5 0.8 copy-start.36
  85.7 11.9 %all-to-all-start = ((bf16[8,32,512]{2,1,0:T(8,128)(2,1)}), bf16[8,32,512]{2,1,0:T(8,128)(2,1)S(1)}, u32[]{:S(2)}, u32[]{:S(2)}) async-start(bf16[8,32,512]{2,1,0:T(8,128)(2,1)} %bitcast.12), calls=%async_computation | async-start | bytes 524288 | tf_op jit(solution)/shard_map/all_to_all | solution.py:577
  97.6 15.2 %copy-start.1 = (bf16[1024,2048]{1,0:T(8,128)(2,1)S(1)}, bf16[1024,2048]{1,0:T(8,128)(2,1)}, u32[]{:S(2)}) copy-start(bf16[1024,2048]{1,0:T(8,128)(2,1)} %w_one.1) | copy-start | bytes 12582916
  97.6 1.7 %copy-start.5 = (bf16[1024,1024]{1,0:T(8,128)(2,1)S(1)}, bf16[1024,1024]{1,0:T(8,128)(2,1)}, u32[]{:S(2)}) copy-start(bf16[1024,1024]{1,0:T(8,128)(2,1)} %w_two.1) | copy-start | bytes 6291460
  99.4 1.2 copy-start.7
  100.6 1.0 copy-start.9
  101.6 1.0 copy-start.11
  102.7 1.0 copy-start.13
  103.7 0.9 copy-start.17
  109.3 14.3 %copy-start.19 = (bf16[1024,128]{1,0:T(8,128)(2,1)S(1)}, bf16[1024,128]{1,0:T(8,128)(2,1)}, u32[]{:S(2)}) copy-start(bf16[1024,128]{1,0:T(8,128)(2,1)} %copy-done.18) | copy-start | bytes 786436
  109.3 14.3 %copy-start.21 = (bf16[1024,128]{1,0:T(8,128)(2,1)S(1)}, bf16[1024,128]{1,0:T(8,128)(2,1)}, u32[]{:S(2)}) copy-start(bf16[1024,128]{1,0:T(8,128)(2,1)} %copy-done.20) | copy-start | bytes 786436
  109.3 14.2 %copy-start.23 = (bf16[1024,128]{1,0:T(8,128)(2,1)S(1)}, bf16[1024,128]{1,0:T(8,128)(2,1)}, u32[]{:S(2)}) copy-start(bf16[1024,128]{1,0:T(8,128)(2,1)} %copy-done.22) | copy-start | bytes 786436
  109.3 14.2 %copy-start.25 = (bf16[1024,128]{1,0:T(8,128)(2,1)S(1)}, bf16[1024,128]{1,0:T(8,128)(2,1)}, u32[]{:S(2)}) copy-start(bf16[1024,128]{1,0:T(8,128)(2,1)} %copy-done.24) | copy-start | bytes 786436
  109.3 8.4 %collective-permute-start.19 = (bf16[160,768]{1,0:T(8,128)(2,1)S(1)}, bf16[160,768]{1,0:T(8,128)(2,1)S(1)}, u32[]{:S(2)}, u32[]{:S(2)}) collective-permute-start(bf16[160,768]{1,0:T(8,128)(2,1)S(1)} %get-tuple-element.86), channel_id=1, source_target_pairs={{0,2},{1,3},{2,0},{3,1},{4,6},{5,7},{6,4},{7,5},{8,10},{9,11},{10,... | collective-permute-start | bytes 737288 | tf_op jit(solution)/shard_map/ppermute | solution.py:25
  110.8 10.9 %collective-permute-start.21 = (bf16[160,768]{1,0:T(8,128)(2,1)S(1)}, bf16[160,768]{1,0:T(8,128)(2,1)S(1)}, u32[]{:S(2)}, u32[]{:S(2)}) collective-permute-start(bf16[160,768]{1,0:T(8,128)(2,1)S(1)} %get-tuple-element.87), channel_id=1, source_target_pairs={{0,4},{1,5},{2,6},{3,7},{4,0},{5,1},{6,2},{7,3},{8,12},{9,13},{10,... | collective-permute-start | bytes 737288 | tf_op jit(solution)/shard_map/ppermute | solution.py:25
  112.2 9.5 %collective-permute-start.23 = (bf16[160,768]{1,0:T(8,128)(2,1)S(1)}, bf16[160,768]{1,0:T(8,128)(2,1)S(1)}, u32[]{:S(2)}, u32[]{:S(2)}) collective-permute-start(bf16[160,768]{1,0:T(8,128)(2,1)S(1)} %get-tuple-element.88), channel_id=1, source_target_pairs={{0,6},{1,7},{2,4},{3,5},{4,2},{5,3},{6,0},{7,1},{8,14},{9,15},{10,... | collective-permute-start | bytes 737288 | tf_op jit(solution)/shard_map/ppermute | solution.py:25
  112.8 9.3 %collective-permute-start.18 = (bf16[160,768]{1,0:T(8,128)(2,1)S(1)}, bf16[160,768]{1,0:T(8,128)(2,1)S(1)}, u32[]{:S(2)}, u32[]{:S(2)}) collective-permute-start(bf16[160,768]{1,0:T(8,128)(2,1)S(1)} %get-tuple-element.85.g0), channel_id=1, source_target_pairs={{0,1},{1,0},{2,3},{3,2},{4,5},{5,4},{6,7},{7,6},{8,9},{9,8},{10,11... | collective-permute-start | bytes 737288 | tf_op jit(solution)/shard_map/ppermute | solution.py:25
  117.7 4.5 %collective-permute-start.20 = (bf16[160,768]{1,0:T(8,128)(2,1)S(1)}, bf16[160,768]{1,0:T(8,128)(2,1)S(1)}, u32[]{:S(2)}, u32[]{:S(2)}) collective-permute-start(bf16[160,768]{1,0:T(8,128)(2,1)S(1)} %collective-permute-done.19.g2), channel_id=1, source_target_pairs={{0,1},{1,0},{2,3},{3,2},{4,5},{5,4},{6,7},{7,6},{8,9},{9,8},{10,11... | collective-permute-start | bytes 737288 | tf_op jit(solution)/shard_map/ppermute | solution.py:25
  121.6 1.5 collective-permute-start.22
  121.7 1.9 %collective-permute-start.24 = (bf16[160,768]{1,0:T(8,128)(2,1)S(1)}, bf16[160,768]{1,0:T(8,128)(2,1)S(1)}, u32[]{:S(2)}, u32[]{:S(2)}) collective-permute-start(bf16[160,768]{1,0:T(8,128)(2,1)S(1)} %collective-permute-done.23.g6), channel_id=1, source_target_pairs={{0,1},{1,0},{2,3},{3,2},{4,5},{5,4},{6,7},{7,6},{8,9},{9,8},{10,11... | collective-permute-start | bytes 737288 | tf_op jit(solution)/shard_map/ppermute | solution.py:25
  125.8 12.0 %collective-permute-start.25 = (bf16[144,768]{1,0:T(8,128)(2,1)S(1)}, bf16[144,768]{1,0:T(8,128)(2,1)S(1)}, u32[]{:S(2)}, u32[]{:S(2)}) collective-permute-start(bf16[144,768]{1,0:T(8,128)(2,1)S(1)} %get-tuple-element.90), channel_id=1, source_target_pairs={{0,8},{1,9},{2,10},{3,11},{4,12},{5,13},{6,14},{7,15},{8,0},{9,1},... | collective-permute-start | bytes 663560 | tf_op jit(solution)/shard_map/ppermute | solution.py:25
  126.5 18.7 %collective-permute-start.26 = (bf16[144,768]{1,0:T(8,128)(2,1)S(1)}, bf16[144,768]{1,0:T(8,128)(2,1)S(1)}, u32[]{:S(2)}, u32[]{:S(2)}) collective-permute-start(bf16[144,768]{1,0:T(8,128)(2,1)S(1)} %get-tuple-element.91), channel_id=1, source_target_pairs={{0,16},{1,17},{2,18},{3,19},{4,20},{5,21},{6,22},{7,23},{8,24},{9,... | collective-permute-start | bytes 663560 | tf_op jit(solution)/shard_map/ppermute | solution.py:25
  129.1 16.1 %collective-permute-start.27 = (bf16[144,768]{1,0:T(8,128)(2,1)S(1)}, bf16[144,768]{1,0:T(8,128)(2,1)S(1)}, u32[]{:S(2)}, u32[]{:S(2)}) collective-permute-start(bf16[144,768]{1,0:T(8,128)(2,1)S(1)} %get-tuple-element.92), channel_id=1, source_target_pairs={{0,24},{1,25},{2,26},{3,27},{4,28},{5,29},{6,30},{7,31},{8,16},{9,... | collective-permute-start | bytes 663560 | tf_op jit(solution)/shard_map/ppermute | solution.py:25
  145.9 4.3 %collective-permute-start.28 = (bf16[32,768]{1,0:T(8,128)(2,1)S(1)}, bf16[32,768]{1,0:T(8,128)(2,1)S(1)}, u32[]{:S(2)}, u32[]{:S(2)}) collective-permute-start(bf16[32,768]{1,0:T(8,128)(2,1)S(1)} %get-tuple-element.94), channel_id=1, source_target_pairs={{0,2},{1,3},{2,0},{3,1},{4,6},{5,7},{6,4},{7,5},{8,10},{9,11},{10,... | collective-permute-start | bytes 147464 | tf_op jit(solution)/shard_map/ppermute | solution.py:25
  147.2 4.1 %collective-permute-start.29 = (bf16[32,768]{1,0:T(8,128)(2,1)S(1)}, bf16[32,768]{1,0:T(8,128)(2,1)S(1)}, u32[]{:S(2)}, u32[]{:S(2)}) collective-permute-start(bf16[32,768]{1,0:T(8,128)(2,1)S(1)} %get-tuple-element.95), channel_id=1, source_target_pairs={{0,4},{1,5},{2,6},{3,7},{4,0},{5,1},{6,2},{7,3},{8,12},{9,13},{10,... | collective-permute-start | bytes 147464 | tf_op jit(solution)/shard_map/ppermute | solution.py:25
  147.8 5.0 %collective-permute-start.30 = (bf16[32,768]{1,0:T(8,128)(2,1)S(1)}, bf16[32,768]{1,0:T(8,128)(2,1)S(1)}, u32[]{:S(2)}, u32[]{:S(2)}) collective-permute-start(bf16[32,768]{1,0:T(8,128)(2,1)S(1)} %get-tuple-element.96), channel_id=1, source_target_pairs={{0,6},{1,7},{2,4},{3,5},{4,2},{5,3},{6,0},{7,1},{8,14},{9,15},{10,... | collective-permute-start | bytes 147464 | tf_op jit(solution)/shard_map/ppermute | solution.py:25
  (9 other events, 5.8 us)

commit v3 on v2

--- a/solution.py
+++ b/solution.py
@@ -34,17 +34,19 @@
     return items
 
 
-def local_call(body, ids, operands, outs, scratch=(), flops=0, name=None):
+def local_call(body, ids, operands, outs, scratch=(), flops=0, name=None, stay=(), leave=()):
     moved = sum(o.size * o.dtype.itemsize for o in operands) + sum(
         o.size * o.dtype.itemsize for o in outs
     )
+    vmem, other = pl.BlockSpec(memory_space=pltpu.VMEM), pl.BlockSpec(memory_space=pl.ANY)
     return pl.pallas_call(
         body,
         out_shape=tuple(outs),
-        in_specs=[pl.BlockSpec(memory_space=pltpu.SMEM)] + [pl.BlockSpec(memory_space=pltpu.VMEM)] * len(operands),
-        out_specs=tuple(pl.BlockSpec(memory_space=pltpu.VMEM) for _ in outs),
+        in_specs=[pl.BlockSpec(memory_space=pltpu.SMEM)]
+        + [other if i in stay else vmem for i in range(len(operands))],
+        out_specs=tuple(other if i in leave else vmem for i in range(len(outs))),
         scratch_shapes=list(scratch),
-        compiler_params=pltpu.CompilerParams(vmem_limit_bytes=24 * 1024 * 1024),
+        compiler_params=pltpu.CompilerParams(vmem_limit_bytes=(40 if stay or leave else 24) * 1024 * 1024),
         cost_estimate=pl.CostEstimate(flops=flops, bytes_accessed=moved, transcendentals=0),
         name=name,
     )(ids, *operands)
@@ -58,37 +60,78 @@
     return pl.ds(pl.multiple_of(index * size, size), size)
 
 
-def forward_kernel(
-    ids, x, w_one, taps, scale, shift,
-    standard, inverse, linear, gate_prob, gated, slope, masks, mine, theirs, wide, flipped,
-):
-    core = ids[3]
+def routing_kernel(ids, targets, frames, pack, pick):
+    here = ids[4]
+    width = targets.shape[1]
+    slots, rows = pack.shape
+    quarter = rows // 2
+    blocks = width // quarter
+    capacity = slots // (2 * blocks)
+    shape = (width, width)
+    first, second = lax.broadcasted_iota(jnp.int32, shape, 0), lax.broadcasted_iota(jnp.int32, shape, 1)
+    before = ((first < second) & (first // quarter == second // quarter)).astype(F32).astype(BF)
+    names = lax.broadcasted_iota(jnp.int32, (blocks, width), 0)
+    hits = (names == targets[...]).astype(F32)
+    earlier = jnp.dot(hits.astype(BF), before, preferred_element_type=F32)
+    rank = jnp.sum(hits * earlier, axis=0, keepdims=True)
+    slot = targets[...].astype(F32) * (2 * capacity) + rank
+    shape = (width, rows)
+    row, col = lax.broadcasted_iota(jnp.int32, shape, 0), lax.broadcasted_iota(jnp.int32, shape, 1)
+    wanted = jnp.bitwise_xor(here, col // quarter) * quarter + col % quarter
+    take = (row == wanted).astype(F32).astype(BF)
+    slot_of = jnp.dot(jnp.broadcast_to(slot, (8, width)).astype(BF), take, preferred_element_type=F32)[0:1, :]
+    slot_of = slot_of.astype(jnp.int32) + lax.broadcasted_iota(jnp.int32, (1, rows), 1) // quarter * capacity
+    slot_ids = lax.broadcasted_iota(jnp.int32, (slots, rows), 0)
+    pack[...] = (slot_of == slot_ids).astype(F32).astype(BF)
+    frame_rows = pick.shape[1]
+    frame_ids = lax.broadcasted_iota(jnp.int32, (frame_rows, width), 0)
+    at_frame = (frame_ids == frames[...]).astype(F32).astype(BF)
+    block = lax.broadcasted_iota(jnp.int32, (1, width), 1) // quarter
+    rank = rank.astype(jnp.int32)
+    slot_ids = lax.broadcasted_iota(jnp.int32, (blocks * capacity, width), 0)
+    for p in range(2):
+        held = jnp.where(targets[...] == here, jnp.bitwise_xor(block, p) * capacity + rank, -1)
+        in_slot = (slot_ids == held).astype(F32).astype(BF)
+        pick[p] = lax.dot_general(at_frame, in_slot, COLS, preferred_element_type=F32).astype(BF)
+
+
+def fill_masks(ids, masks):
+    taps_count, frame_rows, _ = masks.shape
+    ends = [ids[5]]
+    for u in range(1, ids.shape[0] - 5):
+        ends.append(ends[-1] + ids[5 + u])
+    position = lax.broadcasted_iota(jnp.int32, masks.shape[1:], 0)
+
+    def segment(at):
+        return sum(jnp.where(at >= e, 1, 0) for e in ends)
+
+    here = segment(position)
+    for k in range(taps_count):
+        at = position + (k - taps_count // 2)
+        good = (segment(at) == here) & (at >= 0) & (at < frame_rows)
+        masks[k] = jnp.where(good, 1.0, 0.0)
+
+
+def clear_edges(wide):
+    edge = jnp.zeros((8, wide.shape[1]), F32)
+    wide[0:8, :] = edge
+    wide[wide.shape[0] - 8 :, :] = edge
+
+
+def standardise(x):
+    as_float = x[...].astype(F32)
+    centred = as_float - jnp.mean(as_float, axis=1, keepdims=True)
+    inverse = lax.rsqrt(jnp.mean(centred * centred, axis=1, keepdims=True) + 1e-05)
+    return centred * inverse, inverse
+
+
+def forward_kernel(ids, x, w_one, taps, scale, shift, acts, sends, kept, wide, masks, flipped, halves, sems):
     frame_rows, feat = x.shape
     taps_count = taps.shape[0]
     half = taps_count // 2
-    utterances = ids.shape[0] - 4
-    ends = [ids[4]]
-    for u in range(1, utterances):
-        ends.append(ends[-1] + ids[4 + u])
-    position = lax.broadcasted_iota(jnp.int32, (frame_rows, 128), 0)
-
-    def segment(at):
-        return sum(jnp.where(at >= e, 1, 0) for e in ends)
-
-    here = segment(position)
-    for k in range(taps_count):
-        at = position + (k - half)
-        good = (segment(at) == here) & (at >= 0) & (at < frame_rows)
-        masks[k] = jnp.where(good, 1.0, 0.0)
-    as_float = x[...].astype(F32)
-    centred = as_float - jnp.mean(as_float, axis=1, keepdims=True)
-    inv = lax.rsqrt(jnp.mean(centred * centred, axis=1, keepdims=True) + 1e-05)
-    inverse[...] = jnp.broadcast_to(inv, inverse.shape)
-    standard[...] = centred * inv
-    normed = standard[...].astype(BF)
-    edge = jnp.zeros((8, feat), F32)
-    wide[0:8, :] = edge
-    wide[8 + frame_rows : 16 + frame_rows, :] = edge
+    fill_masks(ids, masks)
+    normed = standardise(x)[0].astype(BF)
+    clear_edges(wide)
     step = 256
     for c in range(feat // step):
         cols = slice(c * step, (c + 1) * step)
@@ -96,11 +139,9 @@
         gate = jax.nn.sigmoid(
             jnp.dot(normed, w_one[:, feat + c * step : feat + (c + 1) * step], preferred_element_type=F32)
         )
-        linear[:, cols] = lin
-        gate_prob[:, cols] = gate
-        product = (lin * gate).astype(BF)
-        gated[:, cols] = product
-        wide[8 : 8 + frame_rows, cols] = product.astype(F32)
+        kept[0, :, cols] = lin
+        kept[1, :, cols] = gate
+        wide[8 : 8 + frame_rows, cols] = (lin * gate).astype(BF).astype(F32)
     for c in range(feat // 128):
         cols = slice(c * 128, (c + 1) * 128)
         total = jnp.zeros((frame_rows, 128), F32)
@@ -109,35 +150,52 @@
             total = total + taps[k : k + 1, cols] * (wide[start : start + frame_rows, cols] * masks[k])
         pre = total * scale[:, cols] + shift[:, cols]
         prob = jax.nn.sigmoid(pre)
-        slope[:, cols] = prob * (1.0 + pre * (1.0 - prob)) * scale[:, cols]
+        kept[2, :, cols] = prob * (1.0 + pre * (1.0 - prob)) * scale[:, cols]
         flipped[0, cols, :] = normed[:, cols].astype(F32).T
         flipped[1, cols, :] = (pre * prob).astype(BF).astype(F32).T
-    groups = mine.shape[0] // feat * 16
-    part = feat // (2 * groups)
+    out_acts = pltpu.make_async_copy(kept, acts, sems.at[0])
+    out_acts.start()
+    part = feat // 32
     for h in range(2):
-        for g in range(groups):
-            at = slice(h * (feat // 2) + g * part, h * (feat // 2) + (g + 1) * part)
-            mine[at, :] = flipped[h, aligned(2 * g + core, part), :].astype(BF)
-            theirs[at, :] = flipped[h, aligned(2 * g + 1 - core, part), :].astype(BF)
+        for g in range(32):
+            to = h * (feat // 2) + (g // 2) * part
+            halves[g % 2, to : to + part, :] = flipped[h, g * part : (g + 1) * part, :].astype(BF)
+    copies = [pltpu.make_async_copy(halves.at[g % 2], sends.at[g], sems.at[1 + g]) for g in range(8)]
+    for copy in copies:
+        copy.start()
+    out_acts.wait()
+    for copy in copies:
+        copy.wait()
 
 
 def partial_kernel(ids, *refs):
-    own_rows, other_rows, *blocks = refs[:-5]
-    outs, rows = refs[-5:-1], refs[-1]
+    own_rows, other_rows, *blocks = refs[:-8]
+    outs, (rows, own_copy, block_copy, sems) = refs[-8:-4], refs[-4:]
     sec, z = ids[0], ids[1]
+    fetch = [pltpu.make_async_copy(own_rows, own_copy, sems.at[0])]
+    if len(blocks) == 3:
+        fetch.append(pltpu.make_async_copy(blocks[0], block_copy, sems.at[1]))
+    for copy in fetch:
+        copy.start()
     quarter = outs[0].shape[0] // 2
-    piece = blocks[0].shape[0]
     if len(blocks) == 2:
         middle = (z == 1) | (z == 2)
-        lots = [jnp.where(middle, blocks[0][...], blocks[1][...])]
+        lots = [(0, lambda: jnp.where(middle, blocks[0][...], blocks[1][...]))]
     else:
-        lots = [jnp.concatenate([blocks[0][...], blocks[1][...]], axis=0), blocks[2][...]]
-    first = 0
-    for lot in lots:
-        last = first + lot.shape[0]
-        for w, a in enumerate((own_rows, other_rows)):
-            rows[w, :, first:last] = lax.dot_general(a[...], lot, COLS, preferred_element_type=F32)
-        first = last
+        lots = [
+            (1, lambda: jnp.concatenate([blocks[1][...], blocks[2][...]], axis=0)),
+            (0, lambda: block_copy[...]),
+        ]
+    steps = [(1, other_rows, lots[0]), (0, own_copy, lots[0])] + [
+        (w, a, lot) for lot in lots[1:] for w, a in ((1, other_rows), (0, own_copy))
+    ]
+    for n, (w, a, (at, lot)) in enumerate(steps):
+        if n == 1:
+            for copy in fetch:
+                copy.wait()
+        lot = lot()
+        first = at * block_copy.shape[0]
+        rows[w, :, first : first + lot.shape[0]] = lax.dot_general(a[...], lot, COLS, preferred_element_type=F32)
     for m, out in enumerate(outs):
         q = jnp.bitwise_xor(sec, m)
         for w in range(2):
@@ -154,36 +212,43 @@
 
 
 def module_kernel(
-    ids, incoming, order, w_two, slope, gated, masks, gate_prob, linear, taps, halves,
-    grad_out, grad_mixed, p0, p2, p4, p6, wide_gated, wide_grad,
+    ids, incoming, pick, taps, w_two, acts,
+    grad_out, grad_mixed, p0, p2, p4, p6, wide_gated, wide_grad, masks, w_here, kept, sems,
 ):
     place = ids[2]
+    fetch_w = pltpu.make_async_copy(w_two, w_here, sems.at[0])
+    fetch_w.start()
+    fetch_acts = pltpu.make_async_copy(acts, kept, sems.at[1])
+    fetch_acts.start()
     frame_rows, feat = grad_out.shape
     taps_count = taps.shape[0]
     half = taps_count // 2
     sources, slots, width = incoming.shape
     outer = sources // 2
     piece = width // outer
-    frame_ids = lax.broadcasted_iota(jnp.int32, (frame_rows, outer * slots), 0)
+    fill_masks(ids, masks)
+    clear_edges(wide_gated)
+    clear_edges(wide_grad)
     for p in range(2):
-        pick = (frame_ids == order[p : p + 1, :]).astype(F32).astype(BF)
         rows = jnp.concatenate([incoming[2 * o + p] for o in range(outer)], axis=0)
-        got = jnp.dot(pick, rows, preferred_element_type=F32).astype(BF)
+        got = jnp.dot(pick[p], rows, preferred_element_type=F32).astype(BF)
         for o in range(outer):
             first = (2 * o + p) * piece
             grad_out[:, first : first + piece] = got[:, o * piece : (o + 1) * piece]
-    edge = jnp.zeros((8, feat), F32)
-    for wide in (wide_gated, wide_grad):
-        wide[0:8, :] = edge
-        wide[8 + frame_rows : 16 + frame_rows, :] = edge
-    wide_gated[8 : 8 + frame_rows, :] = gated[...].astype(F32)
-    grad_act = lax.dot_general(grad_out[...], w_two[...], COLS, preferred_element_type=F32)
-    wide_grad[8 : 8 + frame_rows, :] = grad_act * slope[...]
+    fetch_acts.wait()
+    fetch_w.wait()
+    here = slice(8, 8 + frame_rows)
+    step = 256
+    for c in range(feat // step):
+        cols = slice(c * step, (c + 1) * step)
+        wide_gated[here, cols] = (kept[0, :, cols] * kept[1, :, cols]).astype(BF).astype(F32)
+        grad_act = lax.dot_general(grad_out[...], w_here[cols, :], COLS, preferred_element_type=F32)
+        wide_grad[here, cols] = grad_act * kept[2, :, cols]
     step = 128
     tap_rows = []
     for c in range(feat // step):
         cols = slice(c * step, (c + 1) * step)
-        grad_conv = wide_grad[8 : 8 + frame_rows, cols]
+        grad_conv = wide_grad[here, cols]
         total = jnp.zeros((frame_rows, step), F32)
         columns = []
         for k in range(taps_count):
@@ -192,17 +257,13 @@
             columns.append(jnp.sum(window * grad_conv, axis=0, keepdims=True))
             start = 8 + half - k
             back = 2 * half - k
-            total = total + taps[k : k + 1, cols] * (
-                wide_grad[start : start + frame_rows, cols] * masks[back]
-            )
+            total = total + taps[k : k + 1, cols] * (wide_grad[start : start + frame_rows, cols] * masks[back])
         tap_rows.append(jnp.concatenate(columns + [jnp.zeros((16 - taps_count, step), F32)], axis=0))
-        gate = gate_prob[:, cols]
+        gate = kept[1, :, cols]
         first = total * gate
         grad_mixed[:, c * step : (c + 1) * step] = first.astype(BF)
-        grad_mixed[:, feat + c * step : feat + (c + 1) * step] = (first * linear[:, cols] * (1.0 - gate)).astype(BF)
+        grad_mixed[:, feat + c * step : feat + (c + 1) * step] = (first * kept[0, :, cols] * (1.0 - gate)).astype(BF)
     tap_rows = jnp.concatenate(tap_rows, axis=1).astype(BF)
-    tap_halves = jnp.dot(tap_rows, halves[...], preferred_element_type=F32)
-    tap_halves = tap_halves.astype(BF)
     w1_cols, w2_cols = feat // 2, feat // 4
     for mask, out in enumerate((p0, p2, p4, p6)):
         q = jnp.bitwise_xor(place, mask)
@@ -210,42 +271,58 @@
         out[0:frame_rows, w1_cols:] = grad_out[:, aligned(q, w2_cols)]
         for h in range(2):
             tap_at = slice(frame_rows + 16 * h, frame_rows + 16 * (h + 1))
-            out[tap_at, 0:w1_cols] = tap_halves[:, h * w1_cols : (h + 1) * w1_cols]
+            out[tap_at, 0:w1_cols] = tap_rows[:, h * w1_cols : (h + 1) * w1_cols]
             out[tap_at, w1_cols:] = jnp.zeros((16, w2_cols), BF)
 
 
-def weights_kernel(ids, e0, e1, e2, e3, e4, e5, e6, e7, g0, g1, g2, g3, g4, g5, g6, g7, own, s1, s2, s3, rows, tap_sum):
-    z, core = ids[1], ids[3]
-    frame_rows = e0.shape[1]
-    half = e0.shape[0] // 2
+def weights_kernel(ids, early, g0, g1, g2, g3, g4, g5, g6, g7, own, s1, s2, s3, rows, tap_sum, feats, sems):
+    z = ids[1]
+    me = 2 * ids[2] + ids[3]
+    copies = []
+    for m in range(8):
+        copies.append(pltpu.make_async_copy(early.at[jnp.bitwise_xor(me, m)], feats.at[m], sems.at[m]))
+        copies[-1].start()
+    gots = (g0, g1, g2, g3, g4, g5, g6, g7)
+    frame_rows = feats.shape[2]
+    half = feats.shape[1] // 2
     w1_cols = half
-    tap_sum[...] = sum(
-        g[aligned(core + frame_rows // 16, 16), 0:w1_cols].astype(F32) for g in (g0, g1, g2, g3, g4, g5, g6, g7))
-    pairs = ((e0, e1, g0, g1), (e2, e3, g2, g3), (e4, e5, g4, g5), (e6, e7, g6, g7))
+    tap_sum[...] = sum(g[frame_rows:, 0:w1_cols].astype(F32) for g in gots)
+    for copy in copies:
+        copy.wait()
     for cols, first in ((slice(0, w1_cols), 0), (slice(w1_cols, g0.shape[1]), half)):
         total = None
-        for ea, eb, ga, gb in pairs:
-            both = jnp.concatenate([ga[0:frame_rows, cols], gb[0:frame_rows, cols]], axis=0)
-            feats = jnp.concatenate([ea[first : first + half, :], eb[first : first + half, :]], axis=1)
-            term = jnp.dot(feats, both, preferred_element_type=F32)
+        for m in range(0, 8, 2):
+            both = jnp.concatenate([gots[m][0:frame_rows, cols], gots[m + 1][0:frame_rows, cols]], axis=0)
+            pair = jnp.concatenate([feats[m, first : first + half, :], feats[m + 1, first : first + half, :]], axis=1)
+            term = jnp.dot(pair, both, preferred_element_type=F32)
             total = term if total is None else total + term
         rows[:, cols] = total
     block = half // 4
     for m, out in enumerate((own, s1, s2, s3)):
         o = jnp.bitwise_xor(z, m)
         out[0:block, :] = rows[aligned(o, block), :].astype(out.dtype)
-        out[block:, 0:block] = tap_sum[:, aligned(o, block)].astype(out.dtype)
-        out[block:, block:] = jnp.zeros((out.shape[0] - block, out.shape[1] - block), out.dtype)
+        out[block:, 0 : 2 * block] = tap_sum[aligned(o // 2, 16), aligned(o % 2, 2 * block)].astype(out.dtype)
+        out[block:, 2 * block :] = jnp.zeros((out.shape[0] - block, out.shape[1] - 2 * block), out.dtype)
+
+
+def tail_kernel(ids, x, grad_mixed, w_one, grad_out, out):
+    standard, inverse = standardise(x)
+    grad_norm = lax.dot_general(grad_mixed[...], w_one[...], COLS, preferred_element_type=F32)
+    grad_input = inverse * (
+        grad_norm
+        - jnp.mean(grad_norm, axis=1, keepdims=True)
+        - standard * jnp.mean(grad_norm * standard, axis=1, keepdims=True)
+    )
+    out[...] = (grad_out[...].astype(F32) + grad_input).astype(BF)
 
 
 def sum_kernel(ids, own, r1, r2, r3, mine, f1, f2, f3, taps, rows):
     place = ids[2]
-    block = taps.shape[1]
+    part = mine.shape[0]
     rows[...] = own[...] + r1[...].astype(F32) + r2[...].astype(F32) + r3[...].astype(F32)
-    part = block // 4
     for m, out in enumerate((mine, f1, f2, f3)):
         out[...] = rows[aligned(jnp.bitwise_xor(place, m), part), :].astype(out.dtype)
-    taps[...] = rows[block:, 0:block]
+    taps[...] = rows[4 * part :, 0 : 8 * part]
 
 
 def assembly_kernel(ids, mine, r1, r2, r3, w1, w2):
@@ -494,7 +571,7 @@
     two = swap("rep", proj_weight, 4)
     one = swap("rep", proj_weight, 2)
     adj_other = swap("rep", adj_grad, 1)
-    proj_again, two = lax.optimization_barrier((proj_weight, two))
+    proj_again, two, layer_later = lax.optimization_barrier((proj_weight, two, layer_input))
     inner = lax.ppermute(proj_again, "rep", [(o * 2 + p, (3 - o) * 2 + p) for o in (1, 2) for p in (0, 1)])
     ends = lax.ppermute(two, "rep", [(o * 2 + p, (o ^ 1) * 2 + p) for o in (1, 2) for p in (0, 1)])
 
@@ -502,23 +579,6 @@
     frames = adj_frame.reshape(reps, sections, quarter)
     sec_targets = lax.dynamic_index_in_dim(targets, sec_here, 1, keepdims=False)
     sec_frames = lax.dynamic_index_in_dim(frames, sec_here, 1, keepdims=False)
-    row_a = lax.broadcasted_iota(jnp.int32, (quarter, quarter), 0)
-    row_b = lax.broadcasted_iota(jnp.int32, (quarter, quarter), 1)
-    same = (sec_targets[:, :, None] == sec_targets[:, None, :]) & (row_b < row_a)[None]
-    rank = jnp.sum(same.astype(jnp.int32), axis=2)
-    mine = sec_targets == rep_here
-    slots = lax.broadcasted_iota(jnp.int32, (1, capacity, 1), 1)
-    hit = mine[:, None, :] & (rank[:, None, :] == slots)
-    slot_frames = jnp.sum(jnp.where(hit, sec_frames[:, None, :] + 1, 0), axis=2) - 1
-
-    pair_blocks = jnp.stack([rep_here, jnp.bitwise_xor(rep_here, 1)])
-    pair_targets = jnp.concatenate([lax.dynamic_index_in_dim(sec_targets, pair_blocks[w], 0, keepdims=False) for w in range(2)])
-    pair_rank = jnp.concatenate([lax.dynamic_index_in_dim(rank, pair_blocks[w], 0, keepdims=False) for w in range(2)])
-    member = lax.broadcasted_iota(jnp.int32, (2 * quarter,), 0) // quarter
-    slot_of = (pair_targets * 2 + member) * capacity + pair_rank
-    slot_ids = lax.broadcasted_iota(jnp.int32, (reps * 2 * capacity, 2 * quarter), 0)
-    pack = (slot_of[None, :] == slot_ids).astype(BF)
-
     part_rows = feat // (reps * sections)
 
     here = rep_here * sections + sec_here
@@ -526,23 +586,46 @@
     place = (here // 2) % 4
     BOTH = ("rep", "section")
 
-    ids = jnp.stack([sec_here, outer_here, place, core]).astype(jnp.int32)
+    ids = jnp.stack([sec_here, outer_here, place, core, rep_here]).astype(jnp.int32)
     ids = jnp.concatenate([ids, utt_frames[0]])
+    pack, pick = local_call(
+        routing_kernel,
+        ids,
+        (sec_targets.reshape(1, -1), sec_frames.reshape(1, -1)),
+        [like((reps * 2 * capacity, 2 * quarter), BF), like((2, frame_rows, reps * capacity), BF)],
+        name="routing",
+    )
     tap_values = conv_taps.astype(F32)
-    square = like((frame_rows, feat), F32)
-    half_t = like((feat, frame_rows), BF)
-    standard, inverse, linear, gate_prob, gated, slope, masks, mine_half, their_half = local_call(
+    square = (frame_rows, feat)
+    group = 8
+    dma = pltpu.SemaphoreType.DMA
+    wide = pltpu.VMEM((frame_rows + 16, feat), F32)
+    mask_space = pltpu.VMEM((taps_count, frame_rows, 128), F32)
+    acts, sends = local_call(
         forward_kernel,
         ids,
-        (layer_input, w_pointwise1, tap_values, conv_scale.reshape(1, -1), conv_shift.reshape(1, -1)),
-        [square, like((frame_rows, 128), F32), square, square, like((frame_rows, feat), BF), square]
-        + [like((taps_count, frame_rows, 128), F32), half_t, half_t],
-        [pltpu.VMEM((frame_rows + 16, feat), F32), pltpu.VMEM((2, feat, frame_rows), F32)],
+        (layer_later, w_pointwise1, tap_values, conv_scale.reshape(1, -1), conv_shift.reshape(1, -1)),
+        [like((3, *square), F32), like((group, feat, frame_rows), BF)],
+        [
+            pltpu.VMEM((3, *square), F32),
+            wide,
+            mask_space,
+            pltpu.VMEM((2, feat, frame_rows), F32),
+            pltpu.VMEM((2, feat, frame_rows), BF),
+            dma((1 + group,)),
+        ],
         flops=4 * frame_rows * feat * feat,
         name="forward",
-    )
-    inverse = inverse[:, :1]
-    early = [mine_half] + [swap(BOTH, their_half if m % 2 else mine_half, m) for m in range(1, 8)]
+        leave=(0, 1),
+    )
+    early = lax.all_to_all(
+        sends,
+        BOTH,
+        split_axis=0,
+        concat_axis=0,
+        axis_index_groups=[[g * group + m for m in range(group)] for g in range(reps * sections // group)],
+        tiled=True,
+    )
 
     rows = 2 * quarter
 
@@ -553,17 +636,17 @@
             ids,
             (adj_grad, adj_other, *lot),
             [like((rows, cols), F32)] + [like((rows, cols), BF)] * 3,
-            [pltpu.VMEM((2, block_rows, cols), F32)],
+            [pltpu.VMEM((2, block_rows, cols), F32), pltpu.VMEM(adj_grad.shape, BF), pltpu.VMEM(proj_weight.shape, BF), dma((2,))],
+            stay=(0, 2) if len(lot) == 3 else (0,),
             flops=4 * block_rows * adj_grad.shape[1] * cols,
             name=name,
         )
         return [sums[0]] + [swap("section", sums[m], m) for m in (1, 2, 3)]
 
-    two, early[1:4] = lax.optimization_barrier((two, early[1:4]))
     lot_one = products("products", proj_weight, one, two)
-    inner, ends, lot_one[0] = lax.optimization_barrier((inner, ends, lot_one[0]))
+    inner, ends, lot_one = lax.optimization_barrier((inner, ends, lot_one))
     lot_two = products("last_products", inner, ends)
-    lot_two[0], early[4:] = lax.optimization_barrier((lot_two[0], early[4:]))
+    lot_two, early = lax.optimization_barrier((lot_two, early))
     lane = outer * piece
     (packed,) = local_call(
         packing_kernel,
@@ -575,24 +658,17 @@
     )
     outgoing = packed.reshape(reps, 2 * capacity, lane)
     incoming = lax.all_to_all(outgoing, "rep", split_axis=0, concat_axis=0, tiled=True)
-    slot_frames = slot_frames.reshape(outer, 2, capacity)
-    order = jnp.stack([jnp.stack([slot_frames[:, p], slot_frames[:, 1 - p]], axis=1).reshape(-1) for p in range(2)])
-    channel = lax.broadcasted_iota(jnp.int32, (feat, feat), 0)
-    column = lax.broadcasted_iota(jnp.int32, (feat, feat), 1)
-    group = channel // part_rows
-    moved = (group % 2) * (feat // 2) + (group // 2) * part_rows + channel % part_rows
-    to_halves = (moved == column).astype(BF)
     late = like((frame_rows + 32, 3 * feat // 4), BF)
     lot = like((frame_rows + 16, 3 * feat // 4), BF)
-    wide = pltpu.VMEM((frame_rows + 16, feat), F32)
     grad_out, grad_mixed, p0, p2, p4, p6 = local_call(
         module_kernel,
         ids,
-        (incoming, order, w_pointwise2, slope, gated, masks, gate_prob, linear, tap_values, to_halves),
-        [like((frame_rows, feat), BF), like((frame_rows, 2 * feat), BF)] + [late] * 4,
-        [wide, wide],
+        (incoming, pick, tap_values, w_pointwise2, acts),
+        [like(square, BF), like((frame_rows, 2 * feat), BF)] + [late] * 4,
+        [wide, wide, mask_space, pltpu.VMEM((feat, feat), BF), pltpu.VMEM((3, *square), F32), dma((2,))],
         flops=2 * frame_rows * feat * feat + 60 * frame_rows * feat,
         name="module",
+        stay=(3, 4),
     )
     got = [p0, swap(BOTH, p0, 1)]
     far = [swap(BOTH, p, m) for m, p in ((2, p2), (4, p4), (6, p6))]
@@ -601,9 +677,15 @@
     sums = local_call(
         weights_kernel,
         ids,
-        (*early, *got),
+        (early, *got),
         [like(lot.shape, F32)] + [lot] * 3,
-        [pltpu.VMEM((feat // 2, 3 * feat // 4), F32), pltpu.VMEM((16, feat // 2), F32)],
+        [
+            pltpu.VMEM((feat // 2, 3 * feat // 4), F32),
+            pltpu.VMEM((32, feat // 2), F32),
+            pltpu.VMEM((group, feat, frame_rows), BF),
+            dma((group,)),
+        ],
+        stay=(0,),
         flops=2 * 8 * frame_rows * (feat // 2) * (3 * feat // 4),
         name="weights",
     )
@@ -613,7 +695,7 @@
         sum_kernel,
         ids,
         (sums[0], *given),
-        [like(final, F32)] + [like(final, BF)] * 3 + [like((16, 4 * part_rows), F32)],
+        [like(final, F32)] + [like(final, BF)] * 3 + [like((16, 8 * part_rows), F32)],
         [pltpu.VMEM(lot.shape, F32)],
         name="sums",
     )
@@ -625,15 +707,18 @@
         [like((part_rows, 2 * feat), F32), like((part_rows, feat), F32)],
         name="assembly",
     )
-    taps_grad = lax.dynamic_index_in_dim(tap_part.reshape(16, 4, part_rows), place, 1, keepdims=False)[:taps_count].T
-
-    grad_norm = lax.dot_general(grad_mixed, w_pointwise1, COLS, preferred_element_type=F32)
-    grad_input = inverse * (
-        grad_norm
-        - jnp.mean(grad_norm, axis=1, keepdims=True)
-        - standard * jnp.mean(grad_norm * standard, axis=1, keepdims=True)
-    )
-    input_grad = (grad_out.astype(F32) + grad_input).astype(BF)
+    here_taps = lax.dynamic_index_in_dim(
+        tap_part.reshape(16, 8, part_rows), 2 * place + core, 1, keepdims=False
+    )
+    taps_grad = here_taps[:taps_count].T
+    (input_grad,) = local_call(
+        tail_kernel,
+        ids,
+        (layer_input, grad_mixed, w_pointwise1, grad_out),
+        [like(square, BF)],
+        flops=4 * frame_rows * feat * feat,
+        name="tail",
+    )
     return input_grad, w1_grad, w2_grad, taps_grad
 
 

time: 157 us -> 186 us (1.18)
  waiting for transfers between devices: 59.1 us -> 90.3 us
  blocking collectives: 0 us -> 12.9 us
  local copies, waits for them, and re-layouts: 31.1 us -> 24 us
  starting transfers between devices: 35.4 us -> 29.6 us
  other arithmetic: 5.34 us -> 1.47 us
  Pallas kernels: 20.6 us -> 24.4 us
    ppermute x29 -> x22, waiting for transfers between devices: 51.9 us -> 90.3 us  [swap(): return lax.ppermute(values, axis, xor_perm(size_of(axis), mask))]
    all_to_all x0 -> x1, blocking collectives: none -> 12.9 us  [line_shards(): lax.all_to_all(outgoing, 'rep', split_axis=0, concat_axis=0, tiled=True)]
    unnamed x85 -> x46, local copies, waits for them, and re-layouts: 28.3 us -> 21 us
    all_to_all x1, waiting for transfers between devices: 7.2 us -> 0.01 us  [line_shards(): lax.all_to_all(sends, BOTH, split_axis=0, concat_axis=0, axis_index_group...]
    ppermute x29 -> x22, starting transfers between devices: 29.1 us -> 22.9 us  [swap(): return lax.ppermute(values, axis, xor_perm(size_of(axis), mask))]
    pallas_call x8 -> x10, Pallas kernels: 20.6 us -> 24.4 us  [local_call(): pl.pallas_call(body, out_shape=tuple(outs), in_specs=[pl.BlockSpec(memory...]
    convert_element_type x3 -> x0, other arithmetic: 2.5 us -> none  [the longest x1 1.58 us: line_shards(): to_halves = (moved == column).astype(BF)]
  transfers between devices with their start and end apart: 32 -> 25, of which waited for: 17 -> 14; matrix products, arithmetic and copies ran while one was open for 7% -> 3% of each run, Pallas kernels for 7% -> 6%
where the time goes in v3:
time: 186 us; the launch traced here: 184 us
  waiting for transfers between devices  90.3 us (49%)
  starting transfers between devices  29.6 us (16%)
  Pallas kernels  24.4 us (13%)
  local copies, waits for them, and re-layouts  24 us (13%)
  blocking collectives  12.9 us (7%)
    ppermute x22, waiting for transfers between devices, swap(): return lax.ppermute(values, axis, xor_perm(size_of(axis), mask))  90.3 us
    pallas_call x10, Pallas kernels, local_call(): pl.pallas_call(body, out_shape=tuple(outs), in_specs=[pl.BlockSpec(memory...  24.4 us
    ppermute x22, starting transfers between devices, swap(): return lax.ppermute(values, axis, xor_perm(size_of(axis), mask))  22.9 us
    unnamed x46, local copies, waits for them, and re-layouts  21 us
    all_to_all x1, blocking collectives, line_shards(): lax.all_to_all(outgoing, 'rep', split_axis=0, concat_axis=0, tiled=True)  12.9 us
    all_to_all x1, starting transfers between devices, line_shards(): lax.all_to_all(sends, BOTH, split_axis=0, concat_axis=0, axis_index_group...  3.91 us
  transfers between devices with their start and end apart: 25, of which 14 were waited for; matrix products, arithmetic and copies ran while one was open for 3% of the time, Pallas kernels for 6%

profile of v3, /device:TPU:0, one launch (start us, length us, event | category | flops | bytes accessed | tf_op | source)
XLA Modules:
  0.0 183.5 jit_solution(5411729853022434232)
XLA Ops:
  0.6 4.1 %collective-permute-start = (bf16[128,2048]{1,0:T(8,128)(2,1)}, bf16[128,2048]{1,0:T(8,128)(2,1)S(1)}, u32[]{:S(2)}, u32[]{:S(2)}) collective-permute-start(bf16[128,2048]{1,0:T(8,128)(2,1)} %refs_2_.1), channel_id=1, source_target_pairs={{0,16},{4,20},{8,24},{12,28},{16,0},{20,4},{24,8},{28,12},{1,17},{... | collective-permute-start | bytes 1572872 | tf_op jit(solution)/shard_map/ppermute | solution.py:25
  4.7 0.8 convert_element_type.3.taps
  5.5 0.7 concatenate.3.ids
  6.2 21.9 %collective-permute-done.refs_4_ = bf16[128,2048]{1,0:T(8,128)(2,1)S(1)} collective-permute-done((bf16[128,2048]{1,0:T(8,128)(2,1)}, bf16[128,2048]{1,0:T(8,128)(2,1)S(1)}, u32[]{:S(2)}, u32[]{:S(2)}) %collective-permute-start) | collective-permute-done | bytes 524320 | tf_op jit(solution)/shard_map/ppermute | solution.py:25
  28.1 2.4 %copy-done = bf16[1024,2048]{1,0:T(8,128)(2,1)S(1)} copy-done((bf16[1024,2048]{1,0:T(8,128)(2,1)S(1)}, bf16[1024,2048]{1,0:T(8,128)(2,1)}, u32[]{:S(2)}) %copy-start) | copy-done | bytes 4194328
  30.5 0.9 copy-done.9
  31.4 0.7 copy-done.18
  32.1 0.7 copy-done.19
  32.8 3.3 %forward.1 = (f32[3,128,1024]{2,1,0:T(8,128)S(1)}, bf16[8,1024,128]{2,1,0:T(8,128)(2,1)S(1)}) custom-call(s32[9]{0:T(128)S(1)} %concatenate.3.ids, bf16[128,1024]{1,0:T(8,128)(2,1)S(1)} %copy-done.9, bf16[1024,2048]{1,0:T(8,128)(2,1)S(1)} %copy-done, f32[9,1024]{1,0:T(8,128)S(1)} %convert_element_type.3.taps, f32[1,1024]{1,0:T(1,128)S(1)} %bitcast.20, ...), custom_call_target="tpu_custom_call" | custom-call | flops 536870912 | bytes 8171520 | tf_op jit(solution)/shard_map/forward/pallas_call | solution.py:42
  36.2 1.3 copy-done.6
  37.5 1.2 copy-done.7
  38.7 3.9 %all-to-all-start = ((bf16[8,1024,128]{2,1,0:T(8,128)(2,1)}), bf16[8,1024,128]{2,1,0:T(8,128)(2,1)S(1)}, u32[]{:S(2)}, u32[]{:S(2)}) async-start(bf16[8,1024,128]{2,1,0:T(8,128)(2,1)} %copy-done.6), calls=%async_computation | async-start | bytes 4194304 | tf_op jit(solution)/shard_map/all_to_all | solution.py:621
  42.6 2.0 %collective-permute-start.3 = (bf16[256,2048]{1,0:T(8,128)(2,1)S(1)}, bf16[256,2048]{1,0:T(8,128)(2,1)S(1)}, u32[]{:S(2)}, u32[]{:S(2)}) collective-permute-start(bf16[256,2048]{1,0:T(8,128)(2,1)S(1)} %copy-done.2), channel_id=1, source_target_pairs={{0,4},{4,0},{8,12},{12,8},{16,20},{20,16},{24,28},{28,24},{1,5},{5... | collective-permute-start | bytes 3145736 | tf_op jit(solution)/shard_map/ppermute | solution.py:25
  44.6 0.8 collective-permute-start.4
  45.4 1.3 collective-permute-start.2
  46.6 1.5 collective-permute-start.1
  48.1 11.5 %collective-permute-done.4.refs_3_ = bf16[128,2048]{1,0:T(8,128)(2,1)S(1)} collective-permute-done((bf16[128,2048]{1,0:T(8,128)(2,1)}, bf16[128,2048]{1,0:T(8,128)(2,1)S(1)}, u32[]{:S(2)}, u32[]{:S(2)}) %collective-permute-start.4) | collective-permute-done | bytes 524320 | tf_op jit(solution)/shard_map/ppermute | solution.py:25
  59.6 31.1 %collective-permute-done.3.refs_1_ = bf16[256,2048]{1,0:T(8,128)(2,1)S(1)} collective-permute-done((bf16[256,2048]{1,0:T(8,128)(2,1)S(1)}, bf16[256,2048]{1,0:T(8,128)(2,1)S(1)}, u32[]{:S(2)}, u32[]{:S(2)}) %collective-permute-start.3) | collective-permute-done | bytes 1048608 | tf_op jit(solution)/shard_map/ppermute | solution.py:25
  90.7 1.0 copy-done.11
  91.8 1.0 copy-done.13
  92.8 3.4 %products.1 = (f32[128,384]{1,0:T(8,128)S(1)}, bf16[128,384]{1,0:T(8,128)(2,1)}, bf16[128,384]{1,0:T(8,128)(2,1)}, bf16[128,384]{1,0:T(8,128)(2,1)}) custom-call(s32[9]{0:T(128)S(1)} %concatenate.3.ids, bf16[256,2048]{1,0:T(8,128)(2,1)S(1)} %copy-done.2, bf16[256,2048]{1,0:T(8,128)(2,1)S(1)} %collective-permute-done.3.refs_1_, ...), custom_call_target="tpu_custom_call" | custom-call | flops 805306368 | bytes 4161536 | tf_op jit(solution)/shard_map/products/pallas_call | solution.py:42
  96.2 1.0 copy-done.3
  97.2 1.5 collective-permute-start.6
  99.7 0.7 reduce.7
  100.4 0.7 reshape_squeeze.3
  101.0 0.7 reshape.35
  101.7 1.4 collective-permute-done.6.r2
  103.1 1.3 collective-permute-done.7.r3
  104.4 1.2 copy-done.4
  105.7 3.3 %last_products.1 = (f32[128,128]{1,0:T(8,128)S(1)}, bf16[128,128]{1,0:T(8,128)(2,1)}, bf16[128,128]{1,0:T(8,128)(2,1)S(1)}, bf16[128,128]{1,0:T(8,128)(2,1)}) custom-call(s32[9]{0:T(128)S(1)} %concatenate.3.ids, bf16[256,2048]{1,0:T(8,128)(2,1)S(1)} %copy-done.2, bf16[256,2048]{1,0:T(8,128)(2,1)S(1)} %copy-done.4, ...), custom_call_target="tpu_custom_call" | custom-call | flops 268435456 | bytes 3309568 | tf_op jit(solution)/shard_map/last_products/pallas_call | solution.py:42
  109.6 1.3 collective-permute-start.10
  111.1 0.6 collective-permute-start.9
  111.8 0.8 dynamic-slice_reduce_fusion
  112.7 1.0 routing.1
  113.7 1.4 collective-permute-done.9.l2
  115.1 0.8 copy-done.17
  115.9 1.2 packing.1
  117.1 12.9 %all_to_all.10.incoming = bf16[8,32,512]{2,1,0:T(8,128)(2,1)S(1)} all-to-all(bf16[8,32,512]{2,1,0:T(8,128)(2,1)S(1)} %bitcast.19), channel_id=1, replica_groups=mesh['rep'=8,'section'=4] {'rep'}, dimensions={0} | all-to-all | bytes 524288 | tf_op jit(solution)/shard_map/all_to_all | solution.py:660
  130.0 1.6 copy-done.5
  131.6 1.4 copy-done.8
  133.0 4.6 %module.1 = (bf16[128,1024]{1,0:T(8,128)(2,1)S(1)}, bf16[128,2048]{1,0:T(8,128)(2,1)S(1)}, bf16[160,768]{1,0:T(8,128)(2,1)S(1)}, bf16[160,768]{1,0:T(8,128)(2,1)...) custom-call(s32[9]{0:T(128)S(1)} %concatenate.3.ids, bf16[8,32,512]{2,1,0:T(8,128)(2,1)S(1)} %all_to_all.10.incoming, ...), custom_call_target="tpu_custom_call" | custom-call | flops 276299776 | bytes 5804032 | tf_op jit(solution)/shard_map/module/pallas_call | solution.py:42
  137.6 0.7 copy-done.14
  138.3 0.8 collective-permute-start.12
  139.1 1.4 collective-permute-start.14
  140.6 1.2 collective-permute-start.16
  141.8 4.7 %collective-permute-done.12.g2 = bf16[160,768]{1,0:T(8,128)(2,1)S(1)} collective-permute-done((bf16[160,768]{1,0:T(8,128)(2,1)S(1)}, bf16[160,768]{1,0:T(8,128)(2,1)S(1)}, u32[]{:S(2)}, u32[]{:S(2)}) %collective-permute-start.12) | collective-permute-done | bytes 245792 | tf_op jit(solution)/shard_map/ppermute | solution.py:25
  146.5 3.3 %collective-permute-done.14.g4 = bf16[160,768]{1,0:T(8,128)(2,1)S(1)} collective-permute-done((bf16[160,768]{1,0:T(8,128)(2,1)S(1)}, bf16[160,768]{1,0:T(8,128)(2,1)S(1)}, u32[]{:S(2)}, u32[]{:S(2)}) %collective-permute-start.14) | collective-permute-done | bytes 245792 | tf_op jit(solution)/shard_map/ppermute | solution.py:25
  150.3 1.0 collective-permute-done.15.g5
  151.6 2.7 %weights.1 = (f32[144,768]{1,0:T(8,128)S(1)}, bf16[144,768]{1,0:T(8,128)(2,1)}, bf16[144,768]{1,0:T(8,128)(2,1)}, bf16[144,768]{1,0:T(8,128)(2,1)}) custom-call(s32[9]{0:T(128)S(1)} %concatenate.3.ids, bf16[8,1024,128]{2,1,0:T(8,128)(2,1)S(1)} %all-to-all-done.early, bf16[160,768]{1,0:T(8,128)(2,1)S(1)} %get-tuple-element.75.g0, ...), custom_call_target="tpu_custom_call" | custom-call | flops 805306368 | bytes 5169152 | tf_op jit(solution)/shard_map/weights/pallas_call | solution.py:42
  154.4 1.0 collective-permute-start.18
  155.4 2.4 %collective-permute-start.19 = (bf16[144,768]{1,0:T(8,128)(2,1)}, bf16[144,768]{1,0:T(8,128)(2,1)S(1)}, u32[]{:S(2)}, u32[]{:S(2)}) collective-permute-start(bf16[144,768]{1,0:T(8,128)(2,1)} %get-tuple-element.81), channel_id=1, source_target_pairs={{0,16},{1,17},{2,18},{3,19},{4,20},{5,21},{6,22},{7,23},{8,24},{9,... | collective-permute-start | bytes 663560 | tf_op jit(solution)/shard_map/ppermute | solution.py:25
  157.8 1.0 collective-permute-start.20
  158.8 2.2 %copy-done.1 = bf16[1024,2048]{1,0:T(8,128)(2,1)S(1)} copy-done((bf16[1024,2048]{1,0:T(8,128)(2,1)S(1)}, bf16[1024,2048]{1,0:T(8,128)(2,1)}, u32[]{:S(2)}) %copy-start.1) | copy-done | bytes 4194328
  161.0 0.9 copy-done.15
  162.0 2.9 %tail.1 = bf16[128,1024]{1,0:T(8,128)(2,1)} custom-call(s32[9]{0:T(128)S(1)} %concatenate.3.ids, bf16[128,1024]{1,0:T(8,128)(2,1)S(1)} %copy-done.10, bf16[128,2048]{1,0:T(8,128)(2,1)S(1)} %get-tuple-element.72.grad_mixed, bf16[1024,2048]{1,0:T(8,128)(2,1)S(1)} %copy-done.1, bf16[128,1024]{1,0:T(8,128)(2,1)S(1)} %copy-done.15), custom_call_target="tpu_custom_call" | custom-call | flops 536870912 | bytes 5505024 | tf_op jit(solution)/shard_map/tail/pallas_call | solution.py:42
  164.9 1.2 collective-permute-done.18.r1
  166.1 8.2 %collective-permute-done.19.r2 = bf16[144,768]{1,0:T(8,128)(2,1)S(1)} collective-permute-done((bf16[144,768]{1,0:T(8,128)(2,1)}, bf16[144,768]{1,0:T(8,128)(2,1)S(1)}, u32[]{:S(2)}, u32[]{:S(2)}) %collective-permute-start.19) | collective-permute-done | bytes 221216 | tf_op jit(solution)/shard_map/ppermute | solution.py:25
  174.3 0.7 sums.1
  175.0 1.3 collective-permute-start.21
  176.3 0.9 collective-permute-start.22
  177.2 1.3 collective-permute-start.23
  179.3 1.1 collective-permute-done.22.r2
  180.4 1.8 %collective-permute-done.23.r3 = bf16[32,768]{1,0:T(8,128)(2,1)S(1)} collective-permute-done((bf16[32,768]{1,0:T(8,128)(2,1)S(1)}, bf16[32,768]{1,0:T(8,128)(2,1)S(1)}, u32[]{:S(2)}, u32[]{:S(2)}) %collective-permute-start.23) | collective-permute-done | bytes 49184 | tf_op jit(solution)/shard_map/ppermute | solution.py:25
  182.2 1.3 assembly.1
  (53 shorter events, 3.6 us)
Async XLA Ops:
  0.6 27.5 %collective-permute-start = (bf16[128,2048]{1,0:T(8,128)(2,1)}, bf16[128,2048]{1,0:T(8,128)(2,1)S(1)}, u32[]{:S(2)}, u32[]{:S(2)}) collective-permute-start(bf16[128,2048]{1,0:T(8,128)(2,1)} %refs_2_.1), channel_id=1, source_target_pairs={{0,16},{4,20},{8,24},{12,28},{16,0},{20,4},{24,8},{28,12},{1,17},{... | collective-permute-start | bytes 1572872 | tf_op jit(solution)/shard_map/ppermute | solution.py:25
  28.1 8.0 %copy-start.12 = (bf16[128,2048]{1,0:T(8,128)(2,1)}, bf16[128,2048]{1,0:T(8,128)(2,1)S(1)}, u32[]{:S(2)}) copy-start(bf16[128,2048]{1,0:T(8,128)(2,1)S(1)} %collective-permute-done.refs_4_) | copy-start | bytes 1572868
  28.1 2.4 %copy-start = (bf16[1024,2048]{1,0:T(8,128)(2,1)S(1)}, bf16[1024,2048]{1,0:T(8,128)(2,1)}, u32[]{:S(2)}) copy-start(bf16[1024,2048]{1,0:T(8,128)(2,1)} %w_one.3) | copy-start | bytes 12582916
  30.5 0.9 copy-start.9
  31.4 0.7 copy-start.18
  32.1 0.7 copy-start.19
  36.1 1.3 copy-start.6
  37.5 1.2 copy-start.7
  38.6 3.9 %copy-start.2 = (bf16[256,2048]{1,0:T(8,128)(2,1)S(1)}, bf16[256,2048]{1,0:T(8,128)(2,1)}, u32[]{:S(2)}) copy-start(bf16[256,2048]{1,0:T(8,128)(2,1)} %refs_0_.3) | copy-start | bytes 3145732
  38.7 61.0 %copy-start.21 = (s32[2048,1]{0,1:T(1,128)S(1)}, s32[2048,1]{0,1:T(1,128)}, u32[]{:S(2)}) copy-start(s32[2048,1]{0,1:T(1,128)} %param.20) | copy-start | bytes 24580
  38.7 62.4 %copy-start.20 = (s32[2048]{0:T(1024)S(1)}, s32[2048]{0:T(1024)}, u32[]{:S(2)}) copy-start(s32[2048]{0:T(1024)} %param.21) | copy-start | bytes 24580
  38.7 76.4 %all-to-all-start = ((bf16[8,1024,128]{2,1,0:T(8,128)(2,1)}), bf16[8,1024,128]{2,1,0:T(8,128)(2,1)S(1)}, u32[]{:S(2)}, u32[]{:S(2)}) async-start(bf16[8,1024,128]{2,1,0:T(8,128)(2,1)} %copy-done.6), calls=%async_computation | async-start | bytes 4194304 | tf_op jit(solution)/shard_map/all_to_all | solution.py:621
  42.6 48.2 %collective-permute-start.3 = (bf16[256,2048]{1,0:T(8,128)(2,1)S(1)}, bf16[256,2048]{1,0:T(8,128)(2,1)S(1)}, u32[]{:S(2)}, u32[]{:S(2)}) collective-permute-start(bf16[256,2048]{1,0:T(8,128)(2,1)S(1)} %copy-done.2), channel_id=1, source_target_pairs={{0,4},{4,0},{8,12},{12,8},{16,20},{20,16},{24,28},{28,24},{1,5},{5... | collective-permute-start | bytes 3145736 | tf_op jit(solution)/shard_map/ppermute | solution.py:25
  44.6 15.0 %collective-permute-start.4 = (bf16[128,2048]{1,0:T(8,128)(2,1)}, bf16[128,2048]{1,0:T(8,128)(2,1)S(1)}, u32[]{:S(2)}, u32[]{:S(2)}) collective-permute-start(bf16[128,2048]{1,0:T(8,128)(2,1)} %refs_2_.1), channel_id=1, source_target_pairs={{0,8},{4,12},{8,0},{12,4},{16,24},{20,28},{24,16},{28,20},{1,9},{5... | collective-permute-start | bytes 1572872 | tf_op jit(solution)/shard_map/ppermute | solution.py:25
  45.4 56.4 %collective-permute-start.2 = (bf16[128,2048]{1,0:T(8,128)(2,1)}, bf16[128,2048]{1,0:T(8,128)(2,1)}, u32[]{:S(2)}, u32[]{:S(2)}) collective-permute-start(bf16[128,2048]{1,0:T(8,128)(2,1)} %copy-done.12), channel_id=1, source_target_pairs={{8,0},{12,4},{16,24},{20,28},{9,1},{13,5},{17,25},{21,29},{10,2},{... | collective-permute-start | bytes 1572872 | tf_op jit(solution)/shard_map/ppermute | solution.py:576
  46.6 55.1 %collective-permute-start.1 = (bf16[128,2048]{1,0:T(8,128)(2,1)}, bf16[128,2048]{1,0:T(8,128)(2,1)}, u32[]{:S(2)}, u32[]{:S(2)}) collective-permute-start(bf16[128,2048]{1,0:T(8,128)(2,1)} %refs_2_.1), channel_id=1, source_target_pairs={{8,16},{12,20},{16,8},{20,12},{9,17},{13,21},{17,9},{21,13},{10,18... | collective-permute-start | bytes 1572872 | tf_op jit(solution)/shard_map/ppermute | solution.py:575
  90.7 1.0 copy-start.11
  91.8 1.0 copy-start.13
  96.2 1.0 copy-start.3
  97.2 4.5 %collective-permute-start.5 = (bf16[128,384]{1,0:T(8,128)(2,1)}, bf16[128,384]{1,0:T(8,128)(2,1)S(1)}, u32[]{:S(2)}, u32[]{:S(2)}) collective-permute-start(bf16[128,384]{1,0:T(8,128)(2,1)} %get-tuple-element.50), channel_id=1, source_target_pairs={{0,1},{1,0},{2,3},{3,2},{4,5},{5,4},{6,7},{7,6},{8,9},{9,8},{10,11... | collective-permute-start | bytes 294920 | tf_op jit(solution)/shard_map/ppermute | solution.py:25
  97.2 5.9 %collective-permute-start.6 = (bf16[128,384]{1,0:T(8,128)(2,1)}, bf16[128,384]{1,0:T(8,128)(2,1)}, u32[]{:S(2)}, u32[]{:S(2)}) collective-permute-start(bf16[128,384]{1,0:T(8,128)(2,1)} %get-tuple-element.51), channel_id=1, source_target_pairs={{0,2},{1,3},{2,0},{3,1},{4,6},{5,7},{6,4},{7,5},{8,10},{9,11},{10,... | collective-permute-start | bytes 294920 | tf_op jit(solution)/shard_map/ppermute | solution.py:25
  98.7 5.7 %collective-permute-start.7 = (bf16[128,384]{1,0:T(8,128)(2,1)}, bf16[128,384]{1,0:T(8,128)(2,1)}, u32[]{:S(2)}, u32[]{:S(2)}) collective-permute-start(bf16[128,384]{1,0:T(8,128)(2,1)} %get-tuple-element.52), channel_id=1, source_target_pairs={{0,3},{1,2},{2,1},{3,0},{4,7},{5,6},{6,5},{7,4},{8,11},{9,10},{10,... | collective-permute-start | bytes 294920 | tf_op jit(solution)/shard_map/ppermute | solution.py:25
  104.4 1.2 copy-start.4
  109.0 0.6 copy-start.16
  109.6 4.0 %collective-permute-start.10 = (bf16[128,128]{1,0:T(8,128)(2,1)}, bf16[128,128]{1,0:T(8,128)(2,1)S(1)}, u32[]{:S(2)}, u32[]{:S(2)}) collective-permute-start(bf16[128,128]{1,0:T(8,128)(2,1)} %get-tuple-element.62), channel_id=1, source_target_pairs={{0,3},{1,2},{2,1},{3,0},{4,7},{5,6},{6,5},{7,4},{8,11},{9,10},{10,... | collective-permute-start | bytes 98312 | tf_op jit(solution)/shard_map/ppermute | solution.py:25
  110.9 2.8 %collective-permute-start.8 = (bf16[128,128]{1,0:T(8,128)(2,1)}, bf16[128,128]{1,0:T(8,128)(2,1)S(1)}, u32[]{:S(2)}, u32[]{:S(2)}) collective-permute-start(bf16[128,128]{1,0:T(8,128)(2,1)} %get-tuple-element.60), channel_id=1, source_target_pairs={{0,1},{1,0},{2,3},{3,2},{4,5},{5,4},{6,7},{7,6},{8,9},{9,8},{10,11... | collective-permute-start | bytes 98312 | tf_op jit(solution)/shard_map/ppermute | solution.py:25
  111.1 3.9 %collective-permute-start.9 = (bf16[128,128]{1,0:T(8,128)(2,1)S(1)}, bf16[128,128]{1,0:T(8,128)(2,1)S(1)}, u32[]{:S(2)}, u32[]{:S(2)}) collective-permute-start(bf16[128,128]{1,0:T(8,128)(2,1)S(1)} %get-tuple-element.61), channel_id=1, source_target_pairs={{0,2},{1,3},{2,0},{3,1},{4,6},{5,7},{6,4},{7,5},{8,10},{9,11},{10,... | collective-permute-start | bytes 98312 | tf_op jit(solution)/shard_map/ppermute | solution.py:25
  115.1 0.8 copy-start.17
  130.0 1.6 copy-start.5
  131.6 1.4 copy-start.8
  137.6 0.7 copy-start.14
  138.3 20.5 %copy-start.10 = (bf16[128,1024]{1,0:T(8,128)(2,1)S(1)}, bf16[128,1024]{1,0:T(8,128)(2,1)}, u32[]{:S(2)}) copy-start(bf16[128,1024]{1,0:T(8,128)(2,1)} %x.2) | copy-start | bytes 786436
  138.3 8.1 %collective-permute-start.12 = (bf16[160,768]{1,0:T(8,128)(2,1)S(1)}, bf16[160,768]{1,0:T(8,128)(2,1)S(1)}, u32[]{:S(2)}, u32[]{:S(2)}) collective-permute-start(bf16[160,768]{1,0:T(8,128)(2,1)S(1)} %get-tuple-element.76), channel_id=1, source_target_pairs={{0,2},{1,3},{2,0},{3,1},{4,6},{5,7},{6,4},{7,5},{8,10},{9,11},{10,... | collective-permute-start | bytes 737288 | tf_op jit(solution)/shard_map/ppermute | solution.py:25
  139.1 10.6 %collective-permute-start.14 = (bf16[160,768]{1,0:T(8,128)(2,1)S(1)}, bf16[160,768]{1,0:T(8,128)(2,1)S(1)}, u32[]{:S(2)}, u32[]{:S(2)}) collective-permute-start(bf16[160,768]{1,0:T(8,128)(2,1)S(1)} %get-tuple-element.77), channel_id=1, source_target_pairs={{0,4},{1,5},{2,6},{3,7},{4,0},{5,1},{6,2},{7,3},{8,12},{9,13},{10,... | collective-permute-start | bytes 737288 | tf_op jit(solution)/shard_map/ppermute | solution.py:25
  140.6 9.2 %collective-permute-start.16 = (bf16[160,768]{1,0:T(8,128)(2,1)S(1)}, bf16[160,768]{1,0:T(8,128)(2,1)S(1)}, u32[]{:S(2)}, u32[]{:S(2)}) collective-permute-start(bf16[160,768]{1,0:T(8,128)(2,1)S(1)} %get-tuple-element.78), channel_id=1, source_target_pairs={{0,6},{1,7},{2,4},{3,5},{4,2},{5,3},{6,0},{7,1},{8,14},{9,15},{10,... | collective-permute-start | bytes 737288 | tf_op jit(solution)/shard_map/ppermute | solution.py:25
  141.8 8.5 %collective-permute-start.11 = (bf16[160,768]{1,0:T(8,128)(2,1)S(1)}, bf16[160,768]{1,0:T(8,128)(2,1)S(1)}, u32[]{:S(2)}, u32[]{:S(2)}) collective-permute-start(bf16[160,768]{1,0:T(8,128)(2,1)S(1)} %get-tuple-element.75.g0), channel_id=1, source_target_pairs={{0,1},{1,0},{2,3},{3,2},{4,5},{5,4},{6,7},{7,6},{8,9},{9,8},{10,11... | collective-permute-start | bytes 737288 | tf_op jit(solution)/shard_map/ppermute | solution.py:25
  146.5 3.8 %collective-permute-start.13 = (bf16[160,768]{1,0:T(8,128)(2,1)S(1)}, bf16[160,768]{1,0:T(8,128)(2,1)S(1)}, u32[]{:S(2)}, u32[]{:S(2)}) collective-permute-start(bf16[160,768]{1,0:T(8,128)(2,1)S(1)} %collective-permute-done.12.g2), channel_id=1, source_target_pairs={{0,1},{1,0},{2,3},{3,2},{4,5},{5,4},{6,7},{7,6},{8,9},{9,8},{10,11... | collective-permute-start | bytes 737288 | tf_op jit(solution)/shard_map/ppermute | solution.py:25
  149.8 1.5 collective-permute-start.15
  149.8 1.9 %collective-permute-start.17 = (bf16[160,768]{1,0:T(8,128)(2,1)S(1)}, bf16[160,768]{1,0:T(8,128)(2,1)S(1)}, u32[]{:S(2)}, u32[]{:S(2)}) collective-permute-start(bf16[160,768]{1,0:T(8,128)(2,1)S(1)} %collective-permute-done.16.g6), channel_id=1, source_target_pairs={{0,1},{1,0},{2,3},{3,2},{4,5},{5,4},{6,7},{7,6},{8,9},{9,8},{10,11... | collective-permute-start | bytes 737288 | tf_op jit(solution)/shard_map/ppermute | solution.py:25
  154.4 11.7 %collective-permute-start.18 = (bf16[144,768]{1,0:T(8,128)(2,1)}, bf16[144,768]{1,0:T(8,128)(2,1)S(1)}, u32[]{:S(2)}, u32[]{:S(2)}) collective-permute-start(bf16[144,768]{1,0:T(8,128)(2,1)} %get-tuple-element.80), channel_id=1, source_target_pairs={{0,8},{1,9},{2,10},{3,11},{4,12},{5,13},{6,14},{7,15},{8,0},{9,1},... | collective-permute-start | bytes 663560 | tf_op jit(solution)/shard_map/ppermute | solution.py:25
  155.4 18.9 %collective-permute-start.19 = (bf16[144,768]{1,0:T(8,128)(2,1)}, bf16[144,768]{1,0:T(8,128)(2,1)S(1)}, u32[]{:S(2)}, u32[]{:S(2)}) collective-permute-start(bf16[144,768]{1,0:T(8,128)(2,1)} %get-tuple-element.81), channel_id=1, source_target_pairs={{0,16},{1,17},{2,18},{3,19},{4,20},{5,21},{6,22},{7,23},{8,24},{9,... | collective-permute-start | bytes 663560 | tf_op jit(solution)/shard_map/ppermute | solution.py:25
  157.8 16.5 %collective-permute-start.20 = (bf16[144,768]{1,0:T(8,128)(2,1)}, bf16[144,768]{1,0:T(8,128)(2,1)S(1)}, u32[]{:S(2)}, u32[]{:S(2)}) collective-permute-start(bf16[144,768]{1,0:T(8,128)(2,1)} %get-tuple-element.82), channel_id=1, source_target_pairs={{0,24},{1,25},{2,26},{3,27},{4,28},{5,29},{6,30},{7,31},{8,16},{9,... | collective-permute-start | bytes 663560 | tf_op jit(solution)/shard_map/ppermute | solution.py:25
  158.8 2.2 %copy-start.1 = (bf16[1024,2048]{1,0:T(8,128)(2,1)S(1)}, bf16[1024,2048]{1,0:T(8,128)(2,1)}, u32[]{:S(2)}) copy-start(bf16[1024,2048]{1,0:T(8,128)(2,1)} %w_one.3) | copy-start | bytes 12582916
  161.0 0.9 copy-start.15
  175.0 4.3 %collective-permute-start.21 = (bf16[32,768]{1,0:T(8,128)(2,1)S(1)}, bf16[32,768]{1,0:T(8,128)(2,1)S(1)}, u32[]{:S(2)}, u32[]{:S(2)}) collective-permute-start(bf16[32,768]{1,0:T(8,128)(2,1)S(1)} %get-tuple-element.84), channel_id=1, source_target_pairs={{0,2},{1,3},{2,0},{3,1},{4,6},{5,7},{6,4},{7,5},{8,10},{9,11},{10,... | collective-permute-start | bytes 147464 | tf_op jit(solution)/shard_map/ppermute | solution.py:25
  176.3 4.1 %collective-permute-start.22 = (bf16[32,768]{1,0:T(8,128)(2,1)S(1)}, bf16[32,768]{1,0:T(8,128)(2,1)S(1)}, u32[]{:S(2)}, u32[]{:S(2)}) collective-permute-start(bf16[32,768]{1,0:T(8,128)(2,1)S(1)} %get-tuple-element.85), channel_id=1, source_target_pairs={{0,4},{1,5},{2,6},{3,7},{4,0},{5,1},{6,2},{7,3},{8,12},{9,13},{10,... | collective-permute-start | bytes 147464 | tf_op jit(solution)/shard_map/ppermute | solution.py:25
  177.2 5.0 %collective-permute-start.23 = (bf16[32,768]{1,0:T(8,128)(2,1)S(1)}, bf16[32,768]{1,0:T(8,128)(2,1)S(1)}, u32[]{:S(2)}, u32[]{:S(2)}) collective-permute-start(bf16[32,768]{1,0:T(8,128)(2,1)S(1)} %get-tuple-element.86), channel_id=1, source_target_pairs={{0,6},{1,7},{2,4},{3,5},{4,2},{5,3},{6,0},{7,1},{8,14},{9,15},{10,... | collective-permute-start | bytes 147464 | tf_op jit(solution)/shard_map/ppermute | solution.py:25

commit v4 on v3

--- a/solution.py
+++ b/solution.py
@@ -38,7 +38,7 @@
     moved = sum(o.size * o.dtype.itemsize for o in operands) + sum(
         o.size * o.dtype.itemsize for o in outs
     )
-    vmem, other = pl.BlockSpec(memory_space=pltpu.VMEM), pl.BlockSpec(memory_space=pl.ANY)
+    vmem, other = pl.BlockSpec(memory_space=pltpu.VMEM), pl.BlockSpec(memory_space=pltpu.HBM)
     return pl.pallas_call(
         body,
         out_shape=tuple(outs),
@@ -571,10 +571,6 @@
     two = swap("rep", proj_weight, 4)
     one = swap("rep", proj_weight, 2)
     adj_other = swap("rep", adj_grad, 1)
-    proj_again, two, layer_later = lax.optimization_barrier((proj_weight, two, layer_input))
-    inner = lax.ppermute(proj_again, "rep", [(o * 2 + p, (3 - o) * 2 + p) for o in (1, 2) for p in (0, 1)])
-    ends = lax.ppermute(two, "rep", [(o * 2 + p, (o ^ 1) * 2 + p) for o in (1, 2) for p in (0, 1)])
-
     targets = adj_target[:, 0].reshape(reps, sections, quarter)
     frames = adj_frame.reshape(reps, sections, quarter)
     sec_targets = lax.dynamic_index_in_dim(targets, sec_here, 1, keepdims=False)
@@ -595,6 +591,12 @@
         [like((reps * 2 * capacity, 2 * quarter), BF), like((2, frame_rows, reps * capacity), BF)],
         name="routing",
     )
+    proj_again, two, one, adj_other, pack, pick = lax.optimization_barrier(
+        (proj_weight, two, one, adj_other, pack, pick)
+    )
+    inner = lax.ppermute(proj_again, "rep", [(o * 2 + p, (3 - o) * 2 + p) for o in (1, 2) for p in (0, 1)])
+    ends = lax.ppermute(two, "rep", [(o * 2 + p, (o ^ 1) * 2 + p) for o in (1, 2) for p in (0, 1)])
+
     tap_values = conv_taps.astype(F32)
     square = (frame_rows, feat)
     group = 8
@@ -604,7 +606,7 @@
     acts, sends = local_call(
         forward_kernel,
         ids,
-        (layer_later, w_pointwise1, tap_values, conv_scale.reshape(1, -1), conv_shift.reshape(1, -1)),
+        (layer_input, w_pointwise1, tap_values, conv_scale.reshape(1, -1), conv_shift.reshape(1, -1)),
         [like((3, *square), F32), like((group, feat, frame_rows), BF)],
         [
             pltpu.VMEM((3, *square), F32),
@@ -618,15 +620,6 @@
         name="forward",
         leave=(0, 1),
     )
-    early = lax.all_to_all(
-        sends,
-        BOTH,
-        split_axis=0,
-        concat_axis=0,
-        axis_index_groups=[[g * group + m for m in range(group)] for g in range(reps * sections // group)],
-        tiled=True,
-    )
-
     rows = 2 * quarter
 
     def products(name, *lot):
@@ -646,7 +639,15 @@
     lot_one = products("products", proj_weight, one, two)
     inner, ends, lot_one = lax.optimization_barrier((inner, ends, lot_one))
     lot_two = products("last_products", inner, ends)
-    lot_two, early = lax.optimization_barrier((lot_two, early))
+    lot_two[0], sends = lax.optimization_barrier((lot_two[0], sends))
+    early = lax.all_to_all(
+        sends,
+        BOTH,
+        split_axis=0,
+        concat_axis=0,
+        axis_index_groups=[[g * group + m for m in range(group)] for g in range(reps * sections // group)],
+        tiled=True,
+    )
     lane = outer * piece
     (packed,) = local_call(
         packing_kernel,
@@ -658,6 +659,7 @@
     )
     outgoing = packed.reshape(reps, 2 * capacity, lane)
     incoming = lax.all_to_all(outgoing, "rep", split_axis=0, concat_axis=0, tiled=True)
+    incoming, early = lax.optimization_barrier((incoming, early))
     late = like((frame_rows + 32, 3 * feat // 4), BF)
     lot = like((frame_rows + 16, 3 * feat // 4), BF)
     grad_out, grad_mixed, p0, p2, p4, p6 = local_call(

time: 186 us -> 148 us (0.80)
  waiting for transfers between devices: 90.3 us -> 46.6 us
  blocking collectives: 12.9 us -> 44 us
  local copies, waits for them, and re-layouts: 24 us -> 7.44 us
  starting transfers between devices: 29.6 us -> 25.1 us
  Pallas kernels: 24.4 us -> 21.3 us
    ppermute x22, waiting for transfers between devices: 90.3 us -> 46.1 us  [swap(): return lax.ppermute(values, axis, xor_perm(size_of(axis), mask))]
    all_to_all x0 -> x1, blocking collectives: none -> 30.1 us  [line_shards(): lax.all_to_all(sends, BOTH, split_axis=0, concat_axis=0, axis_index_group...]
    unnamed x46 -> x20, local copies, waits for them, and re-layouts: 21 us -> 5.59 us
    all_to_all x1 -> x0, starting transfers between devices: 3.91 us -> none  [line_shards(): lax.all_to_all(sends, BOTH, split_axis=0, concat_axis=0, axis_index_group...]
    pallas_call x10, Pallas kernels: 24.4 us -> 21.3 us  [local_call(): pl.pallas_call(body, out_shape=tuple(outs), in_specs=[pl.BlockSpec(memory...]
  transfers between devices with their start and end apart: 25 -> 24, of which waited for: 14 -> 13; matrix products, arithmetic and copies ran while one was open for 3% -> 3% of each run, Pallas kernels for 6% -> 7%
where the time goes in v4:
time: 148 us; the launch traced here: 147 us
  waiting for transfers between devices  46.6 us (31%)
  blocking collectives  44 us (30%)
  starting transfers between devices  25.1 us (17%)
  Pallas kernels  21.3 us (14%)
  local copies, waits for them, and re-layouts  7.44 us (5%)
    ppermute x22, waiting for transfers between devices, swap(): return lax.ppermute(values, axis, xor_perm(size_of(axis), mask))  46.1 us
    all_to_all x1, blocking collectives, line_shards(): lax.all_to_all(sends, BOTH, split_axis=0, concat_axis=0, axis_index_group...  30.1 us
    ppermute x22, starting transfers between devices, swap(): return lax.ppermute(values, axis, xor_perm(size_of(axis), mask))  23.1 us
    pallas_call x10, Pallas kernels, local_call(): pl.pallas_call(body, out_shape=tuple(outs), in_specs=[pl.BlockSpec(memory...  21.3 us
    all_to_all x1, blocking collectives, line_shards(): lax.all_to_all(outgoing, 'rep', split_axis=0, concat_axis=0, tiled=True)  13.9 us
    unnamed x20, local copies, waits for them, and re-layouts  5.59 us
  transfers between devices with their start and end apart: 24, of which 13 were waited for; matrix products, arithmetic and copies ran while one was open for 3% of the time, Pallas kernels for 7%

profile of v4, /device:TPU:0, one launch (start us, length us, event | category | flops | bytes accessed | tf_op | source)
XLA Modules:
  0.0 146.7 jit_solution(14686360371439281270)
XLA Ops:
  0.6 3.0 %collective-permute-start.2 = (bf16[256,2048]{1,0:T(8,128)(2,1)}, bf16[256,2048]{1,0:T(8,128)(2,1)S(1)}, u32[]{:S(2)}, u32[]{:S(2)}) collective-permute-start(bf16[256,2048]{1,0:T(8,128)(2,1)} %refs_0_.3), channel_id=1, source_target_pairs={{0,4},{4,0},{8,12},{12,8},{16,20},{20,16},{24,28},{28,24},{1,5},{5... | collective-permute-start | bytes 3145736 | tf_op jit(solution)/shard_map/ppermute | solution.py:25
  3.7 1.6 %collective-permute-start.1 = (bf16[128,2048]{1,0:T(8,128)(2,1)}, bf16[128,2048]{1,0:T(8,128)(2,1)S(1)}, u32[]{:S(2)}, u32[]{:S(2)}) collective-permute-start(bf16[128,2048]{1,0:T(8,128)(2,1)} %refs_2_.1), channel_id=1, source_target_pairs={{0,8},{4,12},{8,0},{12,4},{16,24},{20,28},{24,16},{28,20},{1,9},{5... | collective-permute-start | bytes 1572872 | tf_op jit(solution)/shard_map/ppermute | solution.py:25
  5.2 2.6 %collective-permute-start = (bf16[128,2048]{1,0:T(8,128)(2,1)}, bf16[128,2048]{1,0:T(8,128)(2,1)S(1)}, u32[]{:S(2)}, u32[]{:S(2)}) collective-permute-start(bf16[128,2048]{1,0:T(8,128)(2,1)} %refs_2_.1), channel_id=1, source_target_pairs={{0,16},{4,20},{8,24},{12,28},{16,0},{20,4},{24,8},{28,12},{1,17},{... | collective-permute-start | bytes 1572872 | tf_op jit(solution)/shard_map/ppermute | solution.py:25
  7.8 0.5 broadcast.10
  8.3 1.4 reduce.7
  9.7 0.1 reshape_squeeze.3
  9.8 0.8 reshape.33
  10.6 0.1 reshape.34.frames
  10.7 0.1 reshape.32.targets
  10.7 0.7 concatenate.3.ids
  11.5 1.0 routing.1
  12.5 15.9 %collective-permute-done.1.refs_3_ = bf16[128,2048]{1,0:T(8,128)(2,1)S(1)} collective-permute-done((bf16[128,2048]{1,0:T(8,128)(2,1)}, bf16[128,2048]{1,0:T(8,128)(2,1)S(1)}, u32[]{:S(2)}, u32[]{:S(2)}) %collective-permute-start.1) | collective-permute-done | bytes 524320 | tf_op jit(solution)/shard_map/ppermute | solution.py:25
  28.4 2.4 %collective-permute-done.refs_4_ = bf16[128,2048]{1,0:T(8,128)(2,1)S(1)} collective-permute-done((bf16[128,2048]{1,0:T(8,128)(2,1)}, bf16[128,2048]{1,0:T(8,128)(2,1)S(1)}, u32[]{:S(2)}, u32[]{:S(2)}) %collective-permute-start) | collective-permute-done | bytes 524320 | tf_op jit(solution)/shard_map/ppermute | solution.py:25
  30.8 0.0 collective-permute-done.2.refs_1_
  30.8 0.7 collective-permute-start.3
  31.5 1.3 collective-permute-start.4
  32.8 0.0 copy-start.2
  32.8 1.2 copy-done.2
  34.0 1.0 copy-done.5
  35.0 2.7 %products.1 = (f32[128,384]{1,0:T(8,128)S(1)}, bf16[128,384]{1,0:T(8,128)(2,1)S(1)}, bf16[128,384]{1,0:T(8,128)(2,1)S(1)}, bf16[128,384]{1,0:T(8,128)(2,1)S(1)}) custom-call(s32[9]{0:T(128)S(1)} %concatenate.3.ids, bf16[256,2048]{1,0:T(8,128)(2,1)S(1)} %copy-done.2, bf16[256,2048]{1,0:T(8,128)(2,1)S(1)} %collective-permute-done.2.refs_1_, ...), custom_call_target="tpu_custom_call" | custom-call | flops 805306368 | bytes 4161536 | tf_op jit(solution)/shard_map/products/pallas_call | solution.py:42
  37.7 0.0 copy-start.4
  37.8 0.0 copy-start.6
  37.8 0.0 copy-start.7
  37.8 0.1 collective-permute-start.5
  37.9 1.6 %collective-permute-start.6 = (bf16[128,384]{1,0:T(8,128)(2,1)S(1)}, bf16[128,384]{1,0:T(8,128)(2,1)S(1)}, u32[]{:S(2)}, u32[]{:S(2)}) collective-permute-start(bf16[128,384]{1,0:T(8,128)(2,1)S(1)} %get-tuple-element.57), channel_id=1, source_target_pairs={{0,2},{1,3},{2,0},{3,1},{4,6},{5,7},{6,4},{7,5},{8,10},{9,11},{10,... | collective-permute-start | bytes 294920 | tf_op jit(solution)/shard_map/ppermute | solution.py:25
  39.4 0.3 collective-permute-start.7
  39.7 3.8 %collective-permute-done.6.r2 = bf16[128,384]{1,0:T(8,128)(2,1)S(1)} collective-permute-done((bf16[128,384]{1,0:T(8,128)(2,1)S(1)}, bf16[128,384]{1,0:T(8,128)(2,1)S(1)}, u32[]{:S(2)}, u32[]{:S(2)}) %collective-permute-start.6) | collective-permute-done | bytes 98336 | tf_op jit(solution)/shard_map/ppermute | solution.py:25
  43.5 1.2 collective-permute-done.7.r3
  44.7 0.5 collective-permute-done.4.refs_3_
  45.2 2.0 %last_products.1 = (f32[128,128]{1,0:T(8,128)S(1)}, bf16[128,128]{1,0:T(8,128)(2,1)S(1)}, bf16[128,128]{1,0:T(8,128)(2,1)S(1)}, bf16[128,128]{1,0:T(8,128)(2,1)S(1)}) custom-call(s32[9]{0:T(128)S(1)} %concatenate.3.ids, bf16[256,2048]{1,0:T(8,128)(2,1)S(1)} %copy-done.2, bf16[256,2048]{1,0:T(8,128)(2,1)S(1)} %collective-permute-done.2.refs_1_, ...), custom_call_target="tpu_custom_call" | custom-call | flops 268435456 | bytes 3309568 | tf_op jit(solution)/shard_map/last_products/pallas_call | solution.py:42
  47.3 0.1 collective-permute-start.8
  47.4 1.5 %collective-permute-start.9 = (bf16[128,128]{1,0:T(8,128)(2,1)S(1)}, bf16[128,128]{1,0:T(8,128)(2,1)S(1)}, u32[]{:S(2)}, u32[]{:S(2)}) collective-permute-start(bf16[128,128]{1,0:T(8,128)(2,1)S(1)} %get-tuple-element.69), channel_id=1, source_target_pairs={{0,2},{1,3},{2,0},{3,1},{4,6},{5,7},{6,4},{7,5},{8,10},{9,11},{10,... | collective-permute-start | bytes 98312 | tf_op jit(solution)/shard_map/ppermute | solution.py:25
  48.9 0.3 collective-permute-start.10
  49.2 3.4 %forward.1 = (f32[3,128,1024]{2,1,0:T(8,128)S(1)}, bf16[8,1024,128]{2,1,0:T(8,128)(2,1)S(1)}) custom-call(s32[9]{0:T(128)S(1)} %concatenate.3.ids, bf16[128,1024]{1,0:T(8,128)(2,1)S(1)} %copy-done.4, bf16[1024,2048]{1,0:T(8,128)(2,1)S(1)} %copy-done, f32[9,1024]{1,0:T(8,128)S(1)} %convert_element_type.3.taps, f32[1,1024]{1,0:T(1,128)S(1)} %bitcast.20, ...), custom_call_target="tpu_custom_call" | custom-call | flops 536870912 | bytes 8171520 | tf_op jit(solution)/shard_map/forward/pallas_call | solution.py:42
  52.6 0.0 collective-permute-done.8.l1
  52.6 0.8 packing.1
  53.5 13.9 %all_to_all.10.incoming = bf16[8,32,512]{2,1,0:T(8,128)(2,1)S(1)} all-to-all(bf16[8,32,512]{2,1,0:T(8,128)(2,1)S(1)} %bitcast.19), channel_id=1, replica_groups=mesh['rep'=8,'section'=4] {'rep'}, dimensions={0} | all-to-all | bytes 524288 | tf_op jit(solution)/shard_map/all_to_all | solution.py:661
  67.3 30.1 %all_to_all.11.early = bf16[8,1024,128]{2,1,0:T(8,128)(2,1)S(1)} all-to-all(bf16[8,1024,128]{2,1,0:T(8,128)(2,1)S(1)} %get-tuple-element.72), channel_id=1, replica_groups={{0,1,2,3,4,5,6,7},{8,9,10,11,12,13,14,15},{16,17,18,19,20,21,22,23},{24..., dimensions={0} | all-to-all | bytes 4194304 | tf_op jit(solution)/shard_map/all_to_all | solution.py:643
  97.5 4.6 %module.1 = (bf16[128,1024]{1,0:T(8,128)(2,1)S(1)}, bf16[128,2048]{1,0:T(8,128)(2,1)S(1)}, bf16[160,768]{1,0:T(8,128)(2,1)S(1)}, bf16[160,768]{1,0:T(8,128)(2,1)...) custom-call(s32[9]{0:T(128)S(1)} %concatenate.3.ids, bf16[8,32,512]{2,1,0:T(8,128)(2,1)S(1)} %all_to_all.10.incoming, ...), custom_call_target="tpu_custom_call" | custom-call | flops 276299776 | bytes 5804032 | tf_op jit(solution)/shard_map/module/pallas_call | solution.py:42
  102.1 0.6 collective-permute-start.12
  102.7 0.6 collective-permute-start.14
  103.3 2.4 %collective-permute-start.16 = (bf16[160,768]{1,0:T(8,128)(2,1)S(1)}, bf16[160,768]{1,0:T(8,128)(2,1)S(1)}, u32[]{:S(2)}, u32[]{:S(2)}) collective-permute-start(bf16[160,768]{1,0:T(8,128)(2,1)S(1)} %get-tuple-element.82), channel_id=1, source_target_pairs={{0,6},{1,7},{2,4},{3,5},{4,2},{5,3},{6,0},{7,1},{8,14},{9,15},{10,... | collective-permute-start | bytes 737288 | tf_op jit(solution)/shard_map/ppermute | solution.py:25
  105.6 5.4 %collective-permute-done.12.g2 = bf16[160,768]{1,0:T(8,128)(2,1)S(1)} collective-permute-done((bf16[160,768]{1,0:T(8,128)(2,1)S(1)}, bf16[160,768]{1,0:T(8,128)(2,1)S(1)}, u32[]{:S(2)}, u32[]{:S(2)}) %collective-permute-start.12) | collective-permute-done | bytes 245792 | tf_op jit(solution)/shard_map/ppermute | solution.py:25
  111.0 4.4 %collective-permute-done.14.g4 = bf16[160,768]{1,0:T(8,128)(2,1)S(1)} collective-permute-done((bf16[160,768]{1,0:T(8,128)(2,1)S(1)}, bf16[160,768]{1,0:T(8,128)(2,1)S(1)}, u32[]{:S(2)}, u32[]{:S(2)}) %collective-permute-start.14) | collective-permute-done | bytes 245792 | tf_op jit(solution)/shard_map/ppermute | solution.py:25
  115.5 0.5 collective-permute-start.17
  116.0 1.0 collective-permute-done.15.g5
  117.0 0.4 collective-permute-done.17.g7
  117.3 1.9 %weights.1 = (f32[144,768]{1,0:T(8,128)S(1)}, bf16[144,768]{1,0:T(8,128)(2,1)S(1)}, bf16[144,768]{1,0:T(8,128)(2,1)S(1)}, bf16[144,768]{1,0:T(8,128)(2,1)S(1)}) custom-call(s32[9]{0:T(128)S(1)} %concatenate.3.ids, bf16[8,1024,128]{2,1,0:T(8,128)(2,1)S(1)} %all_to_all.11.early, bf16[160,768]{1,0:T(8,128)(2,1)S(1)} %get-tuple-element.79.g0, ...), custom_call_target="tpu_custom_call" | custom-call | flops 805306368 | bytes 5169152 | tf_op jit(solution)/shard_map/weights/pallas_call | solution.py:42
  119.2 0.3 collective-permute-start.18
  119.5 1.8 %collective-permute-start.19 = (bf16[144,768]{1,0:T(8,128)(2,1)S(1)}, bf16[144,768]{1,0:T(8,128)(2,1)S(1)}, u32[]{:S(2)}, u32[]{:S(2)}) collective-permute-start(bf16[144,768]{1,0:T(8,128)(2,1)S(1)} %get-tuple-element.85), channel_id=1, source_target_pairs={{0,16},{1,17},{2,18},{3,19},{4,20},{5,21},{6,22},{7,23},{8,24},{9,... | collective-permute-start | bytes 663560 | tf_op jit(solution)/shard_map/ppermute | solution.py:25
  121.3 2.4 %collective-permute-start.20 = (bf16[144,768]{1,0:T(8,128)(2,1)S(1)}, bf16[144,768]{1,0:T(8,128)(2,1)S(1)}, u32[]{:S(2)}, u32[]{:S(2)}) collective-permute-start(bf16[144,768]{1,0:T(8,128)(2,1)S(1)} %get-tuple-element.86), channel_id=1, source_target_pairs={{0,24},{1,25},{2,26},{3,27},{4,28},{5,29},{6,30},{7,31},{8,16},{9,... | collective-permute-start | bytes 663560 | tf_op jit(solution)/shard_map/ppermute | solution.py:25
  123.7 2.2 %copy-done.1 = bf16[1024,2048]{1,0:T(8,128)(2,1)S(1)} copy-done((bf16[1024,2048]{1,0:T(8,128)(2,1)S(1)}, bf16[1024,2048]{1,0:T(8,128)(2,1)}, u32[]{:S(2)}) %copy-start.1) | copy-done | bytes 4194328
  125.9 2.9 %tail.1 = bf16[128,1024]{1,0:T(8,128)(2,1)} custom-call(s32[9]{0:T(128)S(1)} %concatenate.3.ids, bf16[128,1024]{1,0:T(8,128)(2,1)S(1)} %copy-done.4, bf16[128,2048]{1,0:T(8,128)(2,1)S(1)} %get-tuple-element.76.grad_mixed, bf16[1024,2048]{1,0:T(8,128)(2,1)S(1)} %copy-done.1, bf16[128,1024]{1,0:T(8,128)(2,1)S(1)} %get-tuple-element.77.grad_out), custom_call_target="tpu_custom_call" | custom-call | flops 536870912 | bytes 5505024 | tf_op jit(solution)/shard_map/tail/pallas_call | solution.py:42
  128.8 1.5 %collective-permute-done.18.r1 = bf16[144,768]{1,0:T(8,128)(2,1)S(1)} collective-permute-done((bf16[144,768]{1,0:T(8,128)(2,1)S(1)}, bf16[144,768]{1,0:T(8,128)(2,1)S(1)}, u32[]{:S(2)}, u32[]{:S(2)}) %collective-permute-start.18) | collective-permute-done | bytes 221216 | tf_op jit(solution)/shard_map/ppermute | solution.py:25
  130.3 7.9 %collective-permute-done.19.r2 = bf16[144,768]{1,0:T(8,128)(2,1)S(1)} collective-permute-done((bf16[144,768]{1,0:T(8,128)(2,1)S(1)}, bf16[144,768]{1,0:T(8,128)(2,1)S(1)}, u32[]{:S(2)}, u32[]{:S(2)}) %collective-permute-start.19) | collective-permute-done | bytes 221216 | tf_op jit(solution)/shard_map/ppermute | solution.py:25
  138.2 0.7 sums.1
  138.9 0.8 collective-permute-start.21
  139.7 0.7 collective-permute-start.22
  140.4 2.1 %collective-permute-start.23 = (bf16[32,768]{1,0:T(8,128)(2,1)S(1)}, bf16[32,768]{1,0:T(8,128)(2,1)S(1)}, u32[]{:S(2)}, u32[]{:S(2)}) collective-permute-start(bf16[32,768]{1,0:T(8,128)(2,1)S(1)} %get-tuple-element.90), channel_id=1, source_target_pairs={{0,6},{1,7},{2,4},{3,5},{4,2},{5,3},{6,0},{7,1},{8,14},{9,15},{10,... | collective-permute-start | bytes 147464 | tf_op jit(solution)/shard_map/ppermute | solution.py:25
  142.5 0.1 reshape.38
  142.6 0.6 copy.23
  143.2 0.6 collective-permute-done.22.r2
  143.8 1.6 %collective-permute-done.23.r3 = bf16[32,768]{1,0:T(8,128)(2,1)S(1)} collective-permute-done((bf16[32,768]{1,0:T(8,128)(2,1)S(1)}, bf16[32,768]{1,0:T(8,128)(2,1)S(1)}, u32[]{:S(2)}, u32[]{:S(2)}) %collective-permute-start.23) | collective-permute-done | bytes 49184 | tf_op jit(solution)/shard_map/ppermute | solution.py:25
  145.4 1.3 assembly.1
  (26 shorter events, 0.1 us)
Async XLA Ops:
  0.6 39.1 %copy-start.8 = (bf16[9,1024]{1,0:T(8,128)(2,1)S(1)}, bf16[9,1024]{1,0:T(8,128)(2,1)}, u32[]{:S(2)}) copy-start(bf16[9,1024]{1,0:T(8,128)(2,1)} %param.14) | copy-start | bytes 55300
  0.6 30.1 %collective-permute-start.2 = (bf16[256,2048]{1,0:T(8,128)(2,1)}, bf16[256,2048]{1,0:T(8,128)(2,1)S(1)}, u32[]{:S(2)}, u32[]{:S(2)}) collective-permute-start(bf16[256,2048]{1,0:T(8,128)(2,1)} %refs_0_.3), channel_id=1, source_target_pairs={{0,4},{4,0},{8,12},{12,8},{16,20},{20,16},{24,28},{28,24},{1,5},{5... | collective-permute-start | bytes 3145736 | tf_op jit(solution)/shard_map/ppermute | solution.py:25
  3.7 24.7 %collective-permute-start.1 = (bf16[128,2048]{1,0:T(8,128)(2,1)}, bf16[128,2048]{1,0:T(8,128)(2,1)S(1)}, u32[]{:S(2)}, u32[]{:S(2)}) collective-permute-start(bf16[128,2048]{1,0:T(8,128)(2,1)} %refs_2_.1), channel_id=1, source_target_pairs={{0,8},{4,12},{8,0},{12,4},{16,24},{20,28},{24,16},{28,20},{1,9},{5... | collective-permute-start | bytes 1572872 | tf_op jit(solution)/shard_map/ppermute | solution.py:25
  5.2 25.5 %collective-permute-start = (bf16[128,2048]{1,0:T(8,128)(2,1)}, bf16[128,2048]{1,0:T(8,128)(2,1)S(1)}, u32[]{:S(2)}, u32[]{:S(2)}) collective-permute-start(bf16[128,2048]{1,0:T(8,128)(2,1)} %refs_2_.1), channel_id=1, source_target_pairs={{0,16},{4,20},{8,24},{12,28},{16,0},{20,4},{24,8},{28,12},{1,17},{... | collective-permute-start | bytes 1572872 | tf_op jit(solution)/shard_map/ppermute | solution.py:25
  30.8 14.0 %collective-permute-start.3 = (bf16[128,2048]{1,0:T(8,128)(2,1)}, bf16[128,2048]{1,0:T(8,128)(2,1)S(1)}, u32[]{:S(2)}, u32[]{:S(2)}) collective-permute-start(bf16[128,2048]{1,0:T(8,128)(2,1)} %refs_2_.1), channel_id=1, source_target_pairs={{8,16},{12,20},{16,8},{20,12},{9,17},{13,21},{17,9},{21,13},{10,18... | collective-permute-start | bytes 1572872 | tf_op jit(solution)/shard_map/ppermute | solution.py:597
  31.5 13.8 %collective-permute-start.4 = (bf16[128,2048]{1,0:T(8,128)(2,1)S(1)}, bf16[128,2048]{1,0:T(8,128)(2,1)S(1)}, u32[]{:S(2)}, u32[]{:S(2)}) collective-permute-start(bf16[128,2048]{1,0:T(8,128)(2,1)S(1)} %collective-permute-done.refs_4_), channel_id=1, source_target_pairs={{8,0},{12,4},{16,24},{20,28},{9,1},{13,5},{17,25},{21,29},{10,2},{... | collective-permute-start | bytes 1572872 | tf_op jit(solution)/shard_map/ppermute | solution.py:598
  32.8 1.2 copy-start.2
  34.0 1.0 copy-start.5
  35.0 14.2 %copy-start = (bf16[1024,2048]{1,0:T(8,128)(2,1)S(1)}, bf16[1024,2048]{1,0:T(8,128)(2,1)}, u32[]{:S(2)}) copy-start(bf16[1024,2048]{1,0:T(8,128)(2,1)} %w_one.3) | copy-start | bytes 12582916
  37.7 11.5 %copy-start.4 = (bf16[128,1024]{1,0:T(8,128)(2,1)S(1)}, bf16[128,1024]{1,0:T(8,128)(2,1)}, u32[]{:S(2)}) copy-start(bf16[128,1024]{1,0:T(8,128)(2,1)} %x.3) | copy-start | bytes 786436
  37.8 11.4 %copy-start.6 = (f32[1024]{0:T(1024)S(1)}, f32[1024]{0:T(1024)}, u32[]{:S(2)}) copy-start(f32[1024]{0:T(1024)} %param.15) | copy-start | bytes 12292
  37.8 11.4 %copy-start.7 = (f32[1024]{0:T(1024)S(1)}, f32[1024]{0:T(1024)}, u32[]{:S(2)}) copy-start(f32[1024]{0:T(1024)} %param.16) | copy-start | bytes 12292
  37.8 2.0 %collective-permute-start.5 = (bf16[128,384]{1,0:T(8,128)(2,1)S(1)}, bf16[128,384]{1,0:T(8,128)(2,1)S(1)}, u32[]{:S(2)}, u32[]{:S(2)}) collective-permute-start(bf16[128,384]{1,0:T(8,128)(2,1)S(1)} %get-tuple-element.56), channel_id=1, source_target_pairs={{0,1},{1,0},{2,3},{3,2},{4,5},{5,4},{6,7},{7,6},{8,9},{9,8},{10,11... | collective-permute-start | bytes 294920 | tf_op jit(solution)/shard_map/ppermute | solution.py:25
  37.9 5.7 %collective-permute-start.6 = (bf16[128,384]{1,0:T(8,128)(2,1)S(1)}, bf16[128,384]{1,0:T(8,128)(2,1)S(1)}, u32[]{:S(2)}, u32[]{:S(2)}) collective-permute-start(bf16[128,384]{1,0:T(8,128)(2,1)S(1)} %get-tuple-element.57), channel_id=1, source_target_pairs={{0,2},{1,3},{2,0},{3,1},{4,6},{5,7},{6,4},{7,5},{8,10},{9,11},{10,... | collective-permute-start | bytes 294920 | tf_op jit(solution)/shard_map/ppermute | solution.py:25
  39.4 5.3 %collective-permute-start.7 = (bf16[128,384]{1,0:T(8,128)(2,1)S(1)}, bf16[128,384]{1,0:T(8,128)(2,1)S(1)}, u32[]{:S(2)}, u32[]{:S(2)}) collective-permute-start(bf16[128,384]{1,0:T(8,128)(2,1)S(1)} %get-tuple-element.58), channel_id=1, source_target_pairs={{0,3},{1,2},{2,1},{3,0},{4,7},{5,6},{6,5},{7,4},{8,11},{9,10},{10,... | collective-permute-start | bytes 294920 | tf_op jit(solution)/shard_map/ppermute | solution.py:25
  47.3 5.3 %collective-permute-start.8 = (bf16[128,128]{1,0:T(8,128)(2,1)S(1)}, bf16[128,128]{1,0:T(8,128)(2,1)S(1)}, u32[]{:S(2)}, u32[]{:S(2)}) collective-permute-start(bf16[128,128]{1,0:T(8,128)(2,1)S(1)} %get-tuple-element.68), channel_id=1, source_target_pairs={{0,1},{1,0},{2,3},{3,2},{4,5},{5,4},{6,7},{7,6},{8,9},{9,8},{10,11... | collective-permute-start | bytes 98312 | tf_op jit(solution)/shard_map/ppermute | solution.py:25
  47.4 5.2 %collective-permute-start.9 = (bf16[128,128]{1,0:T(8,128)(2,1)S(1)}, bf16[128,128]{1,0:T(8,128)(2,1)S(1)}, u32[]{:S(2)}, u32[]{:S(2)}) collective-permute-start(bf16[128,128]{1,0:T(8,128)(2,1)S(1)} %get-tuple-element.69), channel_id=1, source_target_pairs={{0,2},{1,3},{2,0},{3,1},{4,6},{5,7},{6,4},{7,5},{8,10},{9,11},{10,... | collective-permute-start | bytes 98312 | tf_op jit(solution)/shard_map/ppermute | solution.py:25
  48.9 3.7 %collective-permute-start.10 = (bf16[128,128]{1,0:T(8,128)(2,1)S(1)}, bf16[128,128]{1,0:T(8,128)(2,1)S(1)}, u32[]{:S(2)}, u32[]{:S(2)}) collective-permute-start(bf16[128,128]{1,0:T(8,128)(2,1)S(1)} %get-tuple-element.70), channel_id=1, source_target_pairs={{0,3},{1,2},{2,1},{3,0},{4,7},{5,6},{6,5},{7,4},{8,11},{9,10},{10,... | collective-permute-start | bytes 98312 | tf_op jit(solution)/shard_map/ppermute | solution.py:25
  67.3 30.1 %copy-start.3 = (bf16[1024,1024]{1,0:T(8,128)(2,1)S(1)}, bf16[1024,1024]{1,0:T(8,128)(2,1)}, u32[]{:S(2)}) copy-start(bf16[1024,1024]{1,0:T(8,128)(2,1)} %w_two.1) | copy-start | bytes 6291460
  102.1 9.0 %collective-permute-start.12 = (bf16[160,768]{1,0:T(8,128)(2,1)S(1)}, bf16[160,768]{1,0:T(8,128)(2,1)S(1)}, u32[]{:S(2)}, u32[]{:S(2)}) collective-permute-start(bf16[160,768]{1,0:T(8,128)(2,1)S(1)} %get-tuple-element.80), channel_id=1, source_target_pairs={{0,2},{1,3},{2,0},{3,1},{4,6},{5,7},{6,4},{7,5},{8,10},{9,11},{10,... | collective-permute-start | bytes 737288 | tf_op jit(solution)/shard_map/ppermute | solution.py:25
  102.7 12.8 %collective-permute-start.14 = (bf16[160,768]{1,0:T(8,128)(2,1)S(1)}, bf16[160,768]{1,0:T(8,128)(2,1)S(1)}, u32[]{:S(2)}, u32[]{:S(2)}) collective-permute-start(bf16[160,768]{1,0:T(8,128)(2,1)S(1)} %get-tuple-element.81), channel_id=1, source_target_pairs={{0,4},{1,5},{2,6},{3,7},{4,0},{5,1},{6,2},{7,3},{8,12},{9,13},{10,... | collective-permute-start | bytes 737288 | tf_op jit(solution)/shard_map/ppermute | solution.py:25
  103.3 12.2 %collective-permute-start.16 = (bf16[160,768]{1,0:T(8,128)(2,1)S(1)}, bf16[160,768]{1,0:T(8,128)(2,1)S(1)}, u32[]{:S(2)}, u32[]{:S(2)}) collective-permute-start(bf16[160,768]{1,0:T(8,128)(2,1)S(1)} %get-tuple-element.82), channel_id=1, source_target_pairs={{0,6},{1,7},{2,4},{3,5},{4,2},{5,3},{6,0},{7,1},{8,14},{9,15},{10,... | collective-permute-start | bytes 737288 | tf_op jit(solution)/shard_map/ppermute | solution.py:25
  105.6 10.4 %collective-permute-start.11 = (bf16[160,768]{1,0:T(8,128)(2,1)S(1)}, bf16[160,768]{1,0:T(8,128)(2,1)S(1)}, u32[]{:S(2)}, u32[]{:S(2)}) collective-permute-start(bf16[160,768]{1,0:T(8,128)(2,1)S(1)} %get-tuple-element.79.g0), channel_id=1, source_target_pairs={{0,1},{1,0},{2,3},{3,2},{4,5},{5,4},{6,7},{7,6},{8,9},{9,8},{10,11... | collective-permute-start | bytes 737288 | tf_op jit(solution)/shard_map/ppermute | solution.py:25
  111.0 5.0 %collective-permute-start.13 = (bf16[160,768]{1,0:T(8,128)(2,1)S(1)}, bf16[160,768]{1,0:T(8,128)(2,1)S(1)}, u32[]{:S(2)}, u32[]{:S(2)}) collective-permute-start(bf16[160,768]{1,0:T(8,128)(2,1)S(1)} %collective-permute-done.12.g2), channel_id=1, source_target_pairs={{0,1},{1,0},{2,3},{3,2},{4,5},{5,4},{6,7},{7,6},{8,9},{9,8},{10,11... | collective-permute-start | bytes 737288 | tf_op jit(solution)/shard_map/ppermute | solution.py:25
  115.5 1.5 %collective-permute-start.15 = (bf16[160,768]{1,0:T(8,128)(2,1)S(1)}, bf16[160,768]{1,0:T(8,128)(2,1)S(1)}, u32[]{:S(2)}, u32[]{:S(2)}) collective-permute-start(bf16[160,768]{1,0:T(8,128)(2,1)S(1)} %collective-permute-done.14.g4), channel_id=1, source_target_pairs={{0,1},{1,0},{2,3},{3,2},{4,5},{5,4},{6,7},{7,6},{8,9},{9,8},{10,11... | collective-permute-start | bytes 737288 | tf_op jit(solution)/shard_map/ppermute | solution.py:25
  115.5 1.9 %collective-permute-start.17 = (bf16[160,768]{1,0:T(8,128)(2,1)S(1)}, bf16[160,768]{1,0:T(8,128)(2,1)S(1)}, u32[]{:S(2)}, u32[]{:S(2)}) collective-permute-start(bf16[160,768]{1,0:T(8,128)(2,1)S(1)} %collective-permute-done.16.g6), channel_id=1, source_target_pairs={{0,1},{1,0},{2,3},{3,2},{4,5},{5,4},{6,7},{7,6},{8,9},{9,8},{10,11... | collective-permute-start | bytes 737288 | tf_op jit(solution)/shard_map/ppermute | solution.py:25
  119.2 11.1 %collective-permute-start.18 = (bf16[144,768]{1,0:T(8,128)(2,1)S(1)}, bf16[144,768]{1,0:T(8,128)(2,1)S(1)}, u32[]{:S(2)}, u32[]{:S(2)}) collective-permute-start(bf16[144,768]{1,0:T(8,128)(2,1)S(1)} %get-tuple-element.84), channel_id=1, source_target_pairs={{0,8},{1,9},{2,10},{3,11},{4,12},{5,13},{6,14},{7,15},{8,0},{9,1},... | collective-permute-start | bytes 663560 | tf_op jit(solution)/shard_map/ppermute | solution.py:25
  119.5 18.7 %collective-permute-start.19 = (bf16[144,768]{1,0:T(8,128)(2,1)S(1)}, bf16[144,768]{1,0:T(8,128)(2,1)S(1)}, u32[]{:S(2)}, u32[]{:S(2)}) collective-permute-start(bf16[144,768]{1,0:T(8,128)(2,1)S(1)} %get-tuple-element.85), channel_id=1, source_target_pairs={{0,16},{1,17},{2,18},{3,19},{4,20},{5,21},{6,22},{7,23},{8,24},{9,... | collective-permute-start | bytes 663560 | tf_op jit(solution)/shard_map/ppermute | solution.py:25
  121.3 16.9 %collective-permute-start.20 = (bf16[144,768]{1,0:T(8,128)(2,1)S(1)}, bf16[144,768]{1,0:T(8,128)(2,1)S(1)}, u32[]{:S(2)}, u32[]{:S(2)}) collective-permute-start(bf16[144,768]{1,0:T(8,128)(2,1)S(1)} %get-tuple-element.86), channel_id=1, source_target_pairs={{0,24},{1,25},{2,26},{3,27},{4,28},{5,29},{6,30},{7,31},{8,16},{9,... | collective-permute-start | bytes 663560 | tf_op jit(solution)/shard_map/ppermute | solution.py:25
  123.7 2.2 %copy-start.1 = (bf16[1024,2048]{1,0:T(8,128)(2,1)S(1)}, bf16[1024,2048]{1,0:T(8,128)(2,1)}, u32[]{:S(2)}) copy-start(bf16[1024,2048]{1,0:T(8,128)(2,1)} %w_one.3) | copy-start | bytes 12582916
  138.9 4.3 %collective-permute-start.21 = (bf16[32,768]{1,0:T(8,128)(2,1)S(1)}, bf16[32,768]{1,0:T(8,128)(2,1)S(1)}, u32[]{:S(2)}, u32[]{:S(2)}) collective-permute-start(bf16[32,768]{1,0:T(8,128)(2,1)S(1)} %get-tuple-element.88), channel_id=1, source_target_pairs={{0,2},{1,3},{2,0},{3,1},{4,6},{5,7},{6,4},{7,5},{8,10},{9,11},{10,... | collective-permute-start | bytes 147464 | tf_op jit(solution)/shard_map/ppermute | solution.py:25
  139.7 4.1 %collective-permute-start.22 = (bf16[32,768]{1,0:T(8,128)(2,1)S(1)}, bf16[32,768]{1,0:T(8,128)(2,1)S(1)}, u32[]{:S(2)}, u32[]{:S(2)}) collective-permute-start(bf16[32,768]{1,0:T(8,128)(2,1)S(1)} %get-tuple-element.89), channel_id=1, source_target_pairs={{0,4},{1,5},{2,6},{3,7},{4,0},{5,1},{6,2},{7,3},{8,12},{9,13},{10,... | collective-permute-start | bytes 147464 | tf_op jit(solution)/shard_map/ppermute | solution.py:25
  140.4 5.0 %collective-permute-start.23 = (bf16[32,768]{1,0:T(8,128)(2,1)S(1)}, bf16[32,768]{1,0:T(8,128)(2,1)S(1)}, u32[]{:S(2)}, u32[]{:S(2)}) collective-permute-start(bf16[32,768]{1,0:T(8,128)(2,1)S(1)} %get-tuple-element.90), channel_id=1, source_target_pairs={{0,6},{1,7},{2,4},{3,5},{4,2},{5,3},{6,0},{7,1},{8,14},{9,15},{10,... | collective-permute-start | bytes 147464 | tf_op jit(solution)/shard_map/ppermute | solution.py:25

commit v5 on v3

--- a/solution.py
+++ b/solution.py
@@ -38,7 +38,7 @@
     moved = sum(o.size * o.dtype.itemsize for o in operands) + sum(
         o.size * o.dtype.itemsize for o in outs
     )
-    vmem, other = pl.BlockSpec(memory_space=pltpu.VMEM), pl.BlockSpec(memory_space=pl.ANY)
+    vmem, other = pl.BlockSpec(memory_space=pltpu.VMEM), pl.BlockSpec(memory_space=pltpu.HBM)
     return pl.pallas_call(
         body,
         out_shape=tuple(outs),
@@ -125,9 +125,11 @@
     return centred * inverse, inverse
 
 
-def forward_kernel(ids, x, w_one, taps, scale, shift, acts, sends, kept, wide, masks, flipped, halves, sems):
+def forward_kernel(ids, x, w_one, taps, scale, shift, acts, mine, theirs, kept, wide, masks, flipped, halves, sems):
+    core = ids[3]
     frame_rows, feat = x.shape
     taps_count = taps.shape[0]
+    taps = taps[...].astype(F32)
     half = taps_count // 2
     fill_masks(ids, masks)
     normed = standardise(x)[0].astype(BF)
@@ -160,7 +162,10 @@
         for g in range(32):
             to = h * (feat // 2) + (g // 2) * part
             halves[g % 2, to : to + part, :] = flipped[h, g * part : (g + 1) * part, :].astype(BF)
-    copies = [pltpu.make_async_copy(halves.at[g % 2], sends.at[g], sems.at[1 + g]) for g in range(8)]
+    copies = [
+        pltpu.make_async_copy(halves.at[core], mine, sems.at[1]),
+        pltpu.make_async_copy(halves.at[1 - core], theirs, sems.at[2]),
+    ]
     for copy in copies:
         copy.start()
     out_acts.wait()
@@ -222,6 +227,7 @@
     fetch_acts.start()
     frame_rows, feat = grad_out.shape
     taps_count = taps.shape[0]
+    taps = taps[...].astype(F32)
     half = taps_count // 2
     sources, slots, width = incoming.shape
     outer = sources // 2
@@ -275,13 +281,17 @@
             out[tap_at, w1_cols:] = jnp.zeros((16, w2_cols), BF)
 
 
-def weights_kernel(ids, early, g0, g1, g2, g3, g4, g5, g6, g7, own, s1, s2, s3, rows, tap_sum, feats, sems):
+def weights_kernel(
+    ids, near, near_core, far, far_core, g0, g1, g2, g3, g4, g5, g6, g7, own, s1, s2, s3, rows, tap_sum, feats, sems
+):
     z = ids[1]
-    me = 2 * ids[2] + ids[3]
     copies = []
-    for m in range(8):
-        copies.append(pltpu.make_async_copy(early.at[jnp.bitwise_xor(me, m)], feats.at[m], sems.at[m]))
-        copies[-1].start()
+    for n, (three, one) in enumerate(((near, near_core), (far, far_core))):
+        copies.append(pltpu.make_async_copy(three.at[0], feats.at[4 * n], sems.at[3 * n]))
+        copies.append(pltpu.make_async_copy(three.at[1:3], feats.at[4 * n + 2 : 4 * n + 4], sems.at[3 * n + 1]))
+        copies.append(pltpu.make_async_copy(one, feats.at[4 * n + 1], sems.at[3 * n + 2]))
+    for copy in copies:
+        copy.start()
     gots = (g0, g1, g2, g3, g4, g5, g6, g7)
     frame_rows = feats.shape[2]
     half = feats.shape[1] // 2
@@ -571,10 +581,6 @@
     two = swap("rep", proj_weight, 4)
     one = swap("rep", proj_weight, 2)
     adj_other = swap("rep", adj_grad, 1)
-    proj_again, two, layer_later = lax.optimization_barrier((proj_weight, two, layer_input))
-    inner = lax.ppermute(proj_again, "rep", [(o * 2 + p, (3 - o) * 2 + p) for o in (1, 2) for p in (0, 1)])
-    ends = lax.ppermute(two, "rep", [(o * 2 + p, (o ^ 1) * 2 + p) for o in (1, 2) for p in (0, 1)])
-
     targets = adj_target[:, 0].reshape(reps, sections, quarter)
     frames = adj_frame.reshape(reps, sections, quarter)
     sec_targets = lax.dynamic_index_in_dim(targets, sec_here, 1, keepdims=False)
@@ -595,37 +601,39 @@
         [like((reps * 2 * capacity, 2 * quarter), BF), like((2, frame_rows, reps * capacity), BF)],
         name="routing",
     )
-    tap_values = conv_taps.astype(F32)
     square = (frame_rows, feat)
     group = 8
     dma = pltpu.SemaphoreType.DMA
     wide = pltpu.VMEM((frame_rows + 16, feat), F32)
     mask_space = pltpu.VMEM((taps_count, frame_rows, 128), F32)
-    acts, sends = local_call(
+    acts, mine_half, their_half = local_call(
         forward_kernel,
         ids,
-        (layer_later, w_pointwise1, tap_values, conv_scale.reshape(1, -1), conv_shift.reshape(1, -1)),
-        [like((3, *square), F32), like((group, feat, frame_rows), BF)],
+        (layer_input, w_pointwise1, conv_taps, conv_scale.reshape(1, -1), conv_shift.reshape(1, -1)),
+        [like((3, *square), F32), like((feat, frame_rows), BF), like((feat, frame_rows), BF)],
         [
             pltpu.VMEM((3, *square), F32),
             wide,
             mask_space,
             pltpu.VMEM((2, feat, frame_rows), F32),
             pltpu.VMEM((2, feat, frame_rows), BF),
-            dma((1 + group,)),
+            dma((3,)),
         ],
         flops=4 * frame_rows * feat * feat,
         name="forward",
-        leave=(0, 1),
-    )
-    early = lax.all_to_all(
-        sends,
-        BOTH,
-        split_axis=0,
-        concat_axis=0,
-        axis_index_groups=[[g * group + m for m in range(group)] for g in range(reps * sections // group)],
-        tiled=True,
-    )
+        leave=(0, 1, 2),
+    )
+    near = [mine_half, swap(BOTH, mine_half, 2), swap(BOTH, their_half, 3)]
+    two, one, near = lax.optimization_barrier((two, one, near))
+    near = jnp.stack(near)
+    proj_again, two, one, adj_other, pack, pick, near = lax.optimization_barrier(
+        (proj_weight, two, one, adj_other, pack, pick, near)
+    )
+    inner = lax.ppermute(proj_again, "rep", [(o * 2 + p, (3 - o) * 2 + p) for o in (1, 2) for p in (0, 1)])
+    ends = lax.ppermute(two, "rep", [(o * 2 + p, (o ^ 1) * 2 + p) for o in (1, 2) for p in (0, 1)])
+    far_three = swap(BOTH, near, 4)
+    near_core = swap(BOTH, their_half, 1)
+    far_core = swap(BOTH, their_half, 5)
 
     rows = 2 * quarter
 
@@ -646,7 +654,7 @@
     lot_one = products("products", proj_weight, one, two)
     inner, ends, lot_one = lax.optimization_barrier((inner, ends, lot_one))
     lot_two = products("last_products", inner, ends)
-    lot_two, early = lax.optimization_barrier((lot_two, early))
+    lot_two, far_three, far_core = lax.optimization_barrier((lot_two, far_three, far_core))
     lane = outer * piece
     (packed,) = local_call(
         packing_kernel,
@@ -658,12 +666,13 @@
     )
     outgoing = packed.reshape(reps, 2 * capacity, lane)
     incoming = lax.all_to_all(outgoing, "rep", split_axis=0, concat_axis=0, tiled=True)
+    incoming, near_core = lax.optimization_barrier((incoming, near_core))
     late = like((frame_rows + 32, 3 * feat // 4), BF)
     lot = like((frame_rows + 16, 3 * feat // 4), BF)
     grad_out, grad_mixed, p0, p2, p4, p6 = local_call(
         module_kernel,
         ids,
-        (incoming, pick, tap_values, w_pointwise2, acts),
+        (incoming, pick, conv_taps, w_pointwise2, acts),
         [like(square, BF), like((frame_rows, 2 * feat), BF)] + [late] * 4,
         [wide, wide, mask_space, pltpu.VMEM((feat, feat), BF), pltpu.VMEM((3, *square), F32), dma((2,))],
         flops=2 * frame_rows * feat * feat + 60 * frame_rows * feat,
@@ -677,15 +686,15 @@
     sums = local_call(
         weights_kernel,
         ids,
-        (early, *got),
+        (near, near_core, far_three, far_core, *got),
         [like(lot.shape, F32)] + [lot] * 3,
         [
             pltpu.VMEM((feat // 2, 3 * feat // 4), F32),
             pltpu.VMEM((32, feat // 2), F32),
             pltpu.VMEM((group, feat, frame_rows), BF),
-            dma((group,)),
+            dma((6,)),
         ],
-        stay=(0,),
+        stay=(0, 1, 2, 3),
         flops=2 * 8 * frame_rows * (feat // 2) * (3 * feat // 4),
         name="weights",
     )

time: 186 us -> 131 us (0.70)
  waiting for transfers between devices: 90.3 us -> 50.8 us
  blocking collectives: 12.9 us -> 0 us
  local copies, waits for them, and re-layouts: 24 us -> 18 us
  starting transfers between devices: 29.6 us -> 33.4 us
    ppermute x22 -> x27, waiting for transfers between devices: 90.3 us -> 44 us  [swap(): return lax.ppermute(values, axis, xor_perm(size_of(axis), mask))]
    all_to_all x1 -> x0, blocking collectives: 12.9 us -> none  [line_shards(): lax.all_to_all(outgoing, 'rep', split_axis=0, concat_axis=0, tiled=True)]
    all_to_all x1, waiting for transfers between devices: 0.01 us -> 6.81 us  [line_shards(): lax.all_to_all(outgoing, 'rep', split_axis=0, concat_axis=0, tiled=True)]
    ppermute x22 -> x27, starting transfers between devices: 22.9 us -> 27.3 us  [swap(): return lax.ppermute(values, axis, xor_perm(size_of(axis), mask))]
    unnamed x46 -> x48, local copies, waits for them, and re-layouts: 21 us -> 16.9 us
  transfers between devices with their start and end apart: 25 -> 30, of which waited for: 14 -> 15; matrix products, arithmetic and copies ran while one was open for 3% -> 3% of each run, Pallas kernels for 6% -> 10%
where the time goes in v5:
time: 131 us; the launch traced here: 129 us
  waiting for transfers between devices  50.8 us (39%)
  starting transfers between devices  33.4 us (25%)
  Pallas kernels  23.8 us (18%)
  local copies, waits for them, and re-layouts  18 us (14%)
  other arithmetic  1.86 us (1%)
    ppermute x27, waiting for transfers between devices, swap(): return lax.ppermute(values, axis, xor_perm(size_of(axis), mask))  44 us
    ppermute x27, starting transfers between devices, swap(): return lax.ppermute(values, axis, xor_perm(size_of(axis), mask))  27.3 us
    pallas_call x10, Pallas kernels, local_call(): pl.pallas_call(body, out_shape=tuple(outs), in_specs=[pl.BlockSpec(memory...  23.8 us
    unnamed x48, local copies, waits for them, and re-layouts  16.9 us
    all_to_all x1, waiting for transfers between devices, line_shards(): lax.all_to_all(outgoing, 'rep', split_axis=0, concat_axis=0, tiled=True)  6.81 us
    all_to_all x1, starting transfers between devices, line_shards(): lax.all_to_all(outgoing, 'rep', split_axis=0, concat_axis=0, tiled=True)  4.06 us
  transfers between devices with their start and end apart: 30, of which 15 were waited for; matrix products, arithmetic and copies ran while one was open for 3% of the time, Pallas kernels for 10%

profile of v5, /device:TPU:0, one launch (start us, length us, event | category | flops | bytes accessed | tf_op | source)
XLA Modules:
  0.0 128.6 jit_solution(2849812035320832761)
XLA Ops:
  0.6 3.0 %collective-permute-start.4 = (bf16[256,2048]{1,0:T(8,128)(2,1)}, bf16[256,2048]{1,0:T(8,128)(2,1)S(1)}, u32[]{:S(2)}, u32[]{:S(2)}) collective-permute-start(bf16[256,2048]{1,0:T(8,128)(2,1)} %refs_0_.3), channel_id=1, source_target_pairs={{0,4},{4,0},{8,12},{12,8},{16,20},{20,16},{24,28},{28,24},{1,5},{5... | collective-permute-start | bytes 3145736 | tf_op jit(solution)/shard_map/ppermute | solution.py:25
  3.7 2.6 %collective-permute-start = (bf16[128,2048]{1,0:T(8,128)(2,1)}, bf16[128,2048]{1,0:T(8,128)(2,1)S(1)}, u32[]{:S(2)}, u32[]{:S(2)}) collective-permute-start(bf16[128,2048]{1,0:T(8,128)(2,1)} %refs_2_.1), channel_id=1, source_target_pairs={{0,16},{4,20},{8,24},{12,28},{16,0},{20,4},{24,8},{28,12},{1,17},{... | collective-permute-start | bytes 1572872 | tf_op jit(solution)/shard_map/ppermute | solution.py:25
  6.3 1.6 %collective-permute-start.1 = (bf16[128,2048]{1,0:T(8,128)(2,1)}, bf16[128,2048]{1,0:T(8,128)(2,1)}, u32[]{:S(2)}, u32[]{:S(2)}) collective-permute-start(bf16[128,2048]{1,0:T(8,128)(2,1)} %refs_2_.1), channel_id=1, source_target_pairs={{0,8},{4,12},{8,0},{12,4},{16,24},{20,28},{24,16},{28,20},{1,9},{5... | collective-permute-start | bytes 1572872 | tf_op jit(solution)/shard_map/ppermute | solution.py:25
  7.8 0.7 concatenate.3.ids
  8.6 2.2 %copy-done = bf16[1024,2048]{1,0:T(8,128)(2,1)S(1)} copy-done((bf16[1024,2048]{1,0:T(8,128)(2,1)S(1)}, bf16[1024,2048]{1,0:T(8,128)(2,1)}, u32[]{:S(2)}) %copy-start) | copy-done | bytes 4194328
  10.8 0.9 copy-done.6
  11.7 0.8 copy-done.17
  12.5 0.7 copy-done.19
  13.2 0.7 copy-done.20
  13.8 3.9 %forward.1 = (f32[3,128,1024]{2,1,0:T(8,128)S(1)}, bf16[1024,128]{1,0:T(8,128)(2,1)}, bf16[1024,128]{1,0:T(8,128)(2,1)}) custom-call(s32[9]{0:T(128)S(1)} %concatenate.3.ids, bf16[128,1024]{1,0:T(8,128)(2,1)S(1)} %copy-done.6, bf16[1024,2048]{1,0:T(8,128)(2,1)S(1)} %copy-done, bf16[9,1024]{1,0:T(8,128)(2,1)S(1)} %copy-done.17, f32[1,1024]{1,0:T(1,128)S(1)} %bitcast.22, ...), custom_call_target="tpu_custom_call" | custom-call | flops 536870912 | bytes 6580224 | tf_op jit(solution)/shard_map/forward/pallas_call | solution.py:42
  17.7 1.2 copy-done.4
  18.9 1.5 %collective-permute-start.2 = (bf16[1024,128]{1,0:T(8,128)(2,1)}, bf16[1024,128]{1,0:T(8,128)(2,1)}, u32[]{:S(2)}, u32[]{:S(2)}) collective-permute-start(bf16[1024,128]{1,0:T(8,128)(2,1)} %get-tuple-element.66), channel_id=1, source_target_pairs={{0,2},{1,3},{2,0},{3,1},{4,6},{5,7},{6,4},{7,5},{8,10},{9,11},{10,... | collective-permute-start | bytes 786440 | tf_op jit(solution)/shard_map/ppermute | solution.py:25
  20.9 0.7 reduce.7
  21.9 1.0 routing.1
  22.9 5.5 %collective-permute-done.2 = bf16[1024,128]{1,0:T(8,128)(2,1)} collective-permute-done((bf16[1024,128]{1,0:T(8,128)(2,1)}, bf16[1024,128]{1,0:T(8,128)(2,1)}, u32[]{:S(2)}, u32[]{:S(2)}) %collective-permute-start.2) | collective-permute-done | bytes 262176 | tf_op jit(solution)/shard_map/ppermute | solution.py:25
  28.5 2.6 %collective-permute-done.3 = bf16[1024,128]{1,0:T(8,128)(2,1)} collective-permute-done((bf16[1024,128]{1,0:T(8,128)(2,1)}, bf16[1024,128]{1,0:T(8,128)(2,1)}, u32[]{:S(2)}, u32[]{:S(2)}) %collective-permute-start.3) | collective-permute-done | bytes 262176 | tf_op jit(solution)/shard_map/ppermute | solution.py:25
  31.1 0.8 copy-done.11
  31.9 1.2 pad_maximum_fusion.near
  33.1 0.6 collective-permute-start.13
  33.6 0.7 collective-permute-start.5
  34.3 1.3 %collective-permute-start.6 = (bf16[128,2048]{1,0:T(8,128)(2,1)}, bf16[128,2048]{1,0:T(8,128)(2,1)S(1)}, u32[]{:S(2)}, u32[]{:S(2)}) collective-permute-start(bf16[128,2048]{1,0:T(8,128)(2,1)} %copy-done.11), channel_id=1, source_target_pairs={{8,0},{12,4},{16,24},{20,28},{9,1},{13,5},{17,25},{21,29},{10,2},{... | collective-permute-start | bytes 1572872 | tf_op jit(solution)/shard_map/ppermute | solution.py:633
  35.6 1.0 copy-done.12
  36.7 3.2 %products.1 = (f32[128,384]{1,0:T(8,128)S(1)}, bf16[128,384]{1,0:T(8,128)(2,1)S(1)}, bf16[128,384]{1,0:T(8,128)(2,1)S(1)}, bf16[128,384]{1,0:T(8,128)(2,1)S(1)}) custom-call(s32[9]{0:T(128)S(1)} %concatenate.3.ids, bf16[256,2048]{1,0:T(8,128)(2,1)S(1)} %copy-done.2, bf16[256,2048]{1,0:T(8,128)(2,1)S(1)} %collective-permute-done.4.refs_1_, ...), custom_call_target="tpu_custom_call" | custom-call | flops 805306368 | bytes 4161536 | tf_op jit(solution)/shard_map/products/pallas_call | solution.py:42
  39.9 0.6 collective-permute-start.7
  40.5 1.2 collective-permute-start.14
  41.7 1.5 %collective-permute-start.8 = (bf16[128,384]{1,0:T(8,128)(2,1)S(1)}, bf16[128,384]{1,0:T(8,128)(2,1)S(1)}, u32[]{:S(2)}, u32[]{:S(2)}) collective-permute-start(bf16[128,384]{1,0:T(8,128)(2,1)S(1)} %get-tuple-element.75), channel_id=1, source_target_pairs={{0,2},{1,3},{2,0},{3,1},{4,6},{5,7},{6,4},{7,5},{8,10},{9,11},{10,... | collective-permute-start | bytes 294920 | tf_op jit(solution)/shard_map/ppermute | solution.py:25
  43.2 3.6 %collective-permute-done.8.r2 = bf16[128,384]{1,0:T(8,128)(2,1)S(1)} collective-permute-done((bf16[128,384]{1,0:T(8,128)(2,1)S(1)}, bf16[128,384]{1,0:T(8,128)(2,1)S(1)}, u32[]{:S(2)}, u32[]{:S(2)}) %collective-permute-start.8) | collective-permute-done | bytes 98336 | tf_op jit(solution)/shard_map/ppermute | solution.py:25
  46.8 0.8 collective-permute-start.9
  47.6 4.3 %collective-permute-done.9.r3 = bf16[128,384]{1,0:T(8,128)(2,1)S(1)} collective-permute-done((bf16[128,384]{1,0:T(8,128)(2,1)S(1)}, bf16[128,384]{1,0:T(8,128)(2,1)S(1)}, u32[]{:S(2)}, u32[]{:S(2)}) %collective-permute-start.9) | collective-permute-done | bytes 98336 | tf_op jit(solution)/shard_map/ppermute | solution.py:25
  51.9 2.0 %last_products.1 = (f32[128,128]{1,0:T(8,128)S(1)}, bf16[128,128]{1,0:T(8,128)(2,1)S(1)}, bf16[128,128]{1,0:T(8,128)(2,1)S(1)}, bf16[128,128]{1,0:T(8,128)(2,1)S(1)}) custom-call(s32[9]{0:T(128)S(1)} %concatenate.3.ids, bf16[256,2048]{1,0:T(8,128)(2,1)S(1)} %copy-done.2, bf16[256,2048]{1,0:T(8,128)(2,1)S(1)} %collective-permute-done.4.refs_1_, ...), custom_call_target="tpu_custom_call" | custom-call | flops 268435456 | bytes 3309568 | tf_op jit(solution)/shard_map/last_products/pallas_call | solution.py:42
  54.2 1.3 %collective-permute-start.11 = (bf16[128,128]{1,0:T(8,128)(2,1)S(1)}, bf16[128,128]{1,0:T(8,128)(2,1)S(1)}, u32[]{:S(2)}, u32[]{:S(2)}) collective-permute-start(bf16[128,128]{1,0:T(8,128)(2,1)S(1)} %get-tuple-element.85), channel_id=1, source_target_pairs={{0,2},{1,3},{2,0},{3,1},{4,6},{5,7},{6,4},{7,5},{8,10},{9,11},{10,... | collective-permute-start | bytes 98312 | tf_op jit(solution)/shard_map/ppermute | solution.py:25
  55.9 3.0 %collective-permute-done.14.far_core = bf16[1024,128]{1,0:T(8,128)(2,1)S(1)} collective-permute-done((bf16[1024,128]{1,0:T(8,128)(2,1)}, bf16[1024,128]{1,0:T(8,128)(2,1)S(1)}, u32[]{:S(2)}, u32[]{:S(2)}) %collective-permute-start.14) | collective-permute-done | bytes 262176 | tf_op jit(solution)/shard_map/ppermute | solution.py:25
  58.8 0.7 copy-done.13
  59.6 0.9 copy-done.8
  60.4 1.5 %packing.1 = bf16[256,512]{1,0:T(8,128)(2,1)} custom-call(s32[9]{0:T(128)S(1)} %concatenate.3.ids, f32[128,384]{1,0:T(8,128)S(1)} %get-tuple-element.77.own, bf16[128,384]{1,0:T(8,128)(2,1)S(1)} %collective-permute-done.7.r1, bf16[128,384]{1,0:T(8,128)(2,1)S(1)} %collective-permute-done.8.r2, bf16[128,384]{1,0:T(8,128)(2,1)S(1)} %collective-permute-done.9.r3, ...), custom_call_target="tpu_custom_call" | custom-call | flops 33554432 | bytes 983040 | tf_op jit(solution)/shard_map/packing/pallas_call | solution.py:42
  61.9 4.1 %all-to-all-start = ((bf16[8,32,512]{2,1,0:T(8,128)(2,1)}), bf16[8,32,512]{2,1,0:T(8,128)(2,1)S(1)}, u32[]{:S(2)}, u32[]{:S(2)}) async-start(bf16[8,32,512]{2,1,0:T(8,128)(2,1)} %bitcast.11), calls=%async_computation | async-start | bytes 524288 | tf_op jit(solution)/shard_map/all_to_all | solution.py:668
  66.0 1.7 %collective-permute-done.15.near_core = bf16[1024,128]{1,0:T(8,128)(2,1)S(1)} collective-permute-done((bf16[1024,128]{1,0:T(8,128)(2,1)}, bf16[1024,128]{1,0:T(8,128)(2,1)S(1)}, u32[]{:S(2)}, u32[]{:S(2)}) %collective-permute-start.15) | collective-permute-done | bytes 262176 | tf_op jit(solution)/shard_map/ppermute | solution.py:25
  67.8 0.7 copy-done.15
  68.5 6.8 %all-to-all-done.incoming = bf16[8,32,512]{2,1,0:T(8,128)(2,1)S(1)} async-done(((bf16[8,32,512]{2,1,0:T(8,128)(2,1)}), bf16[8,32,512]{2,1,0:T(8,128)(2,1)S(1)}, u32[]{:S(2)}, u32[]{:S(2)}) %all-to-all-start) | async-done | bytes 262176 | tf_op jit(solution)/shard_map/all_to_all | solution.py:668
  75.3 1.6 %copy-done.3 = bf16[1024,1024]{1,0:T(8,128)(2,1)S(1)} copy-done((bf16[1024,1024]{1,0:T(8,128)(2,1)S(1)}, bf16[1024,1024]{1,0:T(8,128)(2,1)}, u32[]{:S(2)}) %copy-start.3) | copy-done | bytes 2097176
  76.9 1.4 %copy-done.5 = f32[3,128,1024]{2,1,0:T(8,128)S(1)} copy-done((f32[3,128,1024]{2,1,0:T(8,128)S(1)}, f32[3,128,1024]{2,1,0:T(8,128)}, u32[]{:S(2)}) %copy-start.5) | copy-done | bytes 1572888
  78.3 4.6 %module.1 = (bf16[128,1024]{1,0:T(8,128)(2,1)S(1)}, bf16[128,2048]{1,0:T(8,128)(2,1)S(1)}, bf16[160,768]{1,0:T(8,128)(2,1)S(1)}, bf16[160,768]{1,0:T(8,128)(2,1)...) custom-call(s32[9]{0:T(128)S(1)} %concatenate.3.ids, bf16[8,32,512]{2,1,0:T(8,128)(2,1)S(1)} %all-to-all-done.incoming, ...), custom_call_target="tpu_custom_call" | custom-call | flops 276299776 | bytes 5785600 | tf_op jit(solution)/shard_map/module/pallas_call | solution.py:42
  82.9 1.1 collective-permute-start.17
  84.0 1.4 %collective-permute-start.19 = (bf16[160,768]{1,0:T(8,128)(2,1)S(1)}, bf16[160,768]{1,0:T(8,128)(2,1)S(1)}, u32[]{:S(2)}, u32[]{:S(2)}) collective-permute-start(bf16[160,768]{1,0:T(8,128)(2,1)S(1)} %get-tuple-element.103), channel_id=1, source_target_pairs={{0,4},{1,5},{2,6},{3,7},{4,0},{5,1},{6,2},{7,3},{8,12},{9,13},{10,... | collective-permute-start | bytes 737288 | tf_op jit(solution)/shard_map/ppermute | solution.py:25
  85.4 1.0 collective-permute-start.21
  86.4 5.4 %collective-permute-done.17.g2 = bf16[160,768]{1,0:T(8,128)(2,1)S(1)} collective-permute-done((bf16[160,768]{1,0:T(8,128)(2,1)S(1)}, bf16[160,768]{1,0:T(8,128)(2,1)S(1)}, u32[]{:S(2)}, u32[]{:S(2)}) %collective-permute-start.17) | collective-permute-done | bytes 245792 | tf_op jit(solution)/shard_map/ppermute | solution.py:25
  91.8 3.3 %collective-permute-done.19.g4 = bf16[160,768]{1,0:T(8,128)(2,1)S(1)} collective-permute-done((bf16[160,768]{1,0:T(8,128)(2,1)S(1)}, bf16[160,768]{1,0:T(8,128)(2,1)S(1)}, u32[]{:S(2)}, u32[]{:S(2)}) %collective-permute-start.19) | collective-permute-done | bytes 245792 | tf_op jit(solution)/shard_map/ppermute | solution.py:25
  95.7 1.0 collective-permute-done.20.g5
  97.0 2.7 %weights.1 = (f32[144,768]{1,0:T(8,128)S(1)}, bf16[144,768]{1,0:T(8,128)(2,1)}, bf16[144,768]{1,0:T(8,128)(2,1)}, bf16[144,768]{1,0:T(8,128)(2,1)}) custom-call(s32[9]{0:T(128)S(1)} %concatenate.3.ids, bf16[3,1024,128]{2,1,0:T(8,128)(2,1)S(1)} %pad_maximum_fusion.near, bf16[1024,128]{1,0:T(8,128)(2,1)S(1)} %copy-done.16, ...), custom_call_target="tpu_custom_call" | custom-call | flops 805306368 | bytes 5169152 | tf_op jit(solution)/shard_map/weights/pallas_call | solution.py:42
  99.7 1.2 collective-permute-start.23
  100.9 1.8 %collective-permute-start.24 = (bf16[144,768]{1,0:T(8,128)(2,1)}, bf16[144,768]{1,0:T(8,128)(2,1)S(1)}, u32[]{:S(2)}, u32[]{:S(2)}) collective-permute-start(bf16[144,768]{1,0:T(8,128)(2,1)} %get-tuple-element.107), channel_id=1, source_target_pairs={{0,16},{1,17},{2,18},{3,19},{4,20},{5,21},{6,22},{7,23},{8,24},{9,... | collective-permute-start | bytes 663560 | tf_op jit(solution)/shard_map/ppermute | solution.py:25
  102.7 1.5 %collective-permute-start.25 = (bf16[144,768]{1,0:T(8,128)(2,1)}, bf16[144,768]{1,0:T(8,128)(2,1)S(1)}, u32[]{:S(2)}, u32[]{:S(2)}) collective-permute-start(bf16[144,768]{1,0:T(8,128)(2,1)} %get-tuple-element.108), channel_id=1, source_target_pairs={{0,24},{1,25},{2,26},{3,27},{4,28},{5,29},{6,30},{7,31},{8,16},{9,... | collective-permute-start | bytes 663560 | tf_op jit(solution)/shard_map/ppermute | solution.py:25
  104.1 2.2 %copy-done.1 = bf16[1024,2048]{1,0:T(8,128)(2,1)S(1)} copy-done((bf16[1024,2048]{1,0:T(8,128)(2,1)S(1)}, bf16[1024,2048]{1,0:T(8,128)(2,1)}, u32[]{:S(2)}) %copy-start.1) | copy-done | bytes 4194328
  106.3 2.9 %tail.1 = bf16[128,1024]{1,0:T(8,128)(2,1)} custom-call(s32[9]{0:T(128)S(1)} %concatenate.3.ids, bf16[128,1024]{1,0:T(8,128)(2,1)S(1)} %copy-done.7, bf16[128,2048]{1,0:T(8,128)(2,1)S(1)} %get-tuple-element.96.grad_mixed, bf16[1024,2048]{1,0:T(8,128)(2,1)S(1)} %copy-done.1, bf16[128,1024]{1,0:T(8,128)(2,1)S(1)} %get-tuple-element.97.grad_out), custom_call_target="tpu_custom_call" | custom-call | flops 536870912 | bytes 5505024 | tf_op jit(solution)/shard_map/tail/pallas_call | solution.py:42
  109.3 2.3 %collective-permute-done.23.r1 = bf16[144,768]{1,0:T(8,128)(2,1)S(1)} collective-permute-done((bf16[144,768]{1,0:T(8,128)(2,1)}, bf16[144,768]{1,0:T(8,128)(2,1)S(1)}, u32[]{:S(2)}, u32[]{:S(2)}) %collective-permute-start.23) | collective-permute-done | bytes 221216 | tf_op jit(solution)/shard_map/ppermute | solution.py:25
  111.5 8.3 %collective-permute-done.24.r2 = bf16[144,768]{1,0:T(8,128)(2,1)S(1)} collective-permute-done((bf16[144,768]{1,0:T(8,128)(2,1)}, bf16[144,768]{1,0:T(8,128)(2,1)S(1)}, u32[]{:S(2)}, u32[]{:S(2)}) %collective-permute-start.24) | collective-permute-done | bytes 221216 | tf_op jit(solution)/shard_map/ppermute | solution.py:25
  119.8 0.7 sums.1
  120.5 1.0 collective-permute-start.26
  121.5 0.8 collective-permute-start.27
  122.3 1.7 %collective-permute-start.28 = (bf16[32,768]{1,0:T(8,128)(2,1)S(1)}, bf16[32,768]{1,0:T(8,128)(2,1)S(1)}, u32[]{:S(2)}, u32[]{:S(2)}) collective-permute-start(bf16[32,768]{1,0:T(8,128)(2,1)S(1)} %get-tuple-element.112), channel_id=1, source_target_pairs={{0,6},{1,7},{2,4},{3,5},{4,2},{5,3},{6,0},{7,1},{8,14},{9,15},{10,... | collective-permute-start | bytes 147464 | tf_op jit(solution)/shard_map/ppermute | solution.py:25
  124.2 0.6 copy.23
  124.8 0.9 collective-permute-done.27.r2
  125.6 1.7 %collective-permute-done.28.r3 = bf16[32,768]{1,0:T(8,128)(2,1)S(1)} collective-permute-done((bf16[32,768]{1,0:T(8,128)(2,1)S(1)}, bf16[32,768]{1,0:T(8,128)(2,1)S(1)}, u32[]{:S(2)}, u32[]{:S(2)}) %collective-permute-start.28) | collective-permute-done | bytes 49184 | tf_op jit(solution)/shard_map/ppermute | solution.py:25
  127.3 1.3 %assembly.1 = (f32[32,2048]{1,0:T(8,128)}, f32[32,1024]{1,0:T(8,128)}) custom-call(s32[9]{0:T(128)S(1)} %concatenate.3.ids, f32[32,768]{1,0:T(8,128)S(1)} %get-tuple-element.109.mine, bf16[32,768]{1,0:T(8,128)(2,1)S(1)} %collective-permute-done.26.r1, bf16[32,768]{1,0:T(8,128)(2,1)S(1)} %collective-permute-done.27.r2, ...), custom_call_target="tpu_custom_call" | custom-call | bytes 638976 | tf_op jit(solution)/shard_map/assembly/pallas_call | solution.py:42
  (64 shorter events, 2.5 us)
Async XLA Ops:
  0.6 32.4 %collective-permute-start.4 = (bf16[256,2048]{1,0:T(8,128)(2,1)}, bf16[256,2048]{1,0:T(8,128)(2,1)S(1)}, u32[]{:S(2)}, u32[]{:S(2)}) collective-permute-start(bf16[256,2048]{1,0:T(8,128)(2,1)} %refs_0_.3), channel_id=1, source_target_pairs={{0,4},{4,0},{8,12},{12,8},{16,20},{20,16},{24,28},{28,24},{1,5},{5... | collective-permute-start | bytes 3145736 | tf_op jit(solution)/shard_map/ppermute | solution.py:25
  3.7 27.4 %collective-permute-start = (bf16[128,2048]{1,0:T(8,128)(2,1)}, bf16[128,2048]{1,0:T(8,128)(2,1)S(1)}, u32[]{:S(2)}, u32[]{:S(2)}) collective-permute-start(bf16[128,2048]{1,0:T(8,128)(2,1)} %refs_2_.1), channel_id=1, source_target_pairs={{0,16},{4,20},{8,24},{12,28},{16,0},{20,4},{24,8},{28,12},{1,17},{... | collective-permute-start | bytes 1572872 | tf_op jit(solution)/shard_map/ppermute | solution.py:25
  6.3 24.8 %collective-permute-start.1 = (bf16[128,2048]{1,0:T(8,128)(2,1)}, bf16[128,2048]{1,0:T(8,128)(2,1)}, u32[]{:S(2)}, u32[]{:S(2)}) collective-permute-start(bf16[128,2048]{1,0:T(8,128)(2,1)} %refs_2_.1), channel_id=1, source_target_pairs={{0,8},{4,12},{8,0},{12,4},{16,24},{20,28},{24,16},{28,20},{1,9},{5... | collective-permute-start | bytes 1572872 | tf_op jit(solution)/shard_map/ppermute | solution.py:25
  8.6 2.2 %copy-start = (bf16[1024,2048]{1,0:T(8,128)(2,1)S(1)}, bf16[1024,2048]{1,0:T(8,128)(2,1)}, u32[]{:S(2)}) copy-start(bf16[1024,2048]{1,0:T(8,128)(2,1)} %w_one.3) | copy-start | bytes 12582916
  10.8 0.9 copy-start.6
  11.7 0.8 copy-start.17
  12.5 0.7 copy-start.19
  13.1 0.7 copy-start.20
  13.8 7.1 %copy-start.22 = (s32[2048,1]{0,1:T(1,128)S(1)}, s32[2048,1]{0,1:T(1,128)}, u32[]{:S(2)}) copy-start(s32[2048,1]{0,1:T(1,128)} %param.20) | copy-start | bytes 24580
  13.8 7.8 %copy-start.21 = (s32[2048]{0:T(1024)S(1)}, s32[2048]{0:T(1024)}, u32[]{:S(2)}) copy-start(s32[2048]{0:T(1024)} %param.21) | copy-start | bytes 24580
  13.8 19.8 %copy-start.10 = (bf16[128,2048]{1,0:T(8,128)(2,1)S(1)}, bf16[128,2048]{1,0:T(8,128)(2,1)}, u32[]{:S(2)}) copy-start(bf16[128,2048]{1,0:T(8,128)(2,1)} %refs_2_.1) | copy-start | bytes 1572868
  13.8 21.8 %copy-start.2 = (bf16[256,2048]{1,0:T(8,128)(2,1)S(1)}, bf16[256,2048]{1,0:T(8,128)(2,1)}, u32[]{:S(2)}) copy-start(bf16[256,2048]{1,0:T(8,128)(2,1)} %refs_0_.3) | copy-start | bytes 3145732
  17.7 1.2 copy-start.4
  18.9 9.6 %collective-permute-start.2 = (bf16[1024,128]{1,0:T(8,128)(2,1)}, bf16[1024,128]{1,0:T(8,128)(2,1)}, u32[]{:S(2)}, u32[]{:S(2)}) collective-permute-start(bf16[1024,128]{1,0:T(8,128)(2,1)} %get-tuple-element.66), channel_id=1, source_target_pairs={{0,2},{1,3},{2,0},{3,1},{4,6},{5,7},{6,4},{7,5},{8,10},{9,11},{10,... | collective-permute-start | bytes 786440 | tf_op jit(solution)/shard_map/ppermute | solution.py:25
  20.4 10.7 %collective-permute-start.3 = (bf16[1024,128]{1,0:T(8,128)(2,1)}, bf16[1024,128]{1,0:T(8,128)(2,1)}, u32[]{:S(2)}, u32[]{:S(2)}) collective-permute-start(bf16[1024,128]{1,0:T(8,128)(2,1)} %get-tuple-element.61), channel_id=1, source_target_pairs={{0,3},{1,2},{2,1},{3,0},{4,7},{5,6},{6,5},{7,4},{8,11},{9,10},{10,... | collective-permute-start | bytes 786440 | tf_op jit(solution)/shard_map/ppermute | solution.py:25
  31.1 0.8 copy-start.11
  33.1 26.5 %collective-permute-start.13 = (bf16[3,1024,128]{2,1,0:T(8,128)(2,1)S(1)}, bf16[3,1024,128]{2,1,0:T(8,128)(2,1)S(1)}, u32[]{:S(2)}, u32[]{:S(2)}) collective-permute-start(bf16[3,1024,128]{2,1,0:T(8,128)(2,1)S(1)} %pad_maximum_fusion.near), channel_id=1, source_target_pairs={{0,4},{1,5},{2,6},{3,7},{4,0},{5,1},{6,2},{7,3},{8,12},{9,13},{10,... | collective-permute-start | bytes 2359304 | tf_op jit(solution)/shard_map/ppermute | solution.py:25
  33.6 18.3 %collective-permute-start.5 = (bf16[128,2048]{1,0:T(8,128)(2,1)S(1)}, bf16[128,2048]{1,0:T(8,128)(2,1)S(1)}, u32[]{:S(2)}, u32[]{:S(2)}) collective-permute-start(bf16[128,2048]{1,0:T(8,128)(2,1)S(1)} %copy-done.10), channel_id=1, source_target_pairs={{8,16},{12,20},{16,8},{20,12},{9,17},{13,21},{17,9},{21,13},{10,18... | collective-permute-start | bytes 1572872 | tf_op jit(solution)/shard_map/ppermute | solution.py:632
  34.3 17.6 %collective-permute-start.6 = (bf16[128,2048]{1,0:T(8,128)(2,1)}, bf16[128,2048]{1,0:T(8,128)(2,1)S(1)}, u32[]{:S(2)}, u32[]{:S(2)}) collective-permute-start(bf16[128,2048]{1,0:T(8,128)(2,1)} %copy-done.11), channel_id=1, source_target_pairs={{8,0},{12,4},{16,24},{20,28},{9,1},{13,5},{17,25},{21,29},{10,2},{... | collective-permute-start | bytes 1572872 | tf_op jit(solution)/shard_map/ppermute | solution.py:633
  35.6 1.0 copy-start.12
  39.9 1.8 %collective-permute-start.7 = (bf16[128,384]{1,0:T(8,128)(2,1)S(1)}, bf16[128,384]{1,0:T(8,128)(2,1)S(1)}, u32[]{:S(2)}, u32[]{:S(2)}) collective-permute-start(bf16[128,384]{1,0:T(8,128)(2,1)S(1)} %get-tuple-element.74), channel_id=1, source_target_pairs={{0,1},{1,0},{2,3},{3,2},{4,5},{5,4},{6,7},{7,6},{8,9},{9,8},{10,11... | collective-permute-start | bytes 294920 | tf_op jit(solution)/shard_map/ppermute | solution.py:25
  40.5 18.3 %collective-permute-start.14 = (bf16[1024,128]{1,0:T(8,128)(2,1)}, bf16[1024,128]{1,0:T(8,128)(2,1)S(1)}, u32[]{:S(2)}, u32[]{:S(2)}) collective-permute-start(bf16[1024,128]{1,0:T(8,128)(2,1)} %get-tuple-element.61), channel_id=1, source_target_pairs={{0,5},{1,4},{2,7},{3,6},{4,1},{5,0},{6,3},{7,2},{8,13},{9,12},{10,... | collective-permute-start | bytes 786440 | tf_op jit(solution)/shard_map/ppermute | solution.py:25
  41.7 5.1 %collective-permute-start.8 = (bf16[128,384]{1,0:T(8,128)(2,1)S(1)}, bf16[128,384]{1,0:T(8,128)(2,1)S(1)}, u32[]{:S(2)}, u32[]{:S(2)}) collective-permute-start(bf16[128,384]{1,0:T(8,128)(2,1)S(1)} %get-tuple-element.75), channel_id=1, source_target_pairs={{0,2},{1,3},{2,0},{3,1},{4,6},{5,7},{6,4},{7,5},{8,10},{9,11},{10,... | collective-permute-start | bytes 294920 | tf_op jit(solution)/shard_map/ppermute | solution.py:25
  46.8 5.0 %collective-permute-start.9 = (bf16[128,384]{1,0:T(8,128)(2,1)S(1)}, bf16[128,384]{1,0:T(8,128)(2,1)S(1)}, u32[]{:S(2)}, u32[]{:S(2)}) collective-permute-start(bf16[128,384]{1,0:T(8,128)(2,1)S(1)} %get-tuple-element.76), channel_id=1, source_target_pairs={{0,3},{1,2},{2,1},{3,0},{4,7},{5,6},{6,5},{7,4},{8,11},{9,10},{10,... | collective-permute-start | bytes 294920 | tf_op jit(solution)/shard_map/ppermute | solution.py:25
  51.9 23.4 %copy-start.18 = (bf16[9,1024]{1,0:T(8,128)(2,1)S(1)}, bf16[9,1024]{1,0:T(8,128)(2,1)}, u32[]{:S(2)}) copy-start(bf16[9,1024]{1,0:T(8,128)(2,1)} %taps.3) | copy-start | bytes 55300
  53.9 5.6 %collective-permute-start.10 = (bf16[128,128]{1,0:T(8,128)(2,1)S(1)}, bf16[128,128]{1,0:T(8,128)(2,1)S(1)}, u32[]{:S(2)}, u32[]{:S(2)}) collective-permute-start(bf16[128,128]{1,0:T(8,128)(2,1)S(1)} %get-tuple-element.84), channel_id=1, source_target_pairs={{0,1},{1,0},{2,3},{3,2},{4,5},{5,4},{6,7},{7,6},{8,9},{9,8},{10,11... | collective-permute-start | bytes 98312 | tf_op jit(solution)/shard_map/ppermute | solution.py:25
  54.2 5.4 %collective-permute-start.11 = (bf16[128,128]{1,0:T(8,128)(2,1)S(1)}, bf16[128,128]{1,0:T(8,128)(2,1)S(1)}, u32[]{:S(2)}, u32[]{:S(2)}) collective-permute-start(bf16[128,128]{1,0:T(8,128)(2,1)S(1)} %get-tuple-element.85), channel_id=1, source_target_pairs={{0,2},{1,3},{2,0},{3,1},{4,6},{5,7},{6,4},{7,5},{8,10},{9,11},{10,... | collective-permute-start | bytes 98312 | tf_op jit(solution)/shard_map/ppermute | solution.py:25
  55.5 4.1 %collective-permute-start.12 = (bf16[128,128]{1,0:T(8,128)(2,1)S(1)}, bf16[128,128]{1,0:T(8,128)(2,1)S(1)}, u32[]{:S(2)}, u32[]{:S(2)}) collective-permute-start(bf16[128,128]{1,0:T(8,128)(2,1)S(1)} %get-tuple-element.86), channel_id=1, source_target_pairs={{0,3},{1,2},{2,1},{3,0},{4,7},{5,6},{6,5},{7,4},{8,11},{9,10},{10,... | collective-permute-start | bytes 98312 | tf_op jit(solution)/shard_map/ppermute | solution.py:25
  58.8 0.7 copy-start.13
  59.5 0.9 copy-start.8
  60.4 36.6 %copy-start.9 = (bf16[3,1024,128]{2,1,0:T(8,128)(2,1)S(1)}, bf16[3,1024,128]{2,1,0:T(8,128)(2,1)}, u32[]{:S(2)}) copy-start(bf16[3,1024,128]{2,1,0:T(8,128)(2,1)} %copy-done.8) | copy-start | bytes 2359300
  61.9 35.1 %copy-start.14 = (bf16[1024,128]{1,0:T(8,128)(2,1)S(1)}, bf16[1024,128]{1,0:T(8,128)(2,1)}, u32[]{:S(2)}) copy-start(bf16[1024,128]{1,0:T(8,128)(2,1)} %copy-done.13) | copy-start | bytes 786436
  61.9 13.3 %all-to-all-start = ((bf16[8,32,512]{2,1,0:T(8,128)(2,1)}), bf16[8,32,512]{2,1,0:T(8,128)(2,1)S(1)}, u32[]{:S(2)}, u32[]{:S(2)}) async-start(bf16[8,32,512]{2,1,0:T(8,128)(2,1)} %bitcast.11), calls=%async_computation | async-start | bytes 524288 | tf_op jit(solution)/shard_map/all_to_all | solution.py:668
  66.0 1.7 %collective-permute-start.15 = (bf16[1024,128]{1,0:T(8,128)(2,1)}, bf16[1024,128]{1,0:T(8,128)(2,1)S(1)}, u32[]{:S(2)}, u32[]{:S(2)}) collective-permute-start(bf16[1024,128]{1,0:T(8,128)(2,1)} %get-tuple-element.61), channel_id=1, source_target_pairs={{0,1},{1,0},{2,3},{3,2},{4,5},{5,4},{6,7},{7,6},{8,9},{9,8},{10,11... | collective-permute-start | bytes 786440 | tf_op jit(solution)/shard_map/ppermute | solution.py:25
  67.8 0.7 copy-start.15
  75.3 1.6 %copy-start.3 = (bf16[1024,1024]{1,0:T(8,128)(2,1)S(1)}, bf16[1024,1024]{1,0:T(8,128)(2,1)}, u32[]{:S(2)}) copy-start(bf16[1024,1024]{1,0:T(8,128)(2,1)} %w_two.1) | copy-start | bytes 6291460
  76.9 1.4 %copy-start.5 = (f32[3,128,1024]{2,1,0:T(8,128)S(1)}, f32[3,128,1024]{2,1,0:T(8,128)}, u32[]{:S(2)}) copy-start(f32[3,128,1024]{2,1,0:T(8,128)} %copy-done.4) | copy-start | bytes 4718596
  78.3 18.7 %copy-start.16 = (bf16[1024,128]{1,0:T(8,128)(2,1)S(1)}, bf16[1024,128]{1,0:T(8,128)(2,1)}, u32[]{:S(2)}) copy-start(bf16[1024,128]{1,0:T(8,128)(2,1)} %copy-done.15) | copy-start | bytes 786436
  82.9 21.3 %copy-start.7 = (bf16[128,1024]{1,0:T(8,128)(2,1)S(1)}, bf16[128,1024]{1,0:T(8,128)(2,1)}, u32[]{:S(2)}) copy-start(bf16[128,1024]{1,0:T(8,128)(2,1)} %x.3) | copy-start | bytes 786436
  82.9 8.9 %collective-permute-start.17 = (bf16[160,768]{1,0:T(8,128)(2,1)S(1)}, bf16[160,768]{1,0:T(8,128)(2,1)S(1)}, u32[]{:S(2)}, u32[]{:S(2)}) collective-permute-start(bf16[160,768]{1,0:T(8,128)(2,1)S(1)} %get-tuple-element.102), channel_id=1, source_target_pairs={{0,2},{1,3},{2,0},{3,1},{4,6},{5,7},{6,4},{7,5},{8,10},{9,11},{10,... | collective-permute-start | bytes 737288 | tf_op jit(solution)/shard_map/ppermute | solution.py:25
  84.0 11.2 %collective-permute-start.19 = (bf16[160,768]{1,0:T(8,128)(2,1)S(1)}, bf16[160,768]{1,0:T(8,128)(2,1)S(1)}, u32[]{:S(2)}, u32[]{:S(2)}) collective-permute-start(bf16[160,768]{1,0:T(8,128)(2,1)S(1)} %get-tuple-element.103), channel_id=1, source_target_pairs={{0,4},{1,5},{2,6},{3,7},{4,0},{5,1},{6,2},{7,3},{8,12},{9,13},{10,... | collective-permute-start | bytes 737288 | tf_op jit(solution)/shard_map/ppermute | solution.py:25
  85.4 9.8 %collective-permute-start.21 = (bf16[160,768]{1,0:T(8,128)(2,1)S(1)}, bf16[160,768]{1,0:T(8,128)(2,1)S(1)}, u32[]{:S(2)}, u32[]{:S(2)}) collective-permute-start(bf16[160,768]{1,0:T(8,128)(2,1)S(1)} %get-tuple-element.104), channel_id=1, source_target_pairs={{0,6},{1,7},{2,4},{3,5},{4,2},{5,3},{6,0},{7,1},{8,14},{9,15},{10,... | collective-permute-start | bytes 737288 | tf_op jit(solution)/shard_map/ppermute | solution.py:25
  86.4 9.2 %collective-permute-start.16 = (bf16[160,768]{1,0:T(8,128)(2,1)S(1)}, bf16[160,768]{1,0:T(8,128)(2,1)S(1)}, u32[]{:S(2)}, u32[]{:S(2)}) collective-permute-start(bf16[160,768]{1,0:T(8,128)(2,1)S(1)} %get-tuple-element.101.g0), channel_id=1, source_target_pairs={{0,1},{1,0},{2,3},{3,2},{4,5},{5,4},{6,7},{7,6},{8,9},{9,8},{10,11... | collective-permute-start | bytes 737288 | tf_op jit(solution)/shard_map/ppermute | solution.py:25
  91.8 3.9 %collective-permute-start.18 = (bf16[160,768]{1,0:T(8,128)(2,1)S(1)}, bf16[160,768]{1,0:T(8,128)(2,1)S(1)}, u32[]{:S(2)}, u32[]{:S(2)}) collective-permute-start(bf16[160,768]{1,0:T(8,128)(2,1)S(1)} %collective-permute-done.17.g2), channel_id=1, source_target_pairs={{0,1},{1,0},{2,3},{3,2},{4,5},{5,4},{6,7},{7,6},{8,9},{9,8},{10,11... | collective-permute-start | bytes 737288 | tf_op jit(solution)/shard_map/ppermute | solution.py:25
  95.1 1.5 %collective-permute-start.20 = (bf16[160,768]{1,0:T(8,128)(2,1)S(1)}, bf16[160,768]{1,0:T(8,128)(2,1)S(1)}, u32[]{:S(2)}, u32[]{:S(2)}) collective-permute-start(bf16[160,768]{1,0:T(8,128)(2,1)S(1)} %collective-permute-done.19.g4), channel_id=1, source_target_pairs={{0,1},{1,0},{2,3},{3,2},{4,5},{5,4},{6,7},{7,6},{8,9},{9,8},{10,11... | collective-permute-start | bytes 737288 | tf_op jit(solution)/shard_map/ppermute | solution.py:25
  95.1 1.9 %collective-permute-start.22 = (bf16[160,768]{1,0:T(8,128)(2,1)S(1)}, bf16[160,768]{1,0:T(8,128)(2,1)S(1)}, u32[]{:S(2)}, u32[]{:S(2)}) collective-permute-start(bf16[160,768]{1,0:T(8,128)(2,1)S(1)} %collective-permute-done.21.g6), channel_id=1, source_target_pairs={{0,1},{1,0},{2,3},{3,2},{4,5},{5,4},{6,7},{7,6},{8,9},{9,8},{10,11... | collective-permute-start | bytes 737288 | tf_op jit(solution)/shard_map/ppermute | solution.py:25
  99.7 11.8 %collective-permute-start.23 = (bf16[144,768]{1,0:T(8,128)(2,1)}, bf16[144,768]{1,0:T(8,128)(2,1)S(1)}, u32[]{:S(2)}, u32[]{:S(2)}) collective-permute-start(bf16[144,768]{1,0:T(8,128)(2,1)} %get-tuple-element.106), channel_id=1, source_target_pairs={{0,8},{1,9},{2,10},{3,11},{4,12},{5,13},{6,14},{7,15},{8,0},{9,1},... | collective-permute-start | bytes 663560 | tf_op jit(solution)/shard_map/ppermute | solution.py:25
  100.9 18.9 %collective-permute-start.24 = (bf16[144,768]{1,0:T(8,128)(2,1)}, bf16[144,768]{1,0:T(8,128)(2,1)S(1)}, u32[]{:S(2)}, u32[]{:S(2)}) collective-permute-start(bf16[144,768]{1,0:T(8,128)(2,1)} %get-tuple-element.107), channel_id=1, source_target_pairs={{0,16},{1,17},{2,18},{3,19},{4,20},{5,21},{6,22},{7,23},{8,24},{9,... | collective-permute-start | bytes 663560 | tf_op jit(solution)/shard_map/ppermute | solution.py:25
  102.7 17.2 %collective-permute-start.25 = (bf16[144,768]{1,0:T(8,128)(2,1)}, bf16[144,768]{1,0:T(8,128)(2,1)S(1)}, u32[]{:S(2)}, u32[]{:S(2)}) collective-permute-start(bf16[144,768]{1,0:T(8,128)(2,1)} %get-tuple-element.108), channel_id=1, source_target_pairs={{0,24},{1,25},{2,26},{3,27},{4,28},{5,29},{6,30},{7,31},{8,16},{9,... | collective-permute-start | bytes 663560 | tf_op jit(solution)/shard_map/ppermute | solution.py:25
  104.1 2.2 %copy-start.1 = (bf16[1024,2048]{1,0:T(8,128)(2,1)S(1)}, bf16[1024,2048]{1,0:T(8,128)(2,1)}, u32[]{:S(2)}) copy-start(bf16[1024,2048]{1,0:T(8,128)(2,1)} %w_one.3) | copy-start | bytes 12582916
  120.5 4.3 %collective-permute-start.26 = (bf16[32,768]{1,0:T(8,128)(2,1)S(1)}, bf16[32,768]{1,0:T(8,128)(2,1)S(1)}, u32[]{:S(2)}, u32[]{:S(2)}) collective-permute-start(bf16[32,768]{1,0:T(8,128)(2,1)S(1)} %get-tuple-element.110), channel_id=1, source_target_pairs={{0,2},{1,3},{2,0},{3,1},{4,6},{5,7},{6,4},{7,5},{8,10},{9,11},{10,... | collective-permute-start | bytes 147464 | tf_op jit(solution)/shard_map/ppermute | solution.py:25
  121.5 4.1 %collective-permute-start.27 = (bf16[32,768]{1,0:T(8,128)(2,1)S(1)}, bf16[32,768]{1,0:T(8,128)(2,1)S(1)}, u32[]{:S(2)}, u32[]{:S(2)}) collective-permute-start(bf16[32,768]{1,0:T(8,128)(2,1)S(1)} %get-tuple-element.111), channel_id=1, source_target_pairs={{0,4},{1,5},{2,6},{3,7},{4,0},{5,1},{6,2},{7,3},{8,12},{9,13},{10,... | collective-permute-start | bytes 147464 | tf_op jit(solution)/shard_map/ppermute | solution.py:25
  122.3 5.0 %collective-permute-start.28 = (bf16[32,768]{1,0:T(8,128)(2,1)S(1)}, bf16[32,768]{1,0:T(8,128)(2,1)S(1)}, u32[]{:S(2)}, u32[]{:S(2)}) collective-permute-start(bf16[32,768]{1,0:T(8,128)(2,1)S(1)} %get-tuple-element.112), channel_id=1, source_target_pairs={{0,6},{1,7},{2,4},{3,5},{4,2},{5,3},{6,0},{7,1},{8,14},{9,15},{10,... | collective-permute-start | bytes 147464 | tf_op jit(solution)/shard_map/ppermute | solution.py:25

commit v6 on v5

--- a/solution.py
+++ b/solution.py
@@ -173,45 +173,54 @@
         copy.wait()
 
 
-def partial_kernel(ids, *refs):
-    own_rows, other_rows, *blocks = refs[:-8]
-    outs, (rows, own_copy, block_copy, sems) = refs[-8:-4], refs[-4:]
-    sec, z = ids[0], ids[1]
-    fetch = [pltpu.make_async_copy(own_rows, own_copy, sems.at[0])]
-    if len(blocks) == 3:
-        fetch.append(pltpu.make_async_copy(blocks[0], block_copy, sems.at[1]))
-    for copy in fetch:
-        copy.start()
+def quarters_out(sec, rows, outs, first):
     quarter = outs[0].shape[0] // 2
-    if len(blocks) == 2:
-        middle = (z == 1) | (z == 2)
-        lots = [(0, lambda: jnp.where(middle, blocks[0][...], blocks[1][...]))]
-    else:
-        lots = [
-            (1, lambda: jnp.concatenate([blocks[1][...], blocks[2][...]], axis=0)),
-            (0, lambda: block_copy[...]),
-        ]
-    steps = [(1, other_rows, lots[0]), (0, own_copy, lots[0])] + [
-        (w, a, lot) for lot in lots[1:] for w, a in ((1, other_rows), (0, own_copy))
-    ]
-    for n, (w, a, (at, lot)) in enumerate(steps):
-        if n == 1:
-            for copy in fetch:
-                copy.wait()
-        lot = lot()
-        first = at * block_copy.shape[0]
-        rows[w, :, first : first + lot.shape[0]] = lax.dot_general(a[...], lot, COLS, preferred_element_type=F32)
+    cols = slice(first, first + rows.shape[2])
     for m, out in enumerate(outs):
         q = jnp.bitwise_xor(sec, m)
         for w in range(2):
-            out[w * quarter : (w + 1) * quarter, :] = rows[w, aligned(q, quarter), :].astype(out.dtype)
-
-
-def packing_kernel(ids, own, r1, r2, r3, own_last, l1, l2, l3, pack, out):
+            out[w * quarter : (w + 1) * quarter, cols] = rows[w, aligned(q, quarter), :].astype(out.dtype)
+
+
+def products_kernel(ids, own_rows, other_rows, b0, b1, b2, own, s1, s2, s3, rows, own_copy, block_copy, sems):
+    fetch = [
+        pltpu.make_async_copy(own_rows, own_copy, sems.at[0]),
+        pltpu.make_async_copy(b0, block_copy, sems.at[1]),
+    ]
+    for copy in fetch:
+        copy.start()
+    piece = b1.shape[0]
+    both = jnp.concatenate([b1[...], b2[...]], axis=0)
+    rows[1, :, piece:] = lax.dot_general(other_rows[...], both, COLS, preferred_element_type=F32)
+    for copy in fetch:
+        copy.wait()
+    rows[0, :, piece:] = lax.dot_general(own_copy[...], both, COLS, preferred_element_type=F32)
+    for w, a in ((1, other_rows), (0, own_copy)):
+        rows[w, :, 0:piece] = lax.dot_general(a[...], block_copy[...], COLS, preferred_element_type=F32)
+    quarters_out(ids[0], rows, (own, s1, s2, s3), 0)
+
+
+def last_kernel(
+    ids, own_rows, other_rows, inner, ends, e0, e1, e2, e3, own, s1, s2, s3, rows, own_copy, sem
+):
+    fetch = pltpu.make_async_copy(own_rows, own_copy, sem)
+    fetch.start()
+    z = ids[1]
+    block = jnp.where((z == 1) | (z == 2), inner[...], ends[...])
+    rows[1] = lax.dot_general(other_rows[...], block, COLS, preferred_element_type=F32)
+    fetch.wait()
+    rows[0] = lax.dot_general(own_copy[...], block, COLS, preferred_element_type=F32)
+    outs = (own, s1, s2, s3)
+    done = e0.shape[1]
+    for earlier, out in zip((e0, e1, e2, e3), outs):
+        out[:, 0:done] = earlier[...]
+    quarters_out(ids[0], rows, outs, done)
+
+
+def packing_kernel(ids, own, r1, r2, r3, pack, out):
     total = own[...] + r1[...].astype(F32) + r2[...].astype(F32) + r3[...].astype(F32)
-    last = own_last[...] + l1[...].astype(F32) + l2[...].astype(F32) + l3[...].astype(F32)
-    piece = last.shape[1]
-    parts = xor_order([total[:, k * piece : (k + 1) * piece] for k in range(3)] + [last], ids[1])
+    piece = total.shape[1] // 4
+    parts = xor_order([total[:, k * piece : (k + 1) * piece] for k in range(4)], ids[1])
     rows = jnp.concatenate(parts, axis=1).astype(BF)
     out[...] = jnp.dot(pack[...], rows, preferred_element_type=F32).astype(BF)
 
@@ -637,36 +646,36 @@
 
     rows = 2 * quarter
 
-    def products(name, *lot):
-        cols = piece * (3 if len(lot) == 3 else 1)
-        sums = local_call(
-            partial_kernel,
+    def products(body, name, cols, done, operands, stay, scratch):
+        return local_call(
+            body,
             ids,
-            (adj_grad, adj_other, *lot),
-            [like((rows, cols), F32)] + [like((rows, cols), BF)] * 3,
-            [pltpu.VMEM((2, block_rows, cols), F32), pltpu.VMEM(adj_grad.shape, BF), pltpu.VMEM(proj_weight.shape, BF), dma((2,))],
-            stay=(0, 2) if len(lot) == 3 else (0,),
+            (adj_grad, adj_other, *operands),
+            [like((rows, done + cols), F32)] + [like((rows, done + cols), BF)] * 3,
+            [pltpu.VMEM((2, block_rows, cols), F32), pltpu.VMEM(adj_grad.shape, BF), *scratch],
+            stay=stay,
             flops=4 * block_rows * adj_grad.shape[1] * cols,
             name=name,
         )
-        return [sums[0]] + [swap("section", sums[m], m) for m in (1, 2, 3)]
-
-    lot_one = products("products", proj_weight, one, two)
-    inner, ends, lot_one = lax.optimization_barrier((inner, ends, lot_one))
-    lot_two = products("last_products", inner, ends)
-    lot_two, far_three, far_core = lax.optimization_barrier((lot_two, far_three, far_core))
+
+    sums = products(
+        products_kernel, "products", 3 * piece, 0, (proj_weight, one, two), (0, 2), (pltpu.VMEM(proj_weight.shape, BF), dma((2,)))
+    )
+    inner, ends, sums, near_core = lax.optimization_barrier((inner, ends, sums, near_core))
+    sums = products(last_kernel, "last_products", piece, 3 * piece, (inner, ends, *sums), (0,), (dma,))
+    given = [swap("section", sums[m], m) for m in (1, 2, 3)]
+    given, far_three, far_core = lax.optimization_barrier((given, far_three, far_core))
     lane = outer * piece
     (packed,) = local_call(
         packing_kernel,
         ids,
-        (*lot_one, *lot_two, pack),
+        (sums[0], *given, pack),
         [like((reps * 2 * capacity, lane), BF)],
         name="packing",
         flops=2 * pack.size * lane,
     )
     outgoing = packed.reshape(reps, 2 * capacity, lane)
     incoming = lax.all_to_all(outgoing, "rep", split_axis=0, concat_axis=0, tiled=True)
-    incoming, near_core = lax.optimization_barrier((incoming, near_core))
     late = like((frame_rows + 32, 3 * feat // 4), BF)
     lot = like((frame_rows + 16, 3 * feat // 4), BF)
     grad_out, grad_mixed, p0, p2, p4, p6 = local_call(

time: 131 us -> 126 us (0.962)
  blocking collectives: 0 us -> 13.3 us
  local copies, waits for them, and re-layouts: 18 us -> 10.9 us
  starting transfers between devices: 33.4 us -> 27 us
  waiting for transfers between devices: 50.8 us -> 47.3 us
  Pallas kernels: 23.8 us -> 22.3 us
    all_to_all x0 -> x1, blocking collectives: none -> 13.3 us  [line_shards(): lax.all_to_all(outgoing, 'rep', split_axis=0, concat_axis=0, tiled=True)]
    ppermute x1, waiting for transfers between devices: 0.01 us -> 9.89 us  [line_shards(): lax.ppermute(two, 'rep', [(o * 2 + p, (o ^ 1) * 2 + p) for o in (1, 2) fo...]
    unnamed x48 -> x32, local copies, waits for them, and re-layouts: 16.9 us -> 9.77 us
    all_to_all x1 -> x0, waiting for transfers between devices: 6.81 us -> none  [line_shards(): lax.all_to_all(outgoing, 'rep', split_axis=0, concat_axis=0, tiled=True)]
    ppermute x27 -> x24, waiting for transfers between devices: 44 us -> 37.4 us  [swap(): return lax.ppermute(values, axis, xor_perm(size_of(axis), mask))]
    all_to_all x1 -> x0, starting transfers between devices: 4.06 us -> none  [line_shards(): lax.all_to_all(outgoing, 'rep', split_axis=0, concat_axis=0, tiled=True)]
    ppermute x27 -> x24, starting transfers between devices: 27.3 us -> 25.1 us  [swap(): return lax.ppermute(values, axis, xor_perm(size_of(axis), mask))]
    pallas_call x10, Pallas kernels: 23.8 us -> 22.3 us  [local_call(): pl.pallas_call(body, out_shape=tuple(outs), in_specs=[pl.BlockSpec(memory...]
  transfers between devices with their start and end apart: 30 -> 26, of which waited for: 15 -> 14; matrix products, arithmetic and copies ran while one was open for 3% -> 3% of each run, Pallas kernels for 10% -> 11%
where the time goes in v6:
time: 126 us; the launch traced here: 124 us
  waiting for transfers between devices  47.3 us (38%)
  starting transfers between devices  27 us (21%)
  Pallas kernels  22.3 us (18%)
  blocking collectives  13.3 us (11%)
  local copies, waits for them, and re-layouts  10.9 us (9%)
  other arithmetic  1.79 us (1%)
    ppermute x24, waiting for transfers between devices, swap(): return lax.ppermute(values, axis, xor_perm(size_of(axis), mask))  37.4 us
    ppermute x24, starting transfers between devices, swap(): return lax.ppermute(values, axis, xor_perm(size_of(axis), mask))  25.1 us
    pallas_call x10, Pallas kernels, local_call(): pl.pallas_call(body, out_shape=tuple(outs), in_specs=[pl.BlockSpec(memory...  22.3 us
    all_to_all x1, blocking collectives, line_shards(): lax.all_to_all(outgoing, 'rep', split_axis=0, concat_axis=0, tiled=True)  13.3 us
    ppermute x1, waiting for transfers between devices, line_shards(): lax.ppermute(two, 'rep', [(o * 2 + p, (o ^ 1) * 2 + p) for o in (1, 2) fo...  9.89 us
    unnamed x32, local copies, waits for them, and re-layouts  9.77 us
  transfers between devices with their start and end apart: 26, of which 14 were waited for; matrix products, arithmetic and copies ran while one was open for 3% of the time, Pallas kernels for 11%

profile of v6, /device:TPU:0, one launch (start us, length us, event | category | flops | bytes accessed | tf_op | source)
XLA Modules:
  0.0 123.5 jit_solution(9967278215617382804)
XLA Ops:
  0.6 3.0 %collective-permute-start.4 = (bf16[256,2048]{1,0:T(8,128)(2,1)}, bf16[256,2048]{1,0:T(8,128)(2,1)S(1)}, u32[]{:S(2)}, u32[]{:S(2)}) collective-permute-start(bf16[256,2048]{1,0:T(8,128)(2,1)} %own_rows.3), channel_id=1, source_target_pairs={{0,4},{4,0},{8,12},{12,8},{16,20},{20,16},{24,28},{28,24},{1,5},{5... | collective-permute-start | bytes 3145736 | tf_op jit(solution)/shard_map/ppermute | solution.py:25
  3.7 1.6 %collective-permute-start.1 = (bf16[128,2048]{1,0:T(8,128)(2,1)}, bf16[128,2048]{1,0:T(8,128)(2,1)}, u32[]{:S(2)}, u32[]{:S(2)}) collective-permute-start(bf16[128,2048]{1,0:T(8,128)(2,1)} %b0.1), channel_id=1, source_target_pairs={{0,8},{4,12},{8,0},{12,4},{16,24},{20,28},{24,16},{28,20},{1,9},{5... | collective-permute-start | bytes 1572872 | tf_op jit(solution)/shard_map/ppermute | solution.py:25
  5.2 2.6 %collective-permute-start = (bf16[128,2048]{1,0:T(8,128)(2,1)}, bf16[128,2048]{1,0:T(8,128)(2,1)S(1)}, u32[]{:S(2)}, u32[]{:S(2)}) collective-permute-start(bf16[128,2048]{1,0:T(8,128)(2,1)} %b0.1), channel_id=1, source_target_pairs={{0,16},{4,20},{8,24},{12,28},{16,0},{20,4},{24,8},{28,12},{1,17},{... | collective-permute-start | bytes 1572872 | tf_op jit(solution)/shard_map/ppermute | solution.py:25
  7.8 0.7 concatenate.3.ids
  8.6 2.2 %copy-done = bf16[1024,2048]{1,0:T(8,128)(2,1)S(1)} copy-done((bf16[1024,2048]{1,0:T(8,128)(2,1)S(1)}, bf16[1024,2048]{1,0:T(8,128)(2,1)}, u32[]{:S(2)}) %copy-start) | copy-done | bytes 4194328
  10.8 0.9 copy-done.6
  11.7 0.8 copy-done.9
  12.5 0.7 copy-done.11
  13.2 0.7 copy-done.12
  13.8 3.9 %forward.1 = (f32[3,128,1024]{2,1,0:T(8,128)S(1)}, bf16[1024,128]{1,0:T(8,128)(2,1)S(1)}, bf16[1024,128]{1,0:T(8,128)(2,1)}) custom-call(s32[9]{0:T(128)S(1)} %concatenate.3.ids, bf16[128,1024]{1,0:T(8,128)(2,1)S(1)} %copy-done.6, bf16[1024,2048]{1,0:T(8,128)(2,1)S(1)} %copy-done, bf16[9,1024]{1,0:T(8,128)(2,1)S(1)} %copy-done.9, f32[1,1024]{1,0:T(1,128)S(1)} %bitcast.24, ...), custom_call_target="tpu_custom_call" | custom-call | flops 536870912 | bytes 6580224 | tf_op jit(solution)/shard_map/forward/pallas_call | solution.py:42
  17.7 1.2 copy-done.4
  18.9 1.5 %collective-permute-start.2 = (bf16[1024,128]{1,0:T(8,128)(2,1)S(1)}, bf16[1024,128]{1,0:T(8,128)(2,1)}, u32[]{:S(2)}, u32[]{:S(2)}) collective-permute-start(bf16[1024,128]{1,0:T(8,128)(2,1)S(1)} %get-tuple-element.64), channel_id=1, source_target_pairs={{0,2},{1,3},{2,0},{3,1},{4,6},{5,7},{6,4},{7,5},{8,10},{9,11},{10,... | collective-permute-start | bytes 786440 | tf_op jit(solution)/shard_map/ppermute | solution.py:25
  20.4 0.5 broadcast.10
  20.9 0.7 reduce.7
  21.6 0.1 reshape_squeeze.3
  21.7 0.1 reshape.35
  21.8 0.1 reshape.36.frames
  21.8 0.1 reshape.34.targets
  21.9 1.0 routing.1
  22.9 5.4 %collective-permute-done.2 = bf16[1024,128]{1,0:T(8,128)(2,1)} collective-permute-done((bf16[1024,128]{1,0:T(8,128)(2,1)S(1)}, bf16[1024,128]{1,0:T(8,128)(2,1)}, u32[]{:S(2)}, u32[]{:S(2)}) %collective-permute-start.2) | collective-permute-done | bytes 262176 | tf_op jit(solution)/shard_map/ppermute | solution.py:25
  28.2 2.6 %collective-permute-done.3 = bf16[1024,128]{1,0:T(8,128)(2,1)} collective-permute-done((bf16[1024,128]{1,0:T(8,128)(2,1)}, bf16[1024,128]{1,0:T(8,128)(2,1)}, u32[]{:S(2)}, u32[]{:S(2)}) %collective-permute-start.3) | collective-permute-done | bytes 262176 | tf_op jit(solution)/shard_map/ppermute | solution.py:25
  30.8 1.1 pad_maximum_fusion.near
  32.0 0.6 collective-permute-start.11
  32.6 0.7 collective-permute-start.5
  33.2 1.3 %collective-permute-start.6 = (bf16[128,2048]{1,0:T(8,128)(2,1)S(1)}, bf16[128,2048]{1,0:T(8,128)(2,1)S(1)}, u32[]{:S(2)}, u32[]{:S(2)}) collective-permute-start(bf16[128,2048]{1,0:T(8,128)(2,1)S(1)} %collective-permute-done.b2), channel_id=1, source_target_pairs={{8,0},{12,4},{16,24},{20,28},{9,1},{13,5},{17,25},{21,29},{10,2},{... | collective-permute-start | bytes 1572872 | tf_op jit(solution)/shard_map/ppermute | solution.py:642
  34.5 0.6 collective-permute-start.7
  35.1 1.2 collective-permute-start.12
  36.3 3.2 %products.1 = (f32[128,384]{1,0:T(8,128)S(1)}, bf16[128,384]{1,0:T(8,128)(2,1)S(1)}, bf16[128,384]{1,0:T(8,128)(2,1)S(1)}, bf16[128,384]{1,0:T(8,128)(2,1)S(1)}) custom-call(s32[9]{0:T(128)S(1)} %concatenate.3.ids, bf16[256,2048]{1,0:T(8,128)(2,1)S(1)} %copy-done.2, bf16[256,2048]{1,0:T(8,128)(2,1)S(1)} %collective-permute-done.4.other_rows, ...), custom_call_target="tpu_custom_call" | custom-call | flops 805306368 | bytes 4161536 | tf_op jit(solution)/shard_map/products/pallas_call | solution.py:42
  39.6 9.9 %collective-permute-done.6.ends = bf16[128,2048]{1,0:T(8,128)(2,1)S(1)} collective-permute-done((bf16[128,2048]{1,0:T(8,128)(2,1)S(1)}, bf16[128,2048]{1,0:T(8,128)(2,1)S(1)}, u32[]{:S(2)}, u32[]{:S(2)}) %collective-permute-start.6) | collective-permute-done | bytes 524320 | tf_op jit(solution)/shard_map/ppermute | solution.py:642
  49.5 2.0 %last_products.1 = (f32[128,512]{1,0:T(8,128)S(1)}, bf16[128,512]{1,0:T(8,128)(2,1)S(1)}, bf16[128,512]{1,0:T(8,128)(2,1)S(1)}, bf16[128,512]{1,0:T(8,128)(2,1)S(1)}) custom-call(s32[9]{0:T(128)S(1)} %concatenate.3.ids, bf16[256,2048]{1,0:T(8,128)(2,1)S(1)} %copy-done.2, bf16[256,2048]{1,0:T(8,128)(2,1)S(1)} %collective-permute-done.4.other_rows, ...), custom_call_target="tpu_custom_call" | custom-call | flops 268435456 | bytes 4292608 | tf_op jit(solution)/shard_map/last_products/pallas_call | solution.py:42
  51.5 0.1 collective-permute-start.8
  51.6 1.6 %collective-permute-start.9 = (bf16[128,512]{1,0:T(8,128)(2,1)S(1)}, bf16[128,512]{1,0:T(8,128)(2,1)S(1)}, u32[]{:S(2)}, u32[]{:S(2)}) collective-permute-start(bf16[128,512]{1,0:T(8,128)(2,1)S(1)} %get-tuple-element.83), channel_id=1, source_target_pairs={{0,2},{1,3},{2,0},{3,1},{4,6},{5,7},{6,4},{7,5},{8,10},{9,11},{10,... | collective-permute-start | bytes 393224 | tf_op jit(solution)/shard_map/ppermute | solution.py:25
  53.2 0.3 collective-permute-start.10
  53.5 4.3 %collective-permute-done.12.far_core = bf16[1024,128]{1,0:T(8,128)(2,1)S(1)} collective-permute-done((bf16[1024,128]{1,0:T(8,128)(2,1)}, bf16[1024,128]{1,0:T(8,128)(2,1)S(1)}, u32[]{:S(2)}, u32[]{:S(2)}) %collective-permute-start.12) | collective-permute-done | bytes 262176 | tf_op jit(solution)/shard_map/ppermute | solution.py:25
  57.8 0.2 collective-permute-done.9.r2
  58.0 1.9 %collective-permute-done.10.r3 = bf16[128,512]{1,0:T(8,128)(2,1)S(1)} collective-permute-done((bf16[128,512]{1,0:T(8,128)(2,1)S(1)}, bf16[128,512]{1,0:T(8,128)(2,1)S(1)}, u32[]{:S(2)}, u32[]{:S(2)}) %collective-permute-start.10) | collective-permute-done | bytes 131104 | tf_op jit(solution)/shard_map/ppermute | solution.py:25
  59.9 0.8 packing.1
  60.7 13.3 %all_to_all.5.incoming = bf16[8,32,512]{2,1,0:T(8,128)(2,1)S(1)} all-to-all(bf16[8,32,512]{2,1,0:T(8,128)(2,1)S(1)} %bitcast.22), channel_id=1, replica_groups=mesh['rep'=8,'section'=4] {'rep'}, dimensions={0} | all-to-all | bytes 524288 | tf_op jit(solution)/shard_map/all_to_all | solution.py:678
  74.1 4.6 %module.1 = (bf16[128,1024]{1,0:T(8,128)(2,1)S(1)}, bf16[128,2048]{1,0:T(8,128)(2,1)S(1)}, bf16[160,768]{1,0:T(8,128)(2,1)S(1)}, bf16[160,768]{1,0:T(8,128)(2,1)...) custom-call(s32[9]{0:T(128)S(1)} %concatenate.3.ids, bf16[8,32,512]{2,1,0:T(8,128)(2,1)S(1)} %all_to_all.5.incoming, ...), custom_call_target="tpu_custom_call" | custom-call | flops 276299776 | bytes 5785600 | tf_op jit(solution)/shard_map/module/pallas_call | solution.py:42
  78.7 1.5 %collective-permute-start.14 = (bf16[160,768]{1,0:T(8,128)(2,1)S(1)}, bf16[160,768]{1,0:T(8,128)(2,1)S(1)}, u32[]{:S(2)}, u32[]{:S(2)}) collective-permute-start(bf16[160,768]{1,0:T(8,128)(2,1)S(1)} %get-tuple-element.98), channel_id=1, source_target_pairs={{0,2},{1,3},{2,0},{3,1},{4,6},{5,7},{6,4},{7,5},{8,10},{9,11},{10,... | collective-permute-start | bytes 737288 | tf_op jit(solution)/shard_map/ppermute | solution.py:25
  80.2 1.4 %collective-permute-start.16 = (bf16[160,768]{1,0:T(8,128)(2,1)S(1)}, bf16[160,768]{1,0:T(8,128)(2,1)S(1)}, u32[]{:S(2)}, u32[]{:S(2)}) collective-permute-start(bf16[160,768]{1,0:T(8,128)(2,1)S(1)} %get-tuple-element.99), channel_id=1, source_target_pairs={{0,4},{1,5},{2,6},{3,7},{4,0},{5,1},{6,2},{7,3},{8,12},{9,13},{10,... | collective-permute-start | bytes 737288 | tf_op jit(solution)/shard_map/ppermute | solution.py:25
  81.6 0.6 collective-permute-start.18
  82.2 5.4 %collective-permute-done.14.g2 = bf16[160,768]{1,0:T(8,128)(2,1)S(1)} collective-permute-done((bf16[160,768]{1,0:T(8,128)(2,1)S(1)}, bf16[160,768]{1,0:T(8,128)(2,1)S(1)}, u32[]{:S(2)}, u32[]{:S(2)}) %collective-permute-start.14) | collective-permute-done | bytes 245792 | tf_op jit(solution)/shard_map/ppermute | solution.py:25
  87.6 3.9 %collective-permute-done.16.g4 = bf16[160,768]{1,0:T(8,128)(2,1)S(1)} collective-permute-done((bf16[160,768]{1,0:T(8,128)(2,1)S(1)}, bf16[160,768]{1,0:T(8,128)(2,1)S(1)}, u32[]{:S(2)}, u32[]{:S(2)}) %collective-permute-start.16) | collective-permute-done | bytes 245792 | tf_op jit(solution)/shard_map/ppermute | solution.py:25
  91.6 0.5 collective-permute-start.19
  92.1 1.0 collective-permute-done.17.g5
  93.1 0.4 collective-permute-done.19.g7
  93.4 1.9 %weights.1 = (f32[144,768]{1,0:T(8,128)S(1)}, bf16[144,768]{1,0:T(8,128)(2,1)S(1)}, bf16[144,768]{1,0:T(8,128)(2,1)S(1)}, bf16[144,768]{1,0:T(8,128)(2,1)S(1)}) custom-call(s32[9]{0:T(128)S(1)} %concatenate.3.ids, bf16[3,1024,128]{2,1,0:T(8,128)(2,1)S(1)} %pad_maximum_fusion.near, bf16[1024,128]{1,0:T(8,128)(2,1)S(1)} %collective-permute-done.7.near_core, ...), custom_call_target="tpu_custom_call" | custom-call | flops 805306368 | bytes 5169152 | tf_op jit(solution)/shard_map/weights/pallas_call | solution.py:42
  95.3 0.9 collective-permute-start.20
  96.2 1.8 %collective-permute-start.21 = (bf16[144,768]{1,0:T(8,128)(2,1)S(1)}, bf16[144,768]{1,0:T(8,128)(2,1)S(1)}, u32[]{:S(2)}, u32[]{:S(2)}) collective-permute-start(bf16[144,768]{1,0:T(8,128)(2,1)S(1)} %get-tuple-element.103), channel_id=1, source_target_pairs={{0,16},{1,17},{2,18},{3,19},{4,20},{5,21},{6,22},{7,23},{8,24},{9,... | collective-permute-start | bytes 663560 | tf_op jit(solution)/shard_map/ppermute | solution.py:25
  98.0 1.7 %collective-permute-start.22 = (bf16[144,768]{1,0:T(8,128)(2,1)S(1)}, bf16[144,768]{1,0:T(8,128)(2,1)S(1)}, u32[]{:S(2)}, u32[]{:S(2)}) collective-permute-start(bf16[144,768]{1,0:T(8,128)(2,1)S(1)} %get-tuple-element.104), channel_id=1, source_target_pairs={{0,24},{1,25},{2,26},{3,27},{4,28},{5,29},{6,30},{7,31},{8,16},{9,... | collective-permute-start | bytes 663560 | tf_op jit(solution)/shard_map/ppermute | solution.py:25
  99.8 2.2 %copy-done.1 = bf16[1024,2048]{1,0:T(8,128)(2,1)S(1)} copy-done((bf16[1024,2048]{1,0:T(8,128)(2,1)S(1)}, bf16[1024,2048]{1,0:T(8,128)(2,1)}, u32[]{:S(2)}) %copy-start.1) | copy-done | bytes 4194328
  101.9 2.9 %tail.1 = bf16[128,1024]{1,0:T(8,128)(2,1)} custom-call(s32[9]{0:T(128)S(1)} %concatenate.3.ids, bf16[128,1024]{1,0:T(8,128)(2,1)S(1)} %copy-done.7, bf16[128,2048]{1,0:T(8,128)(2,1)S(1)} %get-tuple-element.92.grad_mixed, bf16[1024,2048]{1,0:T(8,128)(2,1)S(1)} %copy-done.1, bf16[128,1024]{1,0:T(8,128)(2,1)S(1)} %get-tuple-element.93.grad_out), custom_call_target="tpu_custom_call" | custom-call | flops 536870912 | bytes 5505024 | tf_op jit(solution)/shard_map/tail/pallas_call | solution.py:42
  104.9 2.2 %collective-permute-done.20.r1 = bf16[144,768]{1,0:T(8,128)(2,1)S(1)} collective-permute-done((bf16[144,768]{1,0:T(8,128)(2,1)S(1)}, bf16[144,768]{1,0:T(8,128)(2,1)S(1)}, u32[]{:S(2)}, u32[]{:S(2)}) %collective-permute-start.20) | collective-permute-done | bytes 221216 | tf_op jit(solution)/shard_map/ppermute | solution.py:25
  107.1 7.8 %collective-permute-done.21.r2 = bf16[144,768]{1,0:T(8,128)(2,1)S(1)} collective-permute-done((bf16[144,768]{1,0:T(8,128)(2,1)S(1)}, bf16[144,768]{1,0:T(8,128)(2,1)S(1)}, u32[]{:S(2)}, u32[]{:S(2)}) %collective-permute-start.21) | collective-permute-done | bytes 221216 | tf_op jit(solution)/shard_map/ppermute | solution.py:25
  114.9 0.7 sums.1
  115.6 0.9 collective-permute-start.23
  116.6 0.7 collective-permute-start.24
  117.2 1.9 %collective-permute-start.25 = (bf16[32,768]{1,0:T(8,128)(2,1)S(1)}, bf16[32,768]{1,0:T(8,128)(2,1)S(1)}, u32[]{:S(2)}, u32[]{:S(2)}) collective-permute-start(bf16[32,768]{1,0:T(8,128)(2,1)S(1)} %get-tuple-element.108), channel_id=1, source_target_pairs={{0,6},{1,7},{2,4},{3,5},{4,2},{5,3},{6,0},{7,1},{8,14},{9,15},{10,... | collective-permute-start | bytes 147464 | tf_op jit(solution)/shard_map/ppermute | solution.py:25
  119.2 0.1 reshape.38
  119.2 0.6 copy.23
  119.9 0.8 collective-permute-done.24.r2
  120.6 1.6 %collective-permute-done.25.r3 = bf16[32,768]{1,0:T(8,128)(2,1)S(1)} collective-permute-done((bf16[32,768]{1,0:T(8,128)(2,1)S(1)}, bf16[32,768]{1,0:T(8,128)(2,1)S(1)}, u32[]{:S(2)}, u32[]{:S(2)}) %collective-permute-start.25) | collective-permute-done | bytes 49184 | tf_op jit(solution)/shard_map/ppermute | solution.py:25
  122.2 1.3 %assembly.1 = (f32[32,2048]{1,0:T(8,128)}, f32[32,1024]{1,0:T(8,128)}) custom-call(s32[9]{0:T(128)S(1)} %concatenate.3.ids, f32[32,768]{1,0:T(8,128)S(1)} %get-tuple-element.105.mine, bf16[32,768]{1,0:T(8,128)(2,1)S(1)} %collective-permute-done.23.r1, bf16[32,768]{1,0:T(8,128)(2,1)S(1)} %collective-permute-done.24.r2, ...), custom_call_target="tpu_custom_call" | custom-call | bytes 638976 | tf_op jit(solution)/shard_map/assembly/pallas_call | solution.py:42
  (41 shorter events, 0.1 us)
Async XLA Ops:
  0.6 31.3 %collective-permute-start.4 = (bf16[256,2048]{1,0:T(8,128)(2,1)}, bf16[256,2048]{1,0:T(8,128)(2,1)S(1)}, u32[]{:S(2)}, u32[]{:S(2)}) collective-permute-start(bf16[256,2048]{1,0:T(8,128)(2,1)} %own_rows.3), channel_id=1, source_target_pairs={{0,4},{4,0},{8,12},{12,8},{16,20},{20,16},{24,28},{28,24},{1,5},{5... | collective-permute-start | bytes 3145736 | tf_op jit(solution)/shard_map/ppermute | solution.py:25
  3.7 27.2 %collective-permute-start.1 = (bf16[128,2048]{1,0:T(8,128)(2,1)}, bf16[128,2048]{1,0:T(8,128)(2,1)}, u32[]{:S(2)}, u32[]{:S(2)}) collective-permute-start(bf16[128,2048]{1,0:T(8,128)(2,1)} %b0.1), channel_id=1, source_target_pairs={{0,8},{4,12},{8,0},{12,4},{16,24},{20,28},{24,16},{28,20},{1,9},{5... | collective-permute-start | bytes 1572872 | tf_op jit(solution)/shard_map/ppermute | solution.py:25
  5.2 25.6 %collective-permute-start = (bf16[128,2048]{1,0:T(8,128)(2,1)}, bf16[128,2048]{1,0:T(8,128)(2,1)S(1)}, u32[]{:S(2)}, u32[]{:S(2)}) collective-permute-start(bf16[128,2048]{1,0:T(8,128)(2,1)} %b0.1), channel_id=1, source_target_pairs={{0,16},{4,20},{8,24},{12,28},{16,0},{20,4},{24,8},{28,12},{1,17},{... | collective-permute-start | bytes 1572872 | tf_op jit(solution)/shard_map/ppermute | solution.py:25
  8.6 2.2 %copy-start = (bf16[1024,2048]{1,0:T(8,128)(2,1)S(1)}, bf16[1024,2048]{1,0:T(8,128)(2,1)}, u32[]{:S(2)}) copy-start(bf16[1024,2048]{1,0:T(8,128)(2,1)} %w_one.3) | copy-start | bytes 12582916
  10.8 0.9 copy-start.6
  11.7 0.8 copy-start.9
  12.5 0.7 copy-start.11
  13.1 0.7 copy-start.12
  13.8 7.1 %copy-start.14 = (s32[2048,1]{0,1:T(1,128)S(1)}, s32[2048,1]{0,1:T(1,128)}, u32[]{:S(2)}) copy-start(s32[2048,1]{0,1:T(1,128)} %param.20) | copy-start | bytes 24580
  13.8 7.8 %copy-start.13 = (s32[2048]{0:T(1024)S(1)}, s32[2048]{0:T(1024)}, u32[]{:S(2)}) copy-start(s32[2048]{0:T(1024)} %param.21) | copy-start | bytes 24580
  13.8 18.7 %copy-start.8 = (bf16[128,2048]{1,0:T(8,128)(2,1)S(1)}, bf16[128,2048]{1,0:T(8,128)(2,1)}, u32[]{:S(2)}) copy-start(bf16[128,2048]{1,0:T(8,128)(2,1)} %b0.1) | copy-start | bytes 1572868
  13.8 22.5 %copy-start.2 = (bf16[256,2048]{1,0:T(8,128)(2,1)S(1)}, bf16[256,2048]{1,0:T(8,128)(2,1)}, u32[]{:S(2)}) copy-start(bf16[256,2048]{1,0:T(8,128)(2,1)} %own_rows.3) | copy-start | bytes 3145732
  17.7 1.2 copy-start.4
  18.9 9.4 %collective-permute-start.2 = (bf16[1024,128]{1,0:T(8,128)(2,1)S(1)}, bf16[1024,128]{1,0:T(8,128)(2,1)}, u32[]{:S(2)}, u32[]{:S(2)}) collective-permute-start(bf16[1024,128]{1,0:T(8,128)(2,1)S(1)} %get-tuple-element.64), channel_id=1, source_target_pairs={{0,2},{1,3},{2,0},{3,1},{4,6},{5,7},{6,4},{7,5},{8,10},{9,11},{10,... | collective-permute-start | bytes 786440 | tf_op jit(solution)/shard_map/ppermute | solution.py:25
  20.4 10.4 %collective-permute-start.3 = (bf16[1024,128]{1,0:T(8,128)(2,1)}, bf16[1024,128]{1,0:T(8,128)(2,1)}, u32[]{:S(2)}, u32[]{:S(2)}) collective-permute-start(bf16[1024,128]{1,0:T(8,128)(2,1)} %get-tuple-element.59), channel_id=1, source_target_pairs={{0,3},{1,2},{2,1},{3,0},{4,7},{5,6},{6,5},{7,4},{8,11},{9,10},{10,... | collective-permute-start | bytes 786440 | tf_op jit(solution)/shard_map/ppermute | solution.py:25
  32.0 27.9 %collective-permute-start.11 = (bf16[3,1024,128]{2,1,0:T(8,128)(2,1)S(1)}, bf16[3,1024,128]{2,1,0:T(8,128)(2,1)S(1)}, u32[]{:S(2)}, u32[]{:S(2)}) collective-permute-start(bf16[3,1024,128]{2,1,0:T(8,128)(2,1)S(1)} %pad_maximum_fusion.near), channel_id=1, source_target_pairs={{0,4},{1,5},{2,6},{3,7},{4,0},{5,1},{6,2},{7,3},{8,12},{9,13},{10,... | collective-permute-start | bytes 2359304 | tf_op jit(solution)/shard_map/ppermute | solution.py:25
  32.6 7.0 %collective-permute-start.5 = (bf16[128,2048]{1,0:T(8,128)(2,1)S(1)}, bf16[128,2048]{1,0:T(8,128)(2,1)S(1)}, u32[]{:S(2)}, u32[]{:S(2)}) collective-permute-start(bf16[128,2048]{1,0:T(8,128)(2,1)S(1)} %copy-done.8), channel_id=1, source_target_pairs={{8,16},{12,20},{16,8},{20,12},{9,17},{13,21},{17,9},{21,13},{10,18... | collective-permute-start | bytes 1572872 | tf_op jit(solution)/shard_map/ppermute | solution.py:641
  33.2 16.2 %collective-permute-start.6 = (bf16[128,2048]{1,0:T(8,128)(2,1)S(1)}, bf16[128,2048]{1,0:T(8,128)(2,1)S(1)}, u32[]{:S(2)}, u32[]{:S(2)}) collective-permute-start(bf16[128,2048]{1,0:T(8,128)(2,1)S(1)} %collective-permute-done.b2), channel_id=1, source_target_pairs={{8,0},{12,4},{16,24},{20,28},{9,1},{13,5},{17,25},{21,29},{10,2},{... | collective-permute-start | bytes 1572872 | tf_op jit(solution)/shard_map/ppermute | solution.py:642
  34.5 5.0 %collective-permute-start.7 = (bf16[1024,128]{1,0:T(8,128)(2,1)}, bf16[1024,128]{1,0:T(8,128)(2,1)S(1)}, u32[]{:S(2)}, u32[]{:S(2)}) collective-permute-start(bf16[1024,128]{1,0:T(8,128)(2,1)} %get-tuple-element.59), channel_id=1, source_target_pairs={{0,1},{1,0},{2,3},{3,2},{4,5},{5,4},{6,7},{7,6},{8,9},{9,8},{10,11... | collective-permute-start | bytes 786440 | tf_op jit(solution)/shard_map/ppermute | solution.py:25
  35.1 22.6 %collective-permute-start.12 = (bf16[1024,128]{1,0:T(8,128)(2,1)}, bf16[1024,128]{1,0:T(8,128)(2,1)S(1)}, u32[]{:S(2)}, u32[]{:S(2)}) collective-permute-start(bf16[1024,128]{1,0:T(8,128)(2,1)} %get-tuple-element.59), channel_id=1, source_target_pairs={{0,5},{1,4},{2,7},{3,6},{4,1},{5,0},{6,3},{7,2},{8,13},{9,12},{10,... | collective-permute-start | bytes 786440 | tf_op jit(solution)/shard_map/ppermute | solution.py:25
  49.5 24.6 %copy-start.3 = (bf16[1024,1024]{1,0:T(8,128)(2,1)S(1)}, bf16[1024,1024]{1,0:T(8,128)(2,1)}, u32[]{:S(2)}) copy-start(bf16[1024,1024]{1,0:T(8,128)(2,1)} %w_two.1) | copy-start | bytes 6291460
  49.5 24.6 %copy-start.5 = (f32[3,128,1024]{2,1,0:T(8,128)S(1)}, f32[3,128,1024]{2,1,0:T(8,128)}, u32[]{:S(2)}) copy-start(f32[3,128,1024]{2,1,0:T(8,128)} %copy-done.4) | copy-start | bytes 4718596
  49.5 24.6 %copy-start.10 = (bf16[9,1024]{1,0:T(8,128)(2,1)S(1)}, bf16[9,1024]{1,0:T(8,128)(2,1)}, u32[]{:S(2)}) copy-start(bf16[9,1024]{1,0:T(8,128)(2,1)} %taps.3) | copy-start | bytes 55300
  51.5 6.2 %collective-permute-start.8 = (bf16[128,512]{1,0:T(8,128)(2,1)S(1)}, bf16[128,512]{1,0:T(8,128)(2,1)S(1)}, u32[]{:S(2)}, u32[]{:S(2)}) collective-permute-start(bf16[128,512]{1,0:T(8,128)(2,1)S(1)} %get-tuple-element.82), channel_id=1, source_target_pairs={{0,1},{1,0},{2,3},{3,2},{4,5},{5,4},{6,7},{7,6},{8,9},{9,8},{10,11... | collective-permute-start | bytes 393224 | tf_op jit(solution)/shard_map/ppermute | solution.py:25
  51.6 6.4 %collective-permute-start.9 = (bf16[128,512]{1,0:T(8,128)(2,1)S(1)}, bf16[128,512]{1,0:T(8,128)(2,1)S(1)}, u32[]{:S(2)}, u32[]{:S(2)}) collective-permute-start(bf16[128,512]{1,0:T(8,128)(2,1)S(1)} %get-tuple-element.83), channel_id=1, source_target_pairs={{0,2},{1,3},{2,0},{3,1},{4,6},{5,7},{6,4},{7,5},{8,10},{9,11},{10,... | collective-permute-start | bytes 393224 | tf_op jit(solution)/shard_map/ppermute | solution.py:25
  53.2 6.7 %collective-permute-start.10 = (bf16[128,512]{1,0:T(8,128)(2,1)S(1)}, bf16[128,512]{1,0:T(8,128)(2,1)S(1)}, u32[]{:S(2)}, u32[]{:S(2)}) collective-permute-start(bf16[128,512]{1,0:T(8,128)(2,1)S(1)} %get-tuple-element.84), channel_id=1, source_target_pairs={{0,3},{1,2},{2,1},{3,0},{4,7},{5,6},{6,5},{7,4},{8,11},{9,10},{10,... | collective-permute-start | bytes 393224 | tf_op jit(solution)/shard_map/ppermute | solution.py:25
  78.6 21.1 %copy-start.7 = (bf16[128,1024]{1,0:T(8,128)(2,1)S(1)}, bf16[128,1024]{1,0:T(8,128)(2,1)}, u32[]{:S(2)}) copy-start(bf16[128,1024]{1,0:T(8,128)(2,1)} %x.3) | copy-start | bytes 786436
  78.7 9.0 %collective-permute-start.14 = (bf16[160,768]{1,0:T(8,128)(2,1)S(1)}, bf16[160,768]{1,0:T(8,128)(2,1)S(1)}, u32[]{:S(2)}, u32[]{:S(2)}) collective-permute-start(bf16[160,768]{1,0:T(8,128)(2,1)S(1)} %get-tuple-element.98), channel_id=1, source_target_pairs={{0,2},{1,3},{2,0},{3,1},{4,6},{5,7},{6,4},{7,5},{8,10},{9,11},{10,... | collective-permute-start | bytes 737288 | tf_op jit(solution)/shard_map/ppermute | solution.py:25
  80.2 11.4 %collective-permute-start.16 = (bf16[160,768]{1,0:T(8,128)(2,1)S(1)}, bf16[160,768]{1,0:T(8,128)(2,1)S(1)}, u32[]{:S(2)}, u32[]{:S(2)}) collective-permute-start(bf16[160,768]{1,0:T(8,128)(2,1)S(1)} %get-tuple-element.99), channel_id=1, source_target_pairs={{0,4},{1,5},{2,6},{3,7},{4,0},{5,1},{6,2},{7,3},{8,12},{9,13},{10,... | collective-permute-start | bytes 737288 | tf_op jit(solution)/shard_map/ppermute | solution.py:25
  81.6 9.9 %collective-permute-start.18 = (bf16[160,768]{1,0:T(8,128)(2,1)S(1)}, bf16[160,768]{1,0:T(8,128)(2,1)S(1)}, u32[]{:S(2)}, u32[]{:S(2)}) collective-permute-start(bf16[160,768]{1,0:T(8,128)(2,1)S(1)} %get-tuple-element.100), channel_id=1, source_target_pairs={{0,6},{1,7},{2,4},{3,5},{4,2},{5,3},{6,0},{7,1},{8,14},{9,15},{10,... | collective-permute-start | bytes 737288 | tf_op jit(solution)/shard_map/ppermute | solution.py:25
  82.2 9.9 %collective-permute-start.13 = (bf16[160,768]{1,0:T(8,128)(2,1)S(1)}, bf16[160,768]{1,0:T(8,128)(2,1)S(1)}, u32[]{:S(2)}, u32[]{:S(2)}) collective-permute-start(bf16[160,768]{1,0:T(8,128)(2,1)S(1)} %get-tuple-element.97.g0), channel_id=1, source_target_pairs={{0,1},{1,0},{2,3},{3,2},{4,5},{5,4},{6,7},{7,6},{8,9},{9,8},{10,11... | collective-permute-start | bytes 737288 | tf_op jit(solution)/shard_map/ppermute | solution.py:25
  87.6 4.5 %collective-permute-start.15 = (bf16[160,768]{1,0:T(8,128)(2,1)S(1)}, bf16[160,768]{1,0:T(8,128)(2,1)S(1)}, u32[]{:S(2)}, u32[]{:S(2)}) collective-permute-start(bf16[160,768]{1,0:T(8,128)(2,1)S(1)} %collective-permute-done.14.g2), channel_id=1, source_target_pairs={{0,1},{1,0},{2,3},{3,2},{4,5},{5,4},{6,7},{7,6},{8,9},{9,8},{10,11... | collective-permute-start | bytes 737288 | tf_op jit(solution)/shard_map/ppermute | solution.py:25
  91.6 1.5 %collective-permute-start.17 = (bf16[160,768]{1,0:T(8,128)(2,1)S(1)}, bf16[160,768]{1,0:T(8,128)(2,1)S(1)}, u32[]{:S(2)}, u32[]{:S(2)}) collective-permute-start(bf16[160,768]{1,0:T(8,128)(2,1)S(1)} %collective-permute-done.16.g4), channel_id=1, source_target_pairs={{0,1},{1,0},{2,3},{3,2},{4,5},{5,4},{6,7},{7,6},{8,9},{9,8},{10,11... | collective-permute-start | bytes 737288 | tf_op jit(solution)/shard_map/ppermute | solution.py:25
  91.6 1.9 %collective-permute-start.19 = (bf16[160,768]{1,0:T(8,128)(2,1)S(1)}, bf16[160,768]{1,0:T(8,128)(2,1)S(1)}, u32[]{:S(2)}, u32[]{:S(2)}) collective-permute-start(bf16[160,768]{1,0:T(8,128)(2,1)S(1)} %collective-permute-done.18.g6), channel_id=1, source_target_pairs={{0,1},{1,0},{2,3},{3,2},{4,5},{5,4},{6,7},{7,6},{8,9},{9,8},{10,11... | collective-permute-start | bytes 737288 | tf_op jit(solution)/shard_map/ppermute | solution.py:25
  95.3 11.8 %collective-permute-start.20 = (bf16[144,768]{1,0:T(8,128)(2,1)S(1)}, bf16[144,768]{1,0:T(8,128)(2,1)S(1)}, u32[]{:S(2)}, u32[]{:S(2)}) collective-permute-start(bf16[144,768]{1,0:T(8,128)(2,1)S(1)} %get-tuple-element.102), channel_id=1, source_target_pairs={{0,8},{1,9},{2,10},{3,11},{4,12},{5,13},{6,14},{7,15},{8,0},{9,1},... | collective-permute-start | bytes 663560 | tf_op jit(solution)/shard_map/ppermute | solution.py:25
  96.2 18.7 %collective-permute-start.21 = (bf16[144,768]{1,0:T(8,128)(2,1)S(1)}, bf16[144,768]{1,0:T(8,128)(2,1)S(1)}, u32[]{:S(2)}, u32[]{:S(2)}) collective-permute-start(bf16[144,768]{1,0:T(8,128)(2,1)S(1)} %get-tuple-element.103), channel_id=1, source_target_pairs={{0,16},{1,17},{2,18},{3,19},{4,20},{5,21},{6,22},{7,23},{8,24},{9,... | collective-permute-start | bytes 663560 | tf_op jit(solution)/shard_map/ppermute | solution.py:25
  98.0 16.9 %collective-permute-start.22 = (bf16[144,768]{1,0:T(8,128)(2,1)S(1)}, bf16[144,768]{1,0:T(8,128)(2,1)S(1)}, u32[]{:S(2)}, u32[]{:S(2)}) collective-permute-start(bf16[144,768]{1,0:T(8,128)(2,1)S(1)} %get-tuple-element.104), channel_id=1, source_target_pairs={{0,24},{1,25},{2,26},{3,27},{4,28},{5,29},{6,30},{7,31},{8,16},{9,... | collective-permute-start | bytes 663560 | tf_op jit(solution)/shard_map/ppermute | solution.py:25
  99.8 2.2 %copy-start.1 = (bf16[1024,2048]{1,0:T(8,128)(2,1)S(1)}, bf16[1024,2048]{1,0:T(8,128)(2,1)}, u32[]{:S(2)}) copy-start(bf16[1024,2048]{1,0:T(8,128)(2,1)} %w_one.3) | copy-start | bytes 12582916
  115.6 4.3 %collective-permute-start.23 = (bf16[32,768]{1,0:T(8,128)(2,1)S(1)}, bf16[32,768]{1,0:T(8,128)(2,1)S(1)}, u32[]{:S(2)}, u32[]{:S(2)}) collective-permute-start(bf16[32,768]{1,0:T(8,128)(2,1)S(1)} %get-tuple-element.106), channel_id=1, source_target_pairs={{0,2},{1,3},{2,0},{3,1},{4,6},{5,7},{6,4},{7,5},{8,10},{9,11},{10,... | collective-permute-start | bytes 147464 | tf_op jit(solution)/shard_map/ppermute | solution.py:25
  116.6 4.1 %collective-permute-start.24 = (bf16[32,768]{1,0:T(8,128)(2,1)S(1)}, bf16[32,768]{1,0:T(8,128)(2,1)S(1)}, u32[]{:S(2)}, u32[]{:S(2)}) collective-permute-start(bf16[32,768]{1,0:T(8,128)(2,1)S(1)} %get-tuple-element.107), channel_id=1, source_target_pairs={{0,4},{1,5},{2,6},{3,7},{4,0},{5,1},{6,2},{7,3},{8,12},{9,13},{10,... | collective-permute-start | bytes 147464 | tf_op jit(solution)/shard_map/ppermute | solution.py:25
  117.2 5.0 %collective-permute-start.25 = (bf16[32,768]{1,0:T(8,128)(2,1)S(1)}, bf16[32,768]{1,0:T(8,128)(2,1)S(1)}, u32[]{:S(2)}, u32[]{:S(2)}) collective-permute-start(bf16[32,768]{1,0:T(8,128)(2,1)S(1)} %get-tuple-element.108), channel_id=1, source_target_pairs={{0,6},{1,7},{2,4},{3,5},{4,2},{5,3},{6,0},{7,1},{8,14},{9,15},{10,... | collective-permute-start | bytes 147464 | tf_op jit(solution)/shard_map/ppermute | solution.py:25
